TPU v7x, 128 devices: a whole 4x4x4 slice. The times are simulated.
128 devices in a mesh: group: 4 (over x), dev: 32 (over y, z, core).
Axes of the slice: x: 4, y: 4, z: 4, core: 2. Of those that a mesh axis runs over, the one named last changes fastest.
Arguments:
- density: float32 [128, 320, 128], P(('group', 'dev')), may hold values from 0.5 to 2
- velocity: float32 [3, 128, 320, 128], P(None, ('group', 'dev')), may hold values from -0.75 to 0.75
- pressure: float32 [128, 320, 128], P(('group', 'dev')), may hold values from 0.5 to 2
- rbf_blocks: bfloat16 [8192, 128, 128], P(('group', 'dev')), may hold values from -0.5 to 0.5
- correlation: int32 [8192, 128], P(('group', 'dev')), may hold values from 0 to 319
- normals: float32 [8192, 3, 128], P(('group', 'dev')), may hold values from -6 to 6
- routes: int32 [8192, 1], P(('group', 'dev')), may hold values from 0 to 127; in each aligned block of 64 rows (0 to 63, 64 to 127, ...) at most 2 rows name the same one
- targets: int32 [8192], P(('group', 'dev')), may hold values from 0 to 31
- stiffness: bfloat16 [4096, 128, 128], P(('group', 'dev')), may hold values from -0.35 to 2.35
- coupling: bfloat16 [4096, 128, 128], P(('group', 'dev')), may hold values from -0.5 to 0.5
- inverse_diag: float32 [4096, 3, 128], P(('group', 'dev')), may hold values from 0.5 to 1.5
- displacement: float32 [4096, 3, 128], P(('group', 'dev')), may hold values from -6 to 6
- diff_res: float32 [8, 4096, 3, 128], P(None, ('group', 'dev')), may hold values from -2 to 2
- diff_disp: float32 [8, 4096, 3, 128], P(None, ('group', 'dev')), may hold values from -2.4 to 2.4
Outputs:
- fluid_next: float32 [5, 128, 320, 128], P(None, ('group', 'dev'))
- disp_next: float32 [4096, 3, 128], P(('group', 'dev'))
- wall_motion: float32 [8192, 3, 128], P(('group', 'dev'))
Inputs may be any that keep to these rules, and one draw needn't show every extreme that they name: `routes`: among the 64 blocks of one device at most 2 name the same owner, and some device names one owner exactly 2 times.
All inputs are finite; a program needn't handle non-finite values.
Results may differ from a plain program's by a relative error of at most 0.0004.
The roundings to bfloat16 on the way count: a program that leaves them out, or rounds other values in their place, can miss the bound.
Values may be sent and summed in bfloat16 or wider, within the bound.
No kernel may reach another device: no remote copies, remote signals or barrier semaphores. Data moves between devices by JAX's collectives and lax.ppermute only.
A program may use at most 64 MiB of HBM per device.

v0:
```python
import jax
import jax.numpy as jnp
from jax import lax
from jax.sharding import PartitionSpec as P

ratio_heat = 1.4
step_ratio = 0.03


def extended(value, sides, width):
    for axis, dim in sides:
        peers, length = (lax.axis_size(axis), value.shape[dim])
        up = [(i, (i + 1) % peers) for i in range(peers)]
        down = [(j, i) for i, j in up]
        last = lax.slice_in_dim(value, length - width, length, axis=dim)
        leading = lax.slice_in_dim(value, 0, width, axis=dim)
        before = lax.ppermute(last, axis, up)
        after = lax.ppermute(leading, axis, down)
        value = jnp.concatenate([before, value, after], axis=dim)
    return value


def shifted(block, axis, distance):
    devices = range(lax.axis_size(axis))
    route = [(i - distance, i) for i in devices if i - distance in devices]
    return lax.ppermute(block, axis, route)


def euler_flux(state, normal_axis):
    dens = state[0]
    vel = state[1:4] / dens
    press = (ratio_heat - 1.0) * (state[4] - 0.5 * dens * jnp.sum(vel * vel, axis=0))
    normal_speed = vel[normal_axis]
    rows = [dens * normal_speed]
    for comp in range(3):
        moment = state[1 + comp] * normal_speed
        if comp == normal_axis:
            moment = moment + press
        rows.append(moment)
    rows.append((state[4] + press) * normal_speed)
    wave_speed = jnp.abs(normal_speed) + jnp.sqrt(ratio_heat * press / dens)
    return (jnp.stack(rows, axis=0), wave_speed)


def rusanov(left_state, right_state, normal_axis):
    flux_left, speed_left = euler_flux(left_state, normal_axis)
    flux_right, speed_right = euler_flux(right_state, normal_axis)
    return 0.5 * (flux_left + flux_right) - 0.5 * jnp.maximum(speed_left, speed_right) * (
        right_state - left_state
    )


def conserve(density, velocity, pressure):
    energy = pressure / (ratio_heat - 1.0) + 0.5 * density * jnp.sum(velocity * velocity, axis=0)
    return jnp.concatenate([density[None], density[None] * velocity, energy[None]], axis=0)


def advance(padded, conserved):
    face_x = rusanov(padded[:, :-1], padded[:, 1:], 0)
    divergence = face_x[:, 1:] - face_x[:, :-1]
    face_y = rusanov(conserved, jnp.roll(conserved, -1, axis=2), 1)
    divergence = divergence + face_y - jnp.roll(face_y, 1, axis=2)
    mirror_sign = jnp.array([1.0, 1.0, 1.0, -1.0, 1.0], dtype=conserved.dtype)[:, None, None, None]
    padded_z = jnp.concatenate(
        [conserved[..., :1] * mirror_sign, conserved, conserved[..., -1:]], axis=3
    )
    face_z = rusanov(padded_z[..., :-1], padded_z[..., 1:], 2)
    divergence = divergence + face_z[..., 1:] - face_z[..., :-1]
    return conserved - step_ratio * divergence


def wall_pressure(state):
    bottom = state[..., 0]
    return (ratio_heat - 1.0) * (
        bottom[4] - 0.5 * jnp.sum(bottom[1:4] * bottom[1:4], axis=0) / bottom[0]
    )


def cho_apply(gram, projected):
    factor = jnp.linalg.cholesky(gram)
    middle = lax.linalg.triangular_solve(factor, projected[:, None], left_side=True, lower=True)
    return lax.linalg.triangular_solve(
        factor, middle, left_side=True, lower=True, transpose_a=True
    )[:, 0]


def on_device(
    density,
    velocity,
    pressure,
    rbf_blocks,
    correlation,
    normals,
    routes,
    targets,
    stiffness,
    coupling,
    inverse_diag,
    displacement,
    diff_res,
    diff_disp,
):
    conserved = conserve(density, velocity, pressure)
    padded = extended(conserved, ((("group", "dev"), 1),), 1)
    fluid_next = advance(padded, conserved)
    wall_row = wall_pressure(fluid_next).reshape(-1)
    weighted = (wall_row[correlation][:, None, :] * normals).astype(jnp.bfloat16)
    block_loads = jnp.einsum(
        "bci,bij->bcj", weighted, rbf_blocks, preferred_element_type=jnp.float32
    )
    blocks = block_loads.shape[0]
    width_row = block_loads.shape[1] * block_loads.shape[2]
    peer_count = lax.axis_size(("group", "dev"))
    capacity = max(2, 2 * blocks // peer_count)
    slot_count = peer_count * capacity
    target_dev = routes[:, 0]
    member = (target_dev[:, None] == jnp.arange(peer_count, dtype=jnp.int32)[None, :]).astype(
        jnp.int32
    )
    position = jnp.sum((jnp.cumsum(member, axis=0) - member) * member, axis=1)
    slot_id = target_dev * capacity + position
    send_loads = (
        jnp.zeros((slot_count, width_row), jnp.float32)
        .at[slot_id]
        .set(block_loads.reshape(blocks, width_row))
    )
    send_tag = (
        jnp.full((slot_count,), -1.0, jnp.float32).at[slot_id].set(targets.astype(jnp.float32))
    )
    got_loads, got_tag = (
        lax.all_to_all(
            send_loads.reshape(peer_count, capacity, width_row),
            ("group", "dev"),
            split_axis=0,
            concat_axis=0,
            tiled=True,
        ),
        lax.all_to_all(
            send_tag.reshape(peer_count, capacity),
            ("group", "dev"),
            split_axis=0,
            concat_axis=0,
            tiled=True,
        ),
    )
    got_loads = got_loads.reshape(slot_count, width_row)
    got_tag = got_tag.reshape(slot_count)
    solid_count = displacement.shape[0]
    selector = (got_tag[None, :] == jnp.arange(solid_count, dtype=jnp.float32)[:, None]).astype(
        jnp.float32
    )
    solid_load = jnp.dot(
        selector, got_loads, precision=lax.Precision.HIGHEST, preferred_element_type=jnp.float32
    ).reshape(displacement.shape)
    disp_half = displacement.astype(jnp.bfloat16)
    prior_block = shifted(disp_half[-1:], ("group", "dev"), 1)
    earlier = jnp.concatenate([prior_block, disp_half[:-1]], axis=0)
    solid_res = jnp.einsum("bcj,bij->bci", disp_half, stiffness, preferred_element_type=jnp.float32)
    solid_res = (
        solid_res
        + jnp.einsum("bcj,bij->bci", earlier, coupling, preferred_element_type=jnp.float32)
        - solid_load
    )
    coupling_res = -inverse_diag * solid_res
    projected_local = jnp.einsum(
        "mbcj,bcj->m", diff_res, coupling_res, precision=lax.Precision.HIGHEST
    )
    gram_local = jnp.einsum("mbcj,nbcj->mn", diff_res, diff_res, precision=lax.Precision.HIGHEST)
    gram_matrix, projected = lax.psum((gram_local, projected_local), ("group", "dev"))
    mixing = -cho_apply(gram_matrix, projected)
    disp_next = (
        displacement
        + coupling_res
        + jnp.einsum("mbcj,m->bcj", diff_disp, mixing, precision=lax.Precision.HIGHEST)
    )
    reply_rows = disp_next.astype(jnp.bfloat16).reshape(solid_count, width_row)
    replies = jnp.dot(
        selector.T.astype(jnp.bfloat16), reply_rows, preferred_element_type=jnp.float32
    ).astype(jnp.bfloat16)
    returned = lax.all_to_all(
        replies.reshape(peer_count, capacity, width_row),
        ("group", "dev"),
        split_axis=0,
        concat_axis=0,
        tiled=True,
    )
    picked = returned.reshape(slot_count, width_row)[slot_id].reshape(block_loads.shape)
    wall_motion = jnp.einsum("bij,bcj->bci", rbf_blocks, picked, preferred_element_type=jnp.float32)
    return (fluid_next, disp_next, wall_motion)


def solution(mesh):
    placed = (
        P(("group", "dev"), None, None),
        P(None, ("group", "dev"), None, None),
        P(("group", "dev"), None, None),
        P(("group", "dev"), None, None),
        P(("group", "dev"), None),
        P(("group", "dev"), None, None),
        P(("group", "dev"), None),
        P(("group", "dev")),
        P(("group", "dev"), None, None),
        P(("group", "dev"), None, None),
        P(("group", "dev"), None, None),
        P(("group", "dev"), None, None),
        P(None, ("group", "dev"), None, None),
        P(None, ("group", "dev"), None, None),
    )
    return jax.shard_map(
        on_device,
        mesh=mesh,
        in_specs=placed,
        out_specs=(
            P(None, ("group", "dev"), None, None),
            P(("group", "dev"), None, None),
            P(("group", "dev"), None, None),
        ),
        check_vma=False,
    )
```

profile of v0, /device:TPU:1, one launch (start us, length us, event | category | flops | bytes accessed | tf_op | source)
XLA Modules:
  0.0 205.8 jit_solution(3020429876626956091)
XLA Ops:
  0.7 1.4 multiply_reduce_fusion.5
  2.0 0.7 bitcast_dynamic-update-slice_fusion.1
  2.8 0.7 fusion.57
  3.4 0.7 fusion.56
  4.2 0.9 pad_maximum_fusion.3
  5.1 1.4 collective-permute-start.1
  6.5 1.6 collective-permute-start
  8.5 0.8 scatter_custom_fusion
  9.3 0.8 all_to_all.12
  10.1 14.6 %all-to-all-start = ((f32[128,1,2]{2,1,0:T(1,128)}), f32[128,1,2]{2,1,0:T(1,128)S(1)}, u32[]{:S(2)}, u32[]{:S(2)}) async-start(f32[128,1,2]{2,1,0:T(1,128)} %bitcast.30), calls=%async_computation | async-start | bytes 131072 | tf_op jit(solution)/shard_map/all_to_all | solution.py:138
  24.7 0.7 slice.284
  25.5 1.2 slice.283
  26.7 1.7 fusion.107
  28.4 0.5 pad_maximum_fusion.2
  30.0 0.7 fusion.52
  30.8 0.8 copy-done.4
  31.9 0.8 bitcast_dynamic-update-slice_fusion
  32.7 1.4 fusion.6
  34.3 0.6 multiply_subtract_fusion
  34.9 1.7 pad_maximum_fusion.1
  37.8 1.7 multiply_subtract_fusion.1
  40.2 0.5 copy-done.2
  40.8 51.2 %gather_fusion = f32[8192]{0:T(1024)S(1)} fusion(f32[320]{0:T(512)S(1)} %subtract_multiply_fusion, s32[8192]{0:T(1024)S(1)} %fusion.79), kind=kCustom, calls=%fused_computation | custom fusion | bytes 98304 | tf_op jit(solution)/shard_map/gather | solution.py:107
  92.1 0.6 fusion.74
  92.7 0.9 scatter_custom_fusion.1
  93.7 1.0 reshape.784
  94.6 9.8 %all-to-all-start.1 = ((f32[128,2,384]{2,1,0:T(2,128)}), f32[128,2,384]{2,1,0:T(2,128)S(1)}, u32[]{:S(2)}, u32[]{:S(2)}) async-start(f32[128,2,384]{2,1,0:T(2,128)} %reshape.784), calls=%async_computation.1 | async-start | bytes 786432 | tf_op jit(solution)/shard_map/all_to_all | solution.py:131
  104.5 3.8 %collective-permute-start.2 = (bf16[1,3,128]{2,1,0:T(4,128)(2,1)S(1)}, bf16[1,3,128]{2,1,0:T(4,128)(2,1)S(1)}, u32[]{:S(2)}, u32[]{:S(2)}) collective-permute-start(bf16[1,3,128]{2,1,0:T(4,128)(2,1)S(1)} %slice.318), channel_id=1, source_target_pairs={{0,1},{1,2},{2,3},{3,4},{4,5},{5,6},{6,7},{7,8},{8,9},{9,10},{10,1... | collective-permute-start | bytes 2312 | tf_op jit(solution)/shard_map/ppermute | solution.py:26
  108.3 1.0 convolution_bitcast_fusion
  109.3 1.9 fusion.108
  111.2 0.5 broadcast.290
  111.7 0.8 reduce.20
  112.7 4.0 %all-to-all-done.1 = f32[128,2,384]{2,1,0:T(2,128)S(1)} async-done(((f32[128,2,384]{2,1,0:T(2,128)}), f32[128,2,384]{2,1,0:T(2,128)S(1)}, u32[]{:S(2)}, u32[]{:S(2)}) %all-to-all-start.1) | async-done | bytes 393248 | tf_op jit(solution)/shard_map/all_to_all | solution.py:131
  117.4 1.9 fusion.1
  119.3 1.1 convolution_bitcast_fusion.3
  120.4 63.1 %all-reduce = (f32[8,8]{0,1:T(8,128)S(1)}, f32[8]{0:T(128)S(1)}) all-reduce(f32[8,8]{0,1:T(8,128)S(1)} %convolution_bitcast_fusion, f32[8]{0:T(128)S(1)} %convolution_bitcast_fusion.3), channel_id=1, replica_groups=mesh['group'=4,'dev'=32] {'group','dev'}, use_global_device_ids=true, to_apply=%region_12.13 | all-reduce | flops 72 | bytes 576 | tf_op jit(solution)/shard_map/psum | solution.py:169
  183.6 0.7 cholesky.16
  184.3 0.6 compare_reduce_fusion
  185.0 0.6 fusion.90
  185.6 0.6 custom-call.8
  186.5 0.7 fusion.14
  187.5 0.7 reshape.787
  188.3 4.6 %all-to-all-start.2 = ((bf16[128,2,384]{2,1,0:T(2,128)(2,1)}), bf16[128,2,384]{2,1,0:T(2,128)(2,1)S(1)}, u32[]{:S(2)}, u32[]{:S(2)}) async-start(bf16[128,2,384]{2,1,0:T(2,128)(2,1)} %reshape.787), calls=%async_computation.2 | async-start | bytes 393216 | tf_op jit(solution)/shard_map/all_to_all | solution.py:180
  192.9 0.6 copy.55
  193.5 9.6 %all-to-all-done.2 = bf16[128,2,384]{2,1,0:T(2,128)(2,1)S(1)} async-done(((bf16[128,2,384]{2,1,0:T(2,128)(2,1)}), bf16[128,2,384]{2,1,0:T(2,128)(2,1)S(1)}, u32[]{:S(2)}, u32[]{:S(2)}) %all-to-all-start.2) | async-done | bytes 196640 | tf_op jit(solution)/shard_map/all_to_all | solution.py:180
  203.3 0.7 gather_fusion.1
  204.0 1.2 fusion.109
  205.2 0.7 copy.56
  (90 shorter events, 5.6 us)
Async XLA Ops:
  0.6 91.4 %copy-start = (bf16[64,128,128]{2,1,0:T(8,128)(2,1)S(1)}, bf16[64,128,128]{2,1,0:T(8,128)(2,1)}, u32[]{:S(2)}) copy-start(bf16[64,128,128]{2,1,0:T(8,128)(2,1)} %param.18) | copy-start | bytes 6291460
  0.6 1.4 copy-start.1
  0.7 2.8 %copy-start.8 = (f32[1,320,128]{2,1,0:T(8,128)S(1)}, f32[1,320,128]{2,1,0:T(8,128)}, u32[]{:S(2)}) copy-start(f32[1,320,128]{2,1,0:T(8,128)} %param.17) | copy-start | bytes 491524
  2.0 3.1 %copy-start.3 = (f32[320,128]{1,0:T(8,128)}, f32[320,128]{1,0:T(8,128)S(1)}, u32[]{:S(2)}) copy-start(f32[320,128]{1,0:T(8,128)S(1)} %get-tuple-element.29) | copy-start | bytes 491524
  2.7 5.4 %copy-start.11 = (s32[64,1]{0,1:T(1,128)S(1)}, s32[64,1]{0,1:T(1,128)}, u32[]{:S(2)}) copy-start(s32[64,1]{0,1:T(1,128)} %param.21) | copy-start | bytes 772
  3.4 5.1 %copy-start.13 = (s32[64]{0:T(128)S(1)}, s32[64]{0:T(128)}, u32[]{:S(2)}) copy-start(s32[64]{0:T(128)} %param.22) | copy-start | bytes 772
  4.2 22.5 %copy-start.12 = (f32[5]{0:T(128)S(1)}, f32[5]{0:T(128)}, u32[]{:S(2)}) copy-start(f32[5]{0:T(128)} %constant.91.clone) | copy-start | bytes 64
  5.1 29.7 %collective-permute-start.1 = (f32[5,1,320,128]{3,2,1,0:T(8,128)}, f32[5,1,320,128]{3,2,1,0:T(8,128)}, u32[]{:S(2)}, u32[]{:S(2)}) collective-permute-start(f32[5,1,320,128]{3,2,1,0:T(8,128)} %pad_maximum_fusion.3), channel_id=1, source_target_pairs={{1,0},{2,1},{3,2},{4,3},{5,4},{6,5},{7,6},{8,7},{9,8},{10,9},{11,1... | collective-permute-start | bytes 2457608 | tf_op jit(solution)/shard_map/ppermute | solution.py:18
  6.5 28.3 %collective-permute-start = (f32[5,1,320,128]{3,2,1,0:T(8,128)}, f32[5,1,320,128]{3,2,1,0:T(8,128)}, u32[]{:S(2)}, u32[]{:S(2)}) collective-permute-start(f32[5,1,320,128]{3,2,1,0:T(8,128)} %pad_maximum_fusion.3), channel_id=1, source_target_pairs={{0,1},{1,2},{2,3},{3,4},{4,5},{5,6},{6,7},{7,8},{8,9},{9,10},{10,1... | collective-permute-start | bytes 2457608 | tf_op jit(solution)/shard_map/ppermute | solution.py:17
  10.1 84.5 %all-to-all-start = ((f32[128,1,2]{2,1,0:T(1,128)}), f32[128,1,2]{2,1,0:T(1,128)S(1)}, u32[]{:S(2)}, u32[]{:S(2)}) async-start(f32[128,1,2]{2,1,0:T(1,128)} %bitcast.30), calls=%async_computation | async-start | bytes 131072 | tf_op jit(solution)/shard_map/all_to_all | solution.py:138
  30.7 0.9 copy-start.4
  32.7 1.5 copy-start.10
  39.9 0.9 copy-start.2
  40.8 51.2 %copy-start.9 = (f32[64,3,128]{2,0,1:T(8,128)S(1)}, f32[64,3,128]{2,0,1:T(8,128)}, u32[]{:S(2)}) copy-start(f32[64,3,128]{2,0,1:T(8,128)} %param.20) | copy-start | bytes 294916
  92.1 12.3 %copy-start.7 = (f32[32,3,128]{2,0,1:T(8,128)S(1)}, f32[32,3,128]{2,0,1:T(8,128)}, u32[]{:S(2)}) copy-start(f32[32,3,128]{2,0,1:T(8,128)} %param.26) | copy-start | bytes 147460
  92.7 15.6 %copy-start.5 = (f32[8,32,3,128]{3,1,2,0:T(8,128)S(1)}, f32[8,32,3,128]{3,1,2,0:T(8,128)}, u32[]{:S(2)}) copy-start(f32[8,32,3,128]{3,1,2,0:T(8,128)} %param.27) | copy-start | bytes 1179652
  94.6 22.0 %all-to-all-start.1 = ((f32[128,2,384]{2,1,0:T(2,128)}), f32[128,2,384]{2,1,0:T(2,128)S(1)}, u32[]{:S(2)}, u32[]{:S(2)}) async-start(f32[128,2,384]{2,1,0:T(2,128)} %reshape.784), calls=%async_computation.1 | async-start | bytes 786432 | tf_op jit(solution)/shard_map/all_to_all | solution.py:131
  104.5 13.0 %collective-permute-start.2 = (bf16[1,3,128]{2,1,0:T(4,128)(2,1)S(1)}, bf16[1,3,128]{2,1,0:T(4,128)(2,1)S(1)}, u32[]{:S(2)}, u32[]{:S(2)}) collective-permute-start(bf16[1,3,128]{2,1,0:T(4,128)(2,1)S(1)} %slice.318), channel_id=1, source_target_pairs={{0,1},{1,2},{2,3},{3,4},{4,5},{5,6},{6,7},{7,8},{8,9},{9,10},{10,1... | collective-permute-start | bytes 2312 | tf_op jit(solution)/shard_map/ppermute | solution.py:26
  117.1 69.5 %copy-start.6 = (f32[8,32,3,128]{3,1,2,0:T(8,128)S(1)}, f32[8,32,3,128]{3,1,2,0:T(8,128)}, u32[]{:S(2)}) copy-start(f32[8,32,3,128]{3,1,2,0:T(8,128)} %param.28) | copy-start | bytes 1179652
  188.3 14.9 %all-to-all-start.2 = ((bf16[128,2,384]{2,1,0:T(2,128)(2,1)}), bf16[128,2,384]{2,1,0:T(2,128)(2,1)S(1)}, u32[]{:S(2)}, u32[]{:S(2)}) async-start(bf16[128,2,384]{2,1,0:T(2,128)(2,1)} %reshape.787), calls=%async_computation.2 | async-start | bytes 393216 | tf_op jit(solution)/shard_map/all_to_all | solution.py:180
where the time goes:
time: 206 us
  blocking collectives  63.1 us (31%)
  local copies, waits for them, and re-layouts  62.3 us (30%)
  starting transfers between devices  35.9 us (17%)
  other arithmetic  20.6 us (10%)
  waiting for transfers between devices  13.6 us (7%)
  matrix products  9.18 us (4%)
    psum x1, blocking collectives, on_device(): lax.psum((gram_local, projected_local), ('group', 'dev'))  63.1 us
    gather x1, local copies, waits for them, and re-layouts, on_device(): wall_row[correlation][:, None, :] * normals  51.2 us
    all_to_all x1, starting transfers between devices, on_device(): lax.all_to_all(send_tag.reshape(peer_count, capacity), ('group', 'dev'),...  14.6 us
    all_to_all x1, starting transfers between devices, on_device(): lax.all_to_all(send_loads.reshape(peer_count, capacity, width_row), ('gro...  9.76 us
    all_to_all x1, waiting for transfers between devices, on_device(): lax.all_to_all(replies.reshape(peer_count, capacity, width_row), ('group'...  9.64 us
    all_to_all x1, starting transfers between devices, on_device(): lax.all_to_all(replies.reshape(peer_count, capacity, width_row), ('group'...  4.63 us
  transfers between devices with their start and end apart: 6, of which 2 were waited for; matrix products, arithmetic and copies ran while one was open for 37% of the time, Pallas kernels for 0%

commit v1 on v0

v1 whole, which is shorter than its diff:
```python
import functools

import jax
import jax.numpy as jnp
from jax import lax
from jax.experimental import pallas as pl
from jax.experimental.pallas import tpu as pltpu
from jax.sharding import PartitionSpec as P

AXES = ("group", "dev")
ratio_heat = 1.4
step_ratio = 0.03
f32 = jnp.float32
bf16 = jnp.bfloat16


def iota(shape, dim):
    return lax.broadcasted_iota(jnp.int32, shape, dim)


def call(kernel, out, *args, scratch=(), limit=48):
    return pl.pallas_call(
        kernel,
        out_shape=out,
        scratch_shapes=list(scratch),
        compiler_params=pltpu.CompilerParams(vmem_limit_bytes=limit * 2**20),
        name=kernel.__name__,
    )(*args)


def shape(dims, dtype=f32):
    return jax.ShapeDtypeStruct(dims, dtype)


def conserve(cell):
    dens, v0, v1, v2, press = cell
    kinetic = v0 * v0 + v1 * v1 + v2 * v2
    energy = press * (1.0 / (ratio_heat - 1.0)) + 0.5 * dens * kinetic
    return (dens, dens * v0, dens * v1, dens * v2, energy)


def sound(cell):
    return jnp.sqrt(ratio_heat * cell[4] / cell[0])


def with_speed(cell):
    return (cell, conserve(cell), sound(cell))


def euler_flux(state, axis):
    cell, cons, speed = state
    normal = cell[1 + axis]
    rows = [cons[1 + axis]]
    for comp in range(3):
        moment = cons[1 + comp] * normal
        rows.append(moment + cell[4] if comp == axis else moment)
    rows.append((cons[4] + cell[4]) * normal)
    return rows, jnp.abs(normal) + speed


def rusanov(left, right, axis):
    flux_left, speed_left = euler_flux(left, axis)
    flux_right, speed_right = euler_flux(right, axis)
    top = jnp.maximum(speed_left, speed_right)
    return [
        0.5 * (a + b - top * (r - l))
        for a, b, l, r in zip(flux_left, flux_right, left[1], right[1])
    ]


def wall_flux(state):
    cell, cons, speed = state
    return cons[3] * cell[3] + cell[4] - (jnp.abs(cell[3]) + speed) * cons[3]


def edges(dens_ref, vel_ref, press_ref, disp_ref, send_ref, second_ref, bulk_ref):
    depth, lanes = dens_ref.shape[1:]
    wide = send_ref.shape[1]
    lane = iota((depth, lanes), 1)
    packed = jnp.ones((depth, lanes), f32)
    rows = [dens_ref[0], vel_ref[0, 0], vel_ref[1, 0], vel_ref[2, 0], press_ref[0]]
    for i, row in enumerate(rows):
        bulk_ref[i] = row.astype(bf16)
        moved = row if i == 0 else pltpu.roll(row, 2 * i, 1)
        packed = jnp.where((lane >> 1) == i, moved, packed)
    packed = jnp.concatenate([packed, jnp.ones((wide - depth, lanes), f32)], axis=0)
    turned = packed.T
    last = disp_ref.shape[1] - 1
    for i in range(5):
        send_ref[i : i + 1, :] = turned[2 * i : 2 * i + 1, :]
        second_ref[i : i + 1, :] = turned[2 * i + 1 : 2 * i + 2, :]
    nodes = disp_ref.shape[2]
    for c in range(3):
        send_ref[5:6, c * nodes : (c + 1) * nodes] = disp_ref[c, last : last + 1, :]
    send_ref[6:8, :] = jnp.zeros((2, wide), f32)
    second_ref[5:8, :] = jnp.zeros((3, wide), f32)


def fluid(dens_ref, vel_ref, press_ref, below_ref, above_ref, next_ref):
    depth, lanes = dens_ref.shape[1:]
    rows = 16
    sub = iota((rows, lanes), 0)
    lane = iota((rows, lanes), 1)

    def load(at):
        return (
            dens_ref[0, at, :],
            vel_ref[0, 0, at, :],
            vel_ref[1, 0, at, :],
            vel_ref[2, 0, at, :],
            press_ref[0, at, :],
        )

    def step(i, carried):
        start = pl.multiple_of(i * rows, rows)
        after = pl.multiple_of(jnp.where(start + rows == depth, 0, start + rows), 8)
        at = pl.ds(start, rows)
        cell = load(at)
        ahead = load(pl.ds(after, 8))
        me = with_speed(cell)
        below = with_speed([below_ref[q, at, :].astype(f32) for q in range(5)])
        above = with_speed([above_ref[q, at, :].astype(f32) for q in range(5)])
        total = [
            b - a for a, b in zip(rusanov(below, me, 0), rusanov(me, above, 0))
        ]
        beside = with_speed(
            [
                jnp.where(sub == rows - 1, n[0:1, :], pltpu.roll(x, rows - 1, 0))
                for x, n in zip(cell, ahead)
            ]
        )
        face = rusanov(me, beside, 1)
        total = [
            t + f - jnp.where(sub == 0, c, pltpu.roll(f, 1, 0))
            for t, f, c in zip(total, face, carried)
        ]
        carried = tuple(f[rows - 1 : rows, :] for f in face)
        over = with_speed(
            [jnp.where(lane == lanes - 1, x, pltpu.roll(x, lanes - 1, 1)) for x in cell]
        )
        face = rusanov(me, over, 2)
        wall = wall_flux(me)
        for q in range(5):
            lower = jnp.where(
                lane == 0, wall if q == 3 else 0.0, pltpu.roll(face[q], 1, 1)
            )
            next_ref[q, 0, at, :] = me[1][q] - step_ratio * (total[q] + face[q] - lower)
        return carried

    first = with_speed([x[0:1, :] for x in load(pl.ds(0, 8))])
    last = with_speed([x[7:8, :] for x in load(pl.ds(depth - 8, 8))])
    lax.fori_loop(0, depth // rows, step, tuple(rusanov(last, first, 1)))


def wall_pressure(depth, own, second, below, above):
    wide = own[0].shape[1]
    lane = iota((1, wide), 1)
    me = with_speed(own)
    total = [
        b - a
        for a, b in zip(
            rusanov(with_speed(below), me, 0), rusanov(me, with_speed(above), 0)
        )
    ]

    def up(x):
        return jnp.where(lane == depth - 1, x[:, 0:1], pltpu.roll(x, wide - 1, 1))

    def down(x):
        return jnp.where(lane == 0, x[:, depth - 1 : depth], pltpu.roll(x, 1, 1))

    face = rusanov(me, with_speed([up(x) for x in own]), 1)
    total = [t + f - down(f) for t, f in zip(total, face)]
    face = rusanov(me, with_speed(second), 2)
    total = [t + f for t, f in zip(total, face)]
    total[3] = total[3] - wall_flux(me)
    q = [c - step_ratio * t for c, t in zip(me[1], total)]
    return (ratio_heat - 1.0) * (
        q[4] - 0.5 * (q[1] * q[1] + q[2] * q[2] + q[3] * q[3]) / q[0]
    )


def routing(routes_ref, targets_ref, diff_ref, scatter_ref, pick_ref, tag_ref, gram_ref):
    count = routes_ref.shape[1]
    spread, taken = scatter_ref.shape
    peers = tag_ref.shape[0]
    ii, jj = iota((count, count), 0), iota((count, count), 1)
    route_row = jnp.broadcast_to(routes_ref[...], (count, count)).astype(f32)
    target_row = jnp.broadcast_to(targets_ref[...], (count, count)).astype(f32)
    route_col = jnp.sum(jnp.where(ii == jj, route_row, 0.0), axis=1, keepdims=True)
    target_col = jnp.sum(jnp.where(ii == jj, target_row, 0.0), axis=1, keepdims=True)
    same = jnp.where(route_col == route_row, 1.0, 0.0)
    place_col = jnp.sum(jnp.where(jj < ii, same, 0.0), axis=1, keepdims=True)
    place_row = jnp.sum(jnp.where(ii < jj, same, 0.0), axis=0, keepdims=True)
    slot_col = route_col * 8.0 + place_col * 3.0
    slot_row = route_row[0:1, :] * 8.0 + place_row * 3.0
    own = (iota((count, taken), 1) >> 2) == iota((count, taken), 0)
    comp = iota((1, taken), 1) & 3
    at_row = jnp.sum(jnp.where(own, slot_col, 0.0), axis=0, keepdims=True)
    at_row = jnp.where(comp < 3, at_row + comp.astype(f32), -1.0)
    scatter_ref[...] = jnp.where(
        iota((spread, taken), 0).astype(f32) == at_row, 1.0, 0.0
    ).astype(bf16)
    own = (iota((taken, count), 0) >> 2) == iota((taken, count), 1)
    comp = iota((taken, 1), 0) & 3
    at_col = jnp.sum(jnp.where(own, slot_row, 0.0), axis=1, keepdims=True)
    at_col = jnp.where(comp < 3, at_col + comp.astype(f32), -1.0)
    pick_ref[...] = jnp.where(
        iota((taken, spread), 1).astype(f32) == at_col, 1.0, 0.0
    ).astype(bf16)
    to_peer = jnp.where(
        iota((peers, count), 0).astype(f32) == route_row[0:1, :], 1.0, 0.0
    )
    named = jnp.where(
        iota((count, tag_ref.shape[1]), 1).astype(f32) == place_col, target_col + 1.0, 0.0
    )
    tag_ref[...] = (
        jnp.dot(to_peer.astype(bf16), named.astype(bf16), preferred_element_type=f32) - 1.0
    )
    columns = diff_ref.shape[0]
    lanes = diff_ref.shape[3]
    sums = {}
    for m in range(columns):
        for n in range(m, columns):
            part = jnp.sum(diff_ref[m] * diff_ref[n], axis=0)
            sums[m, n] = jnp.sum(part, axis=0, keepdims=True)
    stacked = jnp.concatenate(
        [sums[min(m, n), max(m, n)] for m in range(columns) for n in range(columns)], axis=0
    )
    col = jnp.sum(stacked, axis=1, keepdims=True)
    diag = iota((columns * columns, lanes), 0) == iota((columns * columns, lanes), 1)
    gram_ref[...] = jnp.sum(jnp.where(diag, col, 0.0), axis=0, keepdims=True)


def thirds(value):
    high = value.astype(bf16)
    rest = value - high.astype(f32)
    middle = rest.astype(bf16)
    return high, middle, (rest - middle.astype(f32)).astype(bf16)


def exact_dot(onehot, value):
    return sum(jnp.dot(onehot, part, preferred_element_type=f32) for part in thirds(value))


def pick_half(both):
    lanes = both.shape[1] // 2
    return jnp.where(iota((8, lanes), 0) < 4, both[:, :lanes], both[:, lanes:])


def nt_dot(a, b):
    return lax.dot_general(a, b, (((1,), (1,)), ((), ())), preferred_element_type=f32)


def loads(
    depth, own_ref, second_ref, below_ref, above_ref, corr_ref, normals_ref, rbf_ref,
    scatter_ref, tag_ref, gram_ref, send_ref, weighted, mapped,
):
    def cell(ref):
        return [ref[i : i + 1, :] for i in range(5)]

    wall = wall_pressure(depth, cell(own_ref), cell(second_ref), cell(below_ref), cell(above_ref))
    count, nodes = corr_ref.shape
    at = corr_ref[...]
    within, part = at & (nodes - 1), at >> (nodes.bit_length() - 1)
    found = jnp.zeros((count, nodes), f32)
    for k in range(wall.shape[1] // nodes):
        table = jnp.broadcast_to(wall[:, k * nodes : (k + 1) * nodes], (count, nodes))
        got = jnp.take_along_axis(table, within, axis=1, mode="promise_in_bounds")
        found = jnp.where(part == k, got, found)
    for c in range(3):
        weighted[pl.ds(c, count, stride=4), :] = found * normals_ref[c]
    weighted[pl.ds(3, count, stride=4), :] = jnp.zeros((count, nodes), f32)
    for k in range(count // 2):
        both = jnp.concatenate([rbf_ref[2 * k], rbf_ref[2 * k + 1]], axis=1)
        left = weighted[8 * k : 8 * k + 8, :].astype(bf16)
        mapped[8 * k : 8 * k + 8, :] = pick_half(
            jnp.dot(left, both, preferred_element_type=f32)
        )
    send_ref[...] = exact_dot(scatter_ref[...], mapped[...])
    peers = tag_ref.shape[0]
    send_ref[pl.ds(6, peers, stride=8), :] = tag_ref[...]
    send_ref[pl.ds(7, peers, stride=8), :] = jnp.broadcast_to(gram_ref[...], tag_ref.shape)


def solid(keep_ref, disp_ref, below_ref, stiff_ref, coup_ref, out_ref, here, prior, made):
    count, nodes = disp_ref.shape[1:]
    for c in range(3):
        here[pl.ds(c, count, stride=4), :] = disp_ref[c]
        prior[pl.ds(4 + c, count, stride=4), :] = disp_ref[c]
        first = below_ref[5:6, c * nodes : (c + 1) * nodes]
        prior[c : c + 1, :] = jnp.where(keep_ref[0] > 0, first, 0.0)
    here[pl.ds(3, count, stride=4), :] = jnp.zeros((count, nodes), f32)
    prior[pl.ds(3, count + 1, stride=4), :] = jnp.zeros((count + 1, nodes), f32)
    for k in range(count // 2):
        rows = slice(8 * k, 8 * k + 8)
        left = jnp.concatenate([here[rows, :], prior[rows, :]], axis=1).astype(bf16)
        right = jnp.concatenate(
            [
                jnp.concatenate([stiff_ref[2 * k], stiff_ref[2 * k + 1]], axis=0),
                jnp.concatenate([coup_ref[2 * k], coup_ref[2 * k + 1]], axis=0),
            ],
            axis=1,
        )
        made[rows, :] = pick_half(nt_dot(left, right))
    for c in range(3):
        out_ref[c] = made[pl.ds(c, count, stride=4), :]


def residual(got_ref, kd_ref, inv_ref, disp_ref, diff_ref, base_ref, share_ref):
    count, nodes = disp_ref.shape[1:]
    peers = share_ref.shape[0]
    turned = got_ref[pl.ds(6, peers, stride=8), :].T
    block = iota((count, peers), 0).astype(f32)
    chosen = jnp.concatenate(
        [jnp.where(block == turned[i : i + 1, :], 1.0, 0.0) for i in range(2)], axis=1
    ).astype(bf16)
    res = []
    for c in range(3):
        rows = jnp.concatenate(
            [got_ref[pl.ds(c + 3 * i, peers, stride=8), :] for i in range(2)], axis=0
        )
        part = -inv_ref[c] * (kd_ref[c] - exact_dot(chosen, rows))
        base_ref[c] = disp_ref[c] + part
        res.append(part)
    columns = diff_ref.shape[0]
    sums = []
    for m in range(columns):
        part = sum(diff_ref[m, c] * res[c] for c in range(3))
        sums.append(jnp.sum(part, axis=0, keepdims=True))
    col = jnp.sum(jnp.concatenate(sums, axis=0), axis=1, keepdims=True)
    diag = iota((columns, nodes), 0) == iota((columns, nodes), 1)
    row = jnp.sum(jnp.where(diag, col, 0.0), axis=0, keepdims=True)
    share_ref[...] = jnp.broadcast_to(row, share_ref.shape)


def factor(blocks, got_ref, inverse_ref, serve_ref):
    spread, lanes = serve_ref.shape
    peers = spread // 8
    row = iota((8, lanes), 0)
    lane = iota((8, lanes), 1)
    second = row >= 3
    kept = ((lane // blocks) == jnp.where(second, row - 3, row)) & (row < 6)
    wanted = jnp.where(kept, lane % blocks, -2).astype(f32)
    for d in range(peers):
        tags = got_ref[8 * d + 6 : 8 * d + 7, :]
        tag = jnp.where(second, tags[:, 1:2], tags[:, 0:1])
        serve_ref[8 * d : 8 * d + 8, :] = jnp.where(tag == wanted, 1.0, 0.0).astype(bf16)
    total = jnp.sum(got_ref[pl.ds(7, peers, stride=8), :], axis=0, keepdims=True)
    n = 8
    gram = jnp.concatenate(
        [total if m == 0 else pltpu.roll(total, lanes - n * m, 1) for m in range(n)], axis=0
    )
    work = jnp.where(lane < n, gram, jnp.where(lane == row + n, 1.0, 0.0))
    for k in range(n):
        pivot = work[k : k + 1, :] * lax.rsqrt(work[k : k + 1, k : k + 1])
        below = work[:, k : k + 1] * lax.rsqrt(work[k : k + 1, k : k + 1])
        work = jnp.where(row == k, pivot, jnp.where(row > k, work - below * pivot, work))
    inverse_ref[...] = jnp.where(lane < n, pltpu.roll(work, lanes - n, 1), 0.0)


def update(share_ref, inverse_ref, base_ref, dd_ref, serve_ref, next_ref, reply_ref):
    projected = jnp.sum(share_ref[...], axis=0, keepdims=True)
    inverse = inverse_ref[...]
    middle = jnp.sum(inverse * projected, axis=1, keepdims=True)
    mixing = -jnp.sum(inverse * middle, axis=0, keepdims=True)
    rows = []
    for c in range(3):
        value = base_ref[c]
        for m in range(dd_ref.shape[0]):
            value = value + mixing[:, m : m + 1] * dd_ref[m, c]
        next_ref[c] = value
        rows.append(value)
    blocks = jnp.concatenate(rows, axis=0).astype(bf16)
    spare = serve_ref.shape[1] - blocks.shape[0]
    blocks = jnp.concatenate([blocks, jnp.zeros((spare, blocks.shape[1]), bf16)], axis=0)
    reply_ref[...] = jnp.dot(
        serve_ref[...], blocks, preferred_element_type=f32
    ).astype(bf16)


def motion(back_ref, pick_ref, rbf_ref, out_ref, picked, made):
    count = rbf_ref.shape[0]
    picked[...] = jnp.dot(pick_ref[...], back_ref[...], preferred_element_type=f32)
    for k in range(count // 2):
        rows = slice(8 * k, 8 * k + 8)
        both = jnp.concatenate([rbf_ref[2 * k], rbf_ref[2 * k + 1]], axis=0)
        made[rows, :] = pick_half(nt_dot(picked[rows, :].astype(bf16), both))
    for c in range(3):
        out_ref[c] = made[pl.ds(c, count, stride=4), :]


def exchange(value):
    return lax.all_to_all(value, AXES, split_axis=0, concat_axis=0, tiled=True)


def on_device(
    density, velocity, pressure, rbf, correlation, normals, routes, targets,
    stiffness, coupling, inverse_diag, displacement, diff_res, diff_disp,
):
    peers = lax.axis_size(AXES)
    depth, lanes = density.shape[1:]
    wide = -(-depth // 128) * 128
    count, nodes = correlation.shape
    blocks = displacement.shape[0]
    columns = diff_res.shape[0]
    normals, inverse_diag, displacement = (
        jnp.transpose(x, (1, 0, 2)) for x in (normals, inverse_diag, displacement)
    )
    diff_res, diff_disp = (jnp.transpose(x, (0, 2, 1, 3)) for x in (diff_res, diff_disp))
    ring = [(i, (i + 1) % peers) for i in range(peers)]
    back = [(j, i) for i, j in ring]

    own, second, bulk = call(
        edges,
        [shape((8, wide)), shape((8, wide)), shape((5, depth, lanes), bf16)],
        density, velocity, pressure, displacement,
    )
    below = lax.ppermute(own, AXES, ring)
    above = lax.ppermute(own, AXES, back)
    bulk_below = lax.ppermute(bulk, AXES, ring)
    bulk_above = lax.ppermute(bulk, AXES, back)
    scatter, pick, tag, gram = call(
        routing,
        [
            shape((8 * peers, 4 * count), bf16),
            shape((4 * count, 8 * peers), bf16),
            shape((peers, nodes)),
            shape((1, nodes)),
        ],
        routes.reshape(1, count), targets.reshape(1, count), diff_res,
    )
    kernel = functools.partial(loads, depth)
    kernel.__name__ = "loads"
    sent = call(
        kernel,
        shape((8 * peers, nodes)),
        own, second, below, above, correlation, normals, rbf, scatter, tag, gram,
        scratch=[pltpu.VMEM((4 * count, nodes), f32)] * 2,
    )
    got = exchange(sent.reshape(peers, 8, nodes)).reshape(8 * peers, nodes)
    keep = (lax.axis_index(AXES) > 0).astype(jnp.int32).reshape(1)
    stiff_call = pl.pallas_call(
        solid,
        out_shape=shape((3, blocks, nodes)),
        in_specs=[pl.BlockSpec(memory_space=pltpu.SMEM)]
        + [pl.BlockSpec(memory_space=pltpu.VMEM)] * 4,
        scratch_shapes=[
            pltpu.VMEM((4 * blocks, nodes), f32),
            pltpu.VMEM((4 * blocks + 8, nodes), f32),
            pltpu.VMEM((4 * blocks, nodes), f32),
        ],
        compiler_params=pltpu.CompilerParams(vmem_limit_bytes=48 * 2**20),
        name="solid",
    )
    product = stiff_call(keep, displacement, below, stiffness, coupling)
    base, share = call(
        residual,
        [shape((3, blocks, nodes)), shape((peers, nodes))],
        got, product, inverse_diag, displacement, diff_res,
    )
    shares = exchange(share)
    kernel = functools.partial(factor, blocks)
    kernel.__name__ = "factor"
    inverse, serve = call(
        kernel, [shape((columns, nodes)), shape((8 * peers, nodes), bf16)], got
    )
    disp_next, reply = call(
        update,
        [shape((3, blocks, nodes)), shape((8 * peers, nodes), bf16)],
        shares, inverse, base, diff_disp, serve,
    )
    returned = exchange(reply.reshape(peers, 8, nodes)).reshape(8 * peers, nodes)
    fluid_next = call(
        fluid,
        shape((5, 1, depth, lanes)),
        density, velocity, pressure, bulk_below, bulk_above,
    )
    wall_motion = call(
        motion,
        shape((3, count, nodes)),
        returned, pick, rbf,
        scratch=[pltpu.VMEM((4 * count, nodes), f32)] * 2,
    )
    return (
        fluid_next,
        jnp.transpose(disp_next, (1, 0, 2)),
        jnp.transpose(wall_motion, (1, 0, 2)),
    )


def solution(mesh):
    rows = P(AXES, None, None)
    inner = P(None, AXES, None, None)
    return jax.shard_map(
        on_device,
        mesh=mesh,
        in_specs=(
            rows, inner, rows, rows, P(AXES, None), rows, P(AXES, None), P(AXES),
            rows, rows, rows, rows, inner, inner,
        ),
        out_specs=(inner, rows, rows),
        check_vma=False,
    )
```

time: 206 us -> 81 us (0.39)
  blocking collectives: 63.1 us -> 0 us
  local copies, waits for them, and re-layouts: 62.3 us -> 16.2 us
  other arithmetic: 20.6 us -> 0 us
  Pallas kernels: 0 us -> 14 us
  starting transfers between devices: 35.9 us -> 26.3 us
  waiting for transfers between devices: 13.6 us -> 22.9 us
  matrix products: 9.18 us -> 0 us
    psum x1 -> x0, blocking collectives: 63.1 us -> none  [on_device(): lax.psum((gram_local, projected_local), ('group', 'dev'))]
    gather x2 -> x0, local copies, waits for them, and re-layouts: 51.9 us -> none  [the longest x1 51.2 us: on_device(): wall_row[correlation][:, None, :] * normals]
    pallas_call x0 -> x9, Pallas kernels: none -> 14 us  [the longest x8 13.4 us: call(): pl.pallas_call(kernel, out_shape=out, scratch_shapes=list(scratch), compi...]
    unnamed x31 -> x52, local copies, waits for them, and re-layouts: 2.72 us -> 16.2 us
    all_to_all x3, waiting for transfers between devices: 13.6 us -> 22.9 us  [exchange(): return lax.all_to_all(value, AXES, split_axis=0, concat_axis=0, tiled=True)]
    dot_general x9 -> x0, matrix products: 8.91 us -> none  [the longest x1 1.87 us: on_device(): jnp.einsum('bcj,bij->bci', earlier, coupling, preferred_element_type=jnp....]
    all_to_all x3, starting transfers between devices: 29 us -> 21.5 us  [exchange(): return lax.all_to_all(value, AXES, split_axis=0, concat_axis=0, tiled=True)]
    sub x4 -> x0, other arithmetic: 4.05 us -> none  [the longest x3 3.7 us: rusanov(): 0.5 * (flux_left + flux_right)]
  transfers between devices with their start and end apart: 6 -> 7, of which waited for: 2 -> 3; matrix products, arithmetic and copies ran while one was open for 37% -> 0% of each run, Pallas kernels for 0% -> 12%
where the time goes in v1:
time: 81 us; the launch traced here: 80.2 us
  starting transfers between devices  26.3 us (32%)
  waiting for transfers between devices  22.9 us (28%)
  local copies, waits for them, and re-layouts  16.2 us (20%)
  Pallas kernels  14 us (17%)
    all_to_all x3, waiting for transfers between devices, exchange(): return lax.all_to_all(value, AXES, split_axis=0, concat_axis=0, tiled=True)  22.9 us
    all_to_all x3, starting transfers between devices, exchange(): return lax.all_to_all(value, AXES, split_axis=0, concat_axis=0, tiled=True)  21.5 us
    unnamed x52, local copies, waits for them, and re-layouts  16.2 us
    pallas_call x8, Pallas kernels, call(): pl.pallas_call(kernel, out_shape=out, scratch_shapes=list(scratch), compi...  13.4 us
    ppermute x1, starting transfers between devices, on_device(): below = lax.ppermute(own, AXES, ring)  3.03 us
    ppermute x1, starting transfers between devices, on_device(): bulk_below = lax.ppermute(bulk, AXES, ring)  1.82 us
  transfers between devices with their start and end apart: 7, of which 3 were waited for; matrix products, arithmetic and copies ran while one was open for 0% of the time, Pallas kernels for 12%

profile of v1, /device:TPU:1, one launch (start us, length us, event | category | flops | bytes accessed | tf_op | source)
XLA Modules:
  0.0 80.2 jit_solution(10563463421214054198)
XLA Ops:
  0.6 0.0 copy-start.2
  0.6 1.0 %copy-done.2 = f32[3,1,320,128]{3,2,1,0:T(8,128)S(1)} copy-done((f32[3,1,320,128]{3,2,1,0:T(8,128)S(1)}, f32[3,1,320,128]{3,2,1,0:T(8,128)}, u32[]{:S(2)}) %copy-start.2) | copy-done | bytes 491544
  1.7 0.9 %copy-done.8 = f32[1,320,128]{2,1,0:T(8,128)S(1)} copy-done((f32[1,320,128]{2,1,0:T(8,128)S(1)}, f32[1,320,128]{2,1,0:T(8,128)}, u32[]{:S(2)}) %copy-start.8) | copy-done | bytes 163864
  2.6 0.9 %copy-done.10 = f32[1,320,128]{2,1,0:T(8,128)S(1)} copy-done((f32[1,320,128]{2,1,0:T(8,128)S(1)}, f32[1,320,128]{2,1,0:T(8,128)}, u32[]{:S(2)}) %copy-start.10) | copy-done | bytes 163864
  3.5 0.8 copy-done.14
  4.3 0.9 %edges.1 = (f32[8,384]{1,0:T(8,128)S(1)}, f32[8,384]{1,0:T(8,128)S(1)}, bf16[5,320,128]{2,1,0:T(8,128)(2,1)}) custom-call(f32[1,320,128]{2,1,0:T(8,128)S(1)} %copy-done.8, f32[3,1,320,128]{3,2,1,0:T(8,128)S(1)} %copy-done.2, f32[1,320,128]{2,1,0:T(8,128)S(1)} %copy-done.10, f32[3,32,128]{2,1,0:T(8,128)S(1)} %bitcast.23), custom_call_target="tpu_custom_call" | custom-call | tf_op jit(solution)/shard_map/edges/pallas_call | solution.py:22
  5.2 3.0 %collective-permute-start.2 = (f32[8,384]{1,0:T(8,128)S(1)}, f32[8,384]{1,0:T(8,128)S(1)}, u32[]{:S(2)}, u32[]{:S(2)}) collective-permute-start(f32[8,384]{1,0:T(8,128)S(1)} %get-tuple-element.17.own_ref), channel_id=1, source_target_pairs={{0,1},{1,2},{2,3},{3,4},{4,5},{5,6},{6,7},{7,8},{8,9},{9,10},{10,1... | collective-permute-start | bytes 36872 | tf_op jit(solution)/shard_map/ppermute | solution.py:419
  8.3 0.0 collective-permute-start.3
  8.3 1.0 %copy-done.4 = f32[8,32,3,128]{3,1,2,0:T(8,128)S(1)} copy-done((f32[8,32,3,128]{3,1,2,0:T(8,128)S(1)}, f32[8,32,3,128]{3,1,2,0:T(8,128)}, u32[]{:S(2)}) %copy-start.4) | copy-done | bytes 393240
  9.3 0.7 copy-done.24
  9.9 0.7 copy-done.25
  10.6 0.5 routing.1
  11.1 0.0 copy-start.12
  11.1 0.8 copy-done.12
  11.9 0.0 collective-permute-done.2.below_ref
  11.9 0.0 collective-permute-done.3.above_ref
  11.9 1.6 %copy-done = bf16[64,128,128]{2,1,0:T(8,128)(2,1)S(1)} copy-done((bf16[64,128,128]{2,1,0:T(8,128)(2,1)S(1)}, bf16[64,128,128]{2,1,0:T(8,128)(2,1)}, u32[]{:S(2)}) %copy-start) | copy-done | bytes 2097176
  13.5 0.9 %copy-done.19 = f32[64,3,128]{2,0,1:T(8,128)S(1)} copy-done((f32[64,3,128]{2,0,1:T(8,128)S(1)}, f32[64,3,128]{2,0,1:T(8,128)}, u32[]{:S(2)}) %copy-start.19) | copy-done | bytes 98328
  14.4 0.8 copy-done.21
  15.1 2.0 %loads.1 = f32[1024,128]{1,0:T(8,128)} custom-call(f32[8,384]{1,0:T(8,128)S(1)} %get-tuple-element.17.own_ref, f32[8,384]{1,0:T(8,128)S(1)} %get-tuple-element.18.second_ref, f32[8,384]{1,0:T(8,128)S(1)} %collective-permute-done.2.below_ref, f32[8,384]{1,0:T(8,128)S(1)} %collective-permute-done.3.above_ref, s32[64,128]{1,0:T(8,128)S(1)} %copy-done.21, ...), custom_call_target="tpu_custom_call" | custom-call | tf_op jit(solution)/shard_map/loads/pallas_call | solution.py:22
  17.1 12.4 %all-to-all-start = ((f32[128,8,128]{2,1,0:T(8,128)}), f32[128,8,128]{2,1,0:T(8,128)S(1)}, u32[]{:S(2)}, u32[]{:S(2)}) async-start(f32[128,8,128]{2,1,0:T(8,128)} %bitcast.5), calls=%async_computation | async-start | bytes 1048576 | tf_op jit(solution)/shard_map/all_to_all | solution.py:394
  29.5 1.8 %collective-permute-start = (bf16[5,320,128]{2,1,0:T(8,128)(2,1)}, bf16[5,320,128]{2,1,0:T(8,128)(2,1)}, u32[]{:S(2)}, u32[]{:S(2)}) collective-permute-start(bf16[5,320,128]{2,1,0:T(8,128)(2,1)} %get-tuple-element.16), channel_id=1, source_target_pairs={{0,1},{1,2},{2,3},{3,4},{4,5},{5,6},{6,7},{7,8},{8,9},{9,10},{10,1... | collective-permute-start | bytes 1228808 | tf_op jit(solution)/shard_map/ppermute | solution.py:421
  31.4 0.0 collective-permute-start.1
  31.4 0.0 copy-done.6
  31.4 0.0 copy-done.15
  31.4 0.0 copy-start.7
  31.4 1.2 %copy-done.7 = bf16[32,128,128]{2,1,0:T(8,128)(2,1)S(1)} copy-done((bf16[32,128,128]{2,1,0:T(8,128)(2,1)S(1)}, bf16[32,128,128]{2,1,0:T(8,128)(2,1)}, u32[]{:S(2)}) %copy-start.7) | copy-done | bytes 1048600
  32.6 0.7 solid.1.kd_ref
  33.3 10.2 %all-to-all-done = f32[128,8,128]{2,1,0:T(8,128)S(1)} async-done(((f32[128,8,128]{2,1,0:T(8,128)}), f32[128,8,128]{2,1,0:T(8,128)S(1)}, u32[]{:S(2)}, u32[]{:S(2)}) %all-to-all-start) | async-done | bytes 524320 | tf_op jit(solution)/shard_map/all_to_all | solution.py:394
  43.5 0.0 copy-done.5
  43.5 1.0 %residual.1 = (f32[3,32,128]{2,1,0:T(8,128)S(1)}, f32[128,128]{1,0:T(8,128)}) custom-call(f32[1024,128]{1,0:T(8,128)S(1)} %bitcast.18, f32[3,32,128]{2,1,0:T(8,128)S(1)} %solid.1.kd_ref, f32[3,32,128]{2,1,0:T(8,128)S(1)} %bitcast.29, f32[3,32,128]{2,1,0:T(8,128)S(1)} %bitcast.25, f32[8,3,32,128]{3,2,1,0:T(8,128)S(1)} %bitcast.21), custom_call_target="tpu_custom_call" | custom-call | tf_op jit(solution)/shard_map/residual/pallas_call | solution.py:22
  44.5 4.3 %all-to-all-start.1 = ((f32[128,1,128]{2,1,0:T(1,128)}), f32[128,1,128]{2,1,0:T(1,128)S(1)}, u32[]{:S(2)}, u32[]{:S(2)}) async-start(f32[128,1,128]{2,1,0:T(1,128)} %bitcast.10), calls=%async_computation.1 | async-start | bytes 131072 | tf_op jit(solution)/shard_map/all_to_all | solution.py:394
  48.9 0.0 copy-start.1
  48.9 0.8 %factor.1 = (f32[8,128]{1,0:T(8,128)S(1)}, bf16[1024,128]{1,0:T(8,128)(2,1)S(1)}) custom-call(f32[1024,128]{1,0:T(8,128)S(1)} %bitcast.19), custom_call_target="tpu_custom_call" | custom-call | tf_op jit(solution)/shard_map/factor/pallas_call | solution.py:22
  49.7 0.7 copy-done.17
  50.4 0.6 copy-done.22
  51.0 7.2 %all-to-all-done.1 = f32[128,1,128]{2,1,0:T(1,128)S(1)} async-done(((f32[128,1,128]{2,1,0:T(1,128)}), f32[128,1,128]{2,1,0:T(1,128)S(1)}, u32[]{:S(2)}, u32[]{:S(2)}) %all-to-all-start.1) | async-done | bytes 65568 | tf_op jit(solution)/shard_map/all_to_all | solution.py:394
  58.3 1.0 %copy-done.16 = f32[8,32,3,128]{3,1,2,0:T(8,128)S(1)} copy-done((f32[8,32,3,128]{3,1,2,0:T(8,128)S(1)}, f32[8,32,3,128]{3,1,2,0:T(8,128)}, u32[]{:S(2)}) %copy-start.16) | copy-done | bytes 393240
  59.2 0.9 %copy-done.18 = bf16[1024,128]{1,0:T(8,128)(2,1)S(1)} copy-done((bf16[1024,128]{1,0:T(8,128)(2,1)S(1)}, bf16[1024,128]{1,0:T(8,128)(2,1)}, u32[]{:S(2)}) %copy-start.18) | copy-done | bytes 262168
  60.2 0.7 copy-done.23
  60.9 1.1 %update.1 = (f32[3,32,128]{2,1,0:T(8,128)}, bf16[1024,128]{1,0:T(8,128)(2,1)}) custom-call(f32[128,128]{1,0:T(8,128)S(1)} %bitcast.27, f32[8,128]{1,0:T(8,128)S(1)} %copy-done.23, f32[3,32,128]{2,1,0:T(8,128)S(1)} %get-tuple-element.24.base_ref, f32[8,3,32,128]{3,2,1,0:T(8,128)S(1)} %bitcast.26, bf16[1024,128]{1,0:T(8,128)(2,1)S(1)} %copy-done.18), custom_call_target="tpu_custom_call" | custom-call | tf_op jit(solution)/shard_map/update/pallas_call | solution.py:22
  62.0 4.8 %all-to-all-start.2 = ((bf16[128,8,128]{2,1,0:T(8,128)(2,1)}), bf16[128,8,128]{2,1,0:T(8,128)(2,1)S(1)}, u32[]{:S(2)}, u32[]{:S(2)}) async-start(bf16[128,8,128]{2,1,0:T(8,128)(2,1)} %bitcast.14), calls=%async_computation.2 | async-start | bytes 524288 | tf_op jit(solution)/shard_map/all_to_all | solution.py:394
  66.7 0.0 collective-permute-done.below_ref
  66.8 0.0 collective-permute-done.1.above_ref
  66.8 5.5 %fluid.1 = f32[5,1,320,128]{3,2,1,0:T(8,128)} custom-call(f32[1,320,128]{2,1,0:T(8,128)S(1)} %copy-done.9, f32[3,1,320,128]{3,2,1,0:T(8,128)S(1)} %copy-done.3, f32[1,320,128]{2,1,0:T(8,128)S(1)} %copy-done.11, bf16[5,320,128]{2,1,0:T(8,128)(2,1)} %collective-permute-done.below_ref, bf16[5,320,128]{2,1,0:T(8,128)(2,1)} %collective-permute-done.1.above_ref), custom_call_target="tpu_custom_call" | custom-call | tf_op jit(solution)/shard_map/fluid/pallas_call | solution.py:22
  72.3 5.4 %all-to-all-done.2 = bf16[128,8,128]{2,1,0:T(8,128)(2,1)S(1)} async-done(((bf16[128,8,128]{2,1,0:T(8,128)(2,1)}), bf16[128,8,128]{2,1,0:T(8,128)(2,1)S(1)}, u32[]{:S(2)}, u32[]{:S(2)}) %all-to-all-start.2) | async-done | bytes 262176 | tf_op jit(solution)/shard_map/all_to_all | solution.py:394
  77.7 1.0 %copy-done.13 = bf16[256,1024]{1,0:T(8,128)(2,1)S(1)} copy-done((bf16[256,1024]{1,0:T(8,128)(2,1)S(1)}, bf16[256,1024]{1,0:T(8,128)(2,1)}, u32[]{:S(2)}) %copy-start.13) | copy-done | bytes 524312
  78.7 1.5 %motion.1 = f32[3,64,128]{2,1,0:T(8,128)} custom-call(bf16[1024,128]{1,0:T(8,128)(2,1)S(1)} %bitcast.22, bf16[256,1024]{1,0:T(8,128)(2,1)S(1)} %copy-done.13, bf16[64,128,128]{2,1,0:T(8,128)(2,1)S(1)} %copy-done.1), custom_call_target="tpu_custom_call" | custom-call | tf_op jit(solution)/shard_map/motion/pallas_call | solution.py:22
  (27 shorter events, 0.0 us)
Async XLA Ops:
  0.6 1.0 %copy-start.2 = (f32[3,1,320,128]{3,2,1,0:T(8,128)S(1)}, f32[3,1,320,128]{3,2,1,0:T(8,128)}, u32[]{:S(2)}) copy-start(f32[3,1,320,128]{3,2,1,0:T(8,128)} %vel_ref.3) | copy-start | bytes 1474564
  1.7 0.9 %copy-start.8 = (f32[1,320,128]{2,1,0:T(8,128)S(1)}, f32[1,320,128]{2,1,0:T(8,128)}, u32[]{:S(2)}) copy-start(f32[1,320,128]{2,1,0:T(8,128)} %dens_ref.3) | copy-start | bytes 491524
  2.6 0.9 %copy-start.10 = (f32[1,320,128]{2,1,0:T(8,128)S(1)}, f32[1,320,128]{2,1,0:T(8,128)}, u32[]{:S(2)}) copy-start(f32[1,320,128]{2,1,0:T(8,128)} %press_ref.3) | copy-start | bytes 491524
  3.5 0.8 copy-start.14
  5.2 6.6 %collective-permute-start.2 = (f32[8,384]{1,0:T(8,128)S(1)}, f32[8,384]{1,0:T(8,128)S(1)}, u32[]{:S(2)}, u32[]{:S(2)}) collective-permute-start(f32[8,384]{1,0:T(8,128)S(1)} %get-tuple-element.17.own_ref), channel_id=1, source_target_pairs={{0,1},{1,2},{2,3},{3,4},{4,5},{5,6},{6,7},{7,8},{8,9},{9,10},{10,1... | collective-permute-start | bytes 36872 | tf_op jit(solution)/shard_map/ppermute | solution.py:419
  8.3 3.6 %collective-permute-start.3 = (f32[8,384]{1,0:T(8,128)S(1)}, f32[8,384]{1,0:T(8,128)S(1)}, u32[]{:S(2)}, u32[]{:S(2)}) collective-permute-start(f32[8,384]{1,0:T(8,128)S(1)} %get-tuple-element.17.own_ref), channel_id=1, source_target_pairs={{1,0},{2,1},{3,2},{4,3},{5,4},{6,5},{7,6},{8,7},{9,8},{10,9},{11,1... | collective-permute-start | bytes 36872 | tf_op jit(solution)/shard_map/ppermute | solution.py:420
  8.3 1.0 %copy-start.4 = (f32[8,32,3,128]{3,1,2,0:T(8,128)S(1)}, f32[8,32,3,128]{3,1,2,0:T(8,128)}, u32[]{:S(2)}) copy-start(f32[8,32,3,128]{3,1,2,0:T(8,128)} %param.26) | copy-start | bytes 1179652
  9.3 0.7 copy-start.24
  9.9 0.7 copy-start.25
  11.1 0.8 copy-start.12
  11.9 1.6 %copy-start = (bf16[64,128,128]{2,1,0:T(8,128)(2,1)S(1)}, bf16[64,128,128]{2,1,0:T(8,128)(2,1)}, u32[]{:S(2)}) copy-start(bf16[64,128,128]{2,1,0:T(8,128)(2,1)} %rbf_ref.3) | copy-start | bytes 6291460
  13.5 0.9 %copy-start.19 = (f32[64,3,128]{2,0,1:T(8,128)S(1)}, f32[64,3,128]{2,0,1:T(8,128)}, u32[]{:S(2)}) copy-start(f32[64,3,128]{2,0,1:T(8,128)} %param.19) | copy-start | bytes 294916
  14.4 0.8 copy-start.21
  15.1 16.2 %copy-start.6 = (bf16[32,128,128]{2,1,0:T(8,128)(2,1)S(1)}, bf16[32,128,128]{2,1,0:T(8,128)(2,1)}, u32[]{:S(2)}) copy-start(bf16[32,128,128]{2,1,0:T(8,128)(2,1)} %stiff_ref.1) | copy-start | bytes 3145732
  15.1 16.2 %copy-start.15 = (f32[32,3,128]{2,0,1:T(8,128)S(1)}, f32[32,3,128]{2,0,1:T(8,128)}, u32[]{:S(2)}) copy-start(f32[32,3,128]{2,0,1:T(8,128)} %param.25) | copy-start | bytes 147460
  17.1 26.4 %copy-start.5 = (f32[8,32,3,128]{3,1,2,0:T(8,128)S(1)}, f32[8,32,3,128]{3,1,2,0:T(8,128)}, u32[]{:S(2)}) copy-start(f32[8,32,3,128]{3,1,2,0:T(8,128)} %param.26) | copy-start | bytes 1179652
  17.1 26.4 %copy-start.20 = (f32[32,3,128]{2,0,1:T(8,128)S(1)}, f32[32,3,128]{2,0,1:T(8,128)}, u32[]{:S(2)}) copy-start(f32[32,3,128]{2,0,1:T(8,128)} %param.24) | copy-start | bytes 147460
  17.1 26.4 %all-to-all-start = ((f32[128,8,128]{2,1,0:T(8,128)}), f32[128,8,128]{2,1,0:T(8,128)S(1)}, u32[]{:S(2)}, u32[]{:S(2)}) async-start(f32[128,8,128]{2,1,0:T(8,128)} %bitcast.5), calls=%async_computation | async-start | bytes 1048576 | tf_op jit(solution)/shard_map/all_to_all | solution.py:394
  29.5 37.2 %collective-permute-start = (bf16[5,320,128]{2,1,0:T(8,128)(2,1)}, bf16[5,320,128]{2,1,0:T(8,128)(2,1)}, u32[]{:S(2)}, u32[]{:S(2)}) collective-permute-start(bf16[5,320,128]{2,1,0:T(8,128)(2,1)} %get-tuple-element.16), channel_id=1, source_target_pairs={{0,1},{1,2},{2,3},{3,4},{4,5},{5,6},{6,7},{7,8},{8,9},{9,10},{10,1... | collective-permute-start | bytes 1228808 | tf_op jit(solution)/shard_map/ppermute | solution.py:421
  31.4 35.4 %collective-permute-start.1 = (bf16[5,320,128]{2,1,0:T(8,128)(2,1)}, bf16[5,320,128]{2,1,0:T(8,128)(2,1)}, u32[]{:S(2)}, u32[]{:S(2)}) collective-permute-start(bf16[5,320,128]{2,1,0:T(8,128)(2,1)} %get-tuple-element.16), channel_id=1, source_target_pairs={{1,0},{2,1},{3,2},{4,3},{5,4},{6,5},{7,6},{8,7},{9,8},{10,9},{11,1... | collective-permute-start | bytes 1228808 | tf_op jit(solution)/shard_map/ppermute | solution.py:422
  31.4 1.2 %copy-start.7 = (bf16[32,128,128]{2,1,0:T(8,128)(2,1)S(1)}, bf16[32,128,128]{2,1,0:T(8,128)(2,1)}, u32[]{:S(2)}) copy-start(bf16[32,128,128]{2,1,0:T(8,128)(2,1)} %coup_ref.1) | copy-start | bytes 3145732
  32.6 34.2 %copy-start.3 = (f32[3,1,320,128]{3,2,1,0:T(8,128)S(1)}, f32[3,1,320,128]{3,2,1,0:T(8,128)}, u32[]{:S(2)}) copy-start(f32[3,1,320,128]{3,2,1,0:T(8,128)} %vel_ref.3) | copy-start | bytes 1474564
  32.6 34.2 %copy-start.9 = (f32[1,320,128]{2,1,0:T(8,128)S(1)}, f32[1,320,128]{2,1,0:T(8,128)}, u32[]{:S(2)}) copy-start(f32[1,320,128]{2,1,0:T(8,128)} %dens_ref.3) | copy-start | bytes 491524
  32.6 34.2 %copy-start.11 = (f32[1,320,128]{2,1,0:T(8,128)S(1)}, f32[1,320,128]{2,1,0:T(8,128)}, u32[]{:S(2)}) copy-start(f32[1,320,128]{2,1,0:T(8,128)} %press_ref.3) | copy-start | bytes 491524
  44.5 13.7 %all-to-all-start.1 = ((f32[128,1,128]{2,1,0:T(1,128)}), f32[128,1,128]{2,1,0:T(1,128)S(1)}, u32[]{:S(2)}, u32[]{:S(2)}) async-start(f32[128,1,128]{2,1,0:T(1,128)} %bitcast.10), calls=%async_computation.1 | async-start | bytes 131072 | tf_op jit(solution)/shard_map/all_to_all | solution.py:394
  48.9 28.8 %copy-start.1 = (bf16[64,128,128]{2,1,0:T(8,128)(2,1)S(1)}, bf16[64,128,128]{2,1,0:T(8,128)(2,1)}, u32[]{:S(2)}) copy-start(bf16[64,128,128]{2,1,0:T(8,128)(2,1)} %rbf_ref.3) | copy-start | bytes 6291460
  49.7 0.7 copy-start.17
  50.4 0.6 copy-start.22
  58.2 1.0 %copy-start.16 = (f32[8,32,3,128]{3,1,2,0:T(8,128)S(1)}, f32[8,32,3,128]{3,1,2,0:T(8,128)}, u32[]{:S(2)}) copy-start(f32[8,32,3,128]{3,1,2,0:T(8,128)} %param.27) | copy-start | bytes 1179652
  59.2 0.9 %copy-start.18 = (bf16[1024,128]{1,0:T(8,128)(2,1)S(1)}, bf16[1024,128]{1,0:T(8,128)(2,1)}, u32[]{:S(2)}) copy-start(bf16[1024,128]{1,0:T(8,128)(2,1)} %copy-done.17) | copy-start | bytes 786436
  60.2 0.7 copy-start.23
  62.0 15.7 %all-to-all-start.2 = ((bf16[128,8,128]{2,1,0:T(8,128)(2,1)}), bf16[128,8,128]{2,1,0:T(8,128)(2,1)S(1)}, u32[]{:S(2)}, u32[]{:S(2)}) async-start(bf16[128,8,128]{2,1,0:T(8,128)(2,1)} %bitcast.14), calls=%async_computation.2 | async-start | bytes 524288 | tf_op jit(solution)/shard_map/all_to_all | solution.py:394
  77.7 1.0 %copy-start.13 = (bf16[256,1024]{1,0:T(8,128)(2,1)S(1)}, bf16[256,1024]{1,0:T(8,128)(2,1)}, u32[]{:S(2)}) copy-start(bf16[256,1024]{1,0:T(8,128)(2,1)} %copy-done.12) | copy-start | bytes 1572868

commit v2 on v1

--- a/solution.py
+++ b/solution.py
@@ -9,7 +9,7 @@
 
 AXES = ("group", "dev")
 ratio_heat = 1.4
-step_ratio = 0.03
+half_step = 0.5 * 0.03
 f32 = jnp.float32
 bf16 = jnp.bfloat16
 
@@ -18,14 +18,42 @@
     return lax.broadcasted_iota(jnp.int32, shape, dim)
 
 
-def call(kernel, out, *args, scratch=(), limit=48):
+def call(kernel, out, *args, fetched=(), remote=(), scalars=(), scratch=(), limit=48):
+    held = (*fetched, *remote)
+    buffers = [pltpu.VMEM(args[i].shape, args[i].dtype) for i in fetched]
+    if fetched:
+        buffers.append(pltpu.SemaphoreType.DMA((len(fetched),)))
+    args = [
+        pltpu.with_memory_space_constraint(x, pltpu.HBM) if i in held else x
+        for i, x in enumerate(args)
+    ]
     return pl.pallas_call(
         kernel,
         out_shape=out,
-        scratch_shapes=list(scratch),
+        in_specs=[
+            pl.BlockSpec(
+                memory_space=pltpu.HBM
+                if i in held
+                else pltpu.SMEM
+                if i in scalars
+                else pltpu.VMEM
+            )
+            for i in range(len(args))
+        ],
+        scratch_shapes=buffers + list(scratch),
         compiler_params=pltpu.CompilerParams(vmem_limit_bytes=limit * 2**20),
         name=kernel.__name__,
     )(*args)
+
+
+def fetch(sources, buffers, semaphores):
+    copies = [
+        pltpu.make_async_copy(source, buffer, semaphores.at[i])
+        for i, (source, buffer) in enumerate(zip(sources, buffers))
+    ]
+    for copy in copies:
+        copy.start()
+    return copies
 
 
 def shape(dims, dtype=f32):
@@ -40,7 +68,8 @@
 
 
 def sound(cell):
-    return jnp.sqrt(ratio_heat * cell[4] / cell[0])
+    scaled = ratio_heat * cell[4]
+    return scaled * lax.rsqrt(scaled * cell[0])
 
 
 def with_speed(cell):
@@ -63,29 +92,57 @@
     flux_right, speed_right = euler_flux(right, axis)
     top = jnp.maximum(speed_left, speed_right)
     return [
-        0.5 * (a + b - top * (r - l))
+        a + b - top * (r - l)
         for a, b, l, r in zip(flux_left, flux_right, left[1], right[1])
     ]
 
 
+def divergence(left, me, right, axis):
+    flux_left, speed_left = euler_flux(left, axis)
+    flux_right, speed_right = euler_flux(right, axis)
+    own = jnp.abs(me[0][1 + axis]) + me[2]
+    low, high = jnp.maximum(speed_left, own), jnp.maximum(own, speed_right)
+    return [
+        b - a - high * (r - c) + low * (c - l)
+        for a, b, l, c, r in zip(flux_left, flux_right, left[1], me[1], right[1])
+    ]
+
+
 def wall_flux(state):
     cell, cons, speed = state
-    return cons[3] * cell[3] + cell[4] - (jnp.abs(cell[3]) + speed) * cons[3]
-
-
-def edges(dens_ref, vel_ref, press_ref, disp_ref, send_ref, second_ref, bulk_ref):
+    return 2.0 * (cons[3] * cell[3] + cell[4] - (jnp.abs(cell[3]) + speed) * cons[3])
+
+
+def edges(
+    dens_hbm, vel_hbm, press_hbm, disp_hbm, send_ref, second_ref,
+    dens_ref, vel_ref, press_ref, disp_ref, semaphores,
+):
+    copies = fetch(
+        (dens_hbm, vel_hbm, press_hbm, disp_hbm),
+        (dens_ref, vel_ref, press_ref, disp_ref),
+        semaphores,
+    )
     depth, lanes = dens_ref.shape[1:]
     wide = send_ref.shape[1]
     lane = iota((depth, lanes), 1)
     packed = jnp.ones((depth, lanes), f32)
-    rows = [dens_ref[0], vel_ref[0, 0], vel_ref[1, 0], vel_ref[2, 0], press_ref[0]]
-    for i, row in enumerate(rows):
-        bulk_ref[i] = row.astype(bf16)
+    rows = [
+        (copies[0], dens_ref.at[0]),
+        (copies[1], vel_ref.at[0, 0]),
+        (None, vel_ref.at[1, 0]),
+        (None, vel_ref.at[2, 0]),
+        (copies[2], press_ref.at[0]),
+    ]
+    for i, (copy, ref) in enumerate(rows):
+        if copy is not None:
+            copy.wait()
+        row = ref[...]
         moved = row if i == 0 else pltpu.roll(row, 2 * i, 1)
         packed = jnp.where((lane >> 1) == i, moved, packed)
     packed = jnp.concatenate([packed, jnp.ones((wide - depth, lanes), f32)], axis=0)
     turned = packed.T
     last = disp_ref.shape[1] - 1
+    copies[3].wait()
     for i in range(5):
         send_ref[i : i + 1, :] = turned[2 * i : 2 * i + 1, :]
         second_ref[i : i + 1, :] = turned[2 * i + 1 : 2 * i + 2, :]
@@ -96,7 +153,16 @@
     second_ref[5:8, :] = jnp.zeros((3, wide), f32)
 
 
-def fluid(dens_ref, vel_ref, press_ref, below_ref, above_ref, next_ref):
+def fluid(
+    dens_hbm, vel_hbm, press_hbm, below_hbm, above_hbm, next_ref,
+    dens_ref, vel_ref, press_ref, below_ref, above_ref, semaphores,
+):
+    for copy in fetch(
+        (dens_hbm, vel_hbm, press_hbm, below_hbm, above_hbm),
+        (dens_ref, vel_ref, press_ref, below_ref, above_ref),
+        semaphores,
+    ):
+        copy.wait()
     depth, lanes = dens_ref.shape[1:]
     rows = 16
     sub = iota((rows, lanes), 0)
@@ -120,9 +186,7 @@
         me = with_speed(cell)
         below = with_speed([below_ref[q, at, :].astype(f32) for q in range(5)])
         above = with_speed([above_ref[q, at, :].astype(f32) for q in range(5)])
-        total = [
-            b - a for a, b in zip(rusanov(below, me, 0), rusanov(me, above, 0))
-        ]
+        total = divergence(below, me, above, 0)
         beside = with_speed(
             [
                 jnp.where(sub == rows - 1, n[0:1, :], pltpu.roll(x, rows - 1, 0))
@@ -144,7 +208,7 @@
             lower = jnp.where(
                 lane == 0, wall if q == 3 else 0.0, pltpu.roll(face[q], 1, 1)
             )
-            next_ref[q, 0, at, :] = me[1][q] - step_ratio * (total[q] + face[q] - lower)
+            next_ref[q, 0, at, :] = me[1][q] - half_step * (total[q] + face[q] - lower)
         return carried
 
     first = with_speed([x[0:1, :] for x in load(pl.ds(0, 8))])
@@ -156,12 +220,7 @@
     wide = own[0].shape[1]
     lane = iota((1, wide), 1)
     me = with_speed(own)
-    total = [
-        b - a
-        for a, b in zip(
-            rusanov(with_speed(below), me, 0), rusanov(me, with_speed(above), 0)
-        )
-    ]
+    total = divergence(with_speed(below), me, with_speed(above), 0)
 
     def up(x):
         return jnp.where(lane == depth - 1, x[:, 0:1], pltpu.roll(x, wide - 1, 1))
@@ -174,13 +233,26 @@
     face = rusanov(me, with_speed(second), 2)
     total = [t + f for t, f in zip(total, face)]
     total[3] = total[3] - wall_flux(me)
-    q = [c - step_ratio * t for c, t in zip(me[1], total)]
+    q = [c - half_step * t for c, t in zip(me[1], total)]
     return (ratio_heat - 1.0) * (
         q[4] - 0.5 * (q[1] * q[1] + q[2] * q[2] + q[3] * q[3]) / q[0]
     )
 
 
-def routing(routes_ref, targets_ref, diff_ref, scatter_ref, pick_ref, tag_ref, gram_ref):
+def routing(
+    routes_hbm, targets_hbm, diff_hbm, dens_hbm, vel_hbm, press_hbm,
+    corr_hbm, normals_hbm, rbf_hbm,
+    scatter_ref, slot_ref, tag_ref, gram_ref, bulk_ref, corr_ref, normals_ref, rbf_ref,
+    routes_ref, targets_ref, diff_ref, dens_ref, vel_ref, press_ref, semaphores, ahead,
+):
+    copies = fetch(
+        (routes_hbm, targets_hbm, diff_hbm, dens_hbm, vel_hbm, press_hbm),
+        (routes_ref, targets_ref, diff_ref, dens_ref, vel_ref, press_ref),
+        semaphores,
+    )
+    later = fetch((corr_hbm, normals_hbm, rbf_hbm), (corr_ref, normals_ref, rbf_ref), ahead)
+    copies[0].wait()
+    copies[1].wait()
     count = routes_ref.shape[1]
     spread, taken = scatter_ref.shape
     peers = tag_ref.shape[0]
@@ -205,9 +277,7 @@
     comp = iota((taken, 1), 0) & 3
     at_col = jnp.sum(jnp.where(own, slot_row, 0.0), axis=1, keepdims=True)
     at_col = jnp.where(comp < 3, at_col + comp.astype(f32), -1.0)
-    pick_ref[...] = jnp.where(
-        iota((taken, spread), 1).astype(f32) == at_col, 1.0, 0.0
-    ).astype(bf16)
+    slot_ref[...] = at_col
     to_peer = jnp.where(
         iota((peers, count), 0).astype(f32) == route_row[0:1, :], 1.0, 0.0
     )
@@ -217,6 +287,7 @@
     tag_ref[...] = (
         jnp.dot(to_peer.astype(bf16), named.astype(bf16), preferred_element_type=f32) - 1.0
     )
+    copies[2].wait()
     columns = diff_ref.shape[0]
     lanes = diff_ref.shape[3]
     sums = {}
@@ -230,6 +301,12 @@
     col = jnp.sum(stacked, axis=1, keepdims=True)
     diag = iota((columns * columns, lanes), 0) == iota((columns * columns, lanes), 1)
     gram_ref[...] = jnp.sum(jnp.where(diag, col, 0.0), axis=0, keepdims=True)
+    for copy in copies[3:] + later:
+        copy.wait()
+    bulk_ref[0] = dens_ref[0].astype(bf16)
+    for c in range(3):
+        bulk_ref[1 + c] = vel_ref[c, 0].astype(bf16)
+    bulk_ref[4] = press_ref[0].astype(bf16)
 
 
 def thirds(value):
@@ -240,7 +317,10 @@
 
 
 def exact_dot(onehot, value):
-    return sum(jnp.dot(onehot, part, preferred_element_type=f32) for part in thirds(value))
+    parts = jnp.concatenate(thirds(value), axis=1)
+    made = jnp.dot(onehot, parts, preferred_element_type=f32)
+    lanes = value.shape[1]
+    return made[:, :lanes] + made[:, lanes : 2 * lanes] + made[:, 2 * lanes :]
 
 
 def pick_half(both):
@@ -283,7 +363,11 @@
     send_ref[pl.ds(7, peers, stride=8), :] = jnp.broadcast_to(gram_ref[...], tag_ref.shape)
 
 
-def solid(keep_ref, disp_ref, below_ref, stiff_ref, coup_ref, out_ref, here, prior, made):
+def solid(
+    keep_ref, disp_ref, below_ref, stiff_hbm, coup_hbm, out_ref,
+    stiff_ref, coup_ref, semaphores, here, prior, made,
+):
+    copies = fetch((stiff_hbm, coup_hbm), (stiff_ref, coup_ref), semaphores)
     count, nodes = disp_ref.shape[1:]
     for c in range(3):
         here[pl.ds(c, count, stride=4), :] = disp_ref[c]
@@ -292,6 +376,8 @@
         prior[c : c + 1, :] = jnp.where(keep_ref[0] > 0, first, 0.0)
     here[pl.ds(3, count, stride=4), :] = jnp.zeros((count, nodes), f32)
     prior[pl.ds(3, count + 1, stride=4), :] = jnp.zeros((count + 1, nodes), f32)
+    for copy in copies:
+        copy.wait()
     for k in range(count // 2):
         rows = slice(8 * k, 8 * k + 8)
         left = jnp.concatenate([here[rows, :], prior[rows, :]], axis=1).astype(bf16)
@@ -379,9 +465,11 @@
     ).astype(bf16)
 
 
-def motion(back_ref, pick_ref, rbf_ref, out_ref, picked, made):
+def motion(back_ref, slot_ref, rbf_ref, out_ref, picked, made):
     count = rbf_ref.shape[0]
-    picked[...] = jnp.dot(pick_ref[...], back_ref[...], preferred_element_type=f32)
+    whole = (slot_ref.shape[0], back_ref.shape[0])
+    pick = jnp.where(iota(whole, 1).astype(f32) == slot_ref[...], 1.0, 0.0).astype(bf16)
+    picked[...] = jnp.dot(pick, back_ref[...], preferred_element_type=f32)
     for k in range(count // 2):
         rows = slice(8 * k, 8 * k + 8)
         both = jnp.concatenate([rbf_ref[2 * k], rbf_ref[2 * k + 1]], axis=0)
@@ -411,49 +499,56 @@
     ring = [(i, (i + 1) % peers) for i in range(peers)]
     back = [(j, i) for i, j in ring]
 
-    own, second, bulk = call(
+    own, second = call(
         edges,
-        [shape((8, wide)), shape((8, wide)), shape((5, depth, lanes), bf16)],
+        [shape((8, wide)), shape((8, wide))],
         density, velocity, pressure, displacement,
-    )
+        fetched=(0, 1, 2, 3),
+    )
+    above = lax.ppermute(own, AXES, back)
     below = lax.ppermute(own, AXES, ring)
-    above = lax.ppermute(own, AXES, back)
-    bulk_below = lax.ppermute(bulk, AXES, ring)
-    bulk_above = lax.ppermute(bulk, AXES, back)
-    scatter, pick, tag, gram = call(
+    scatter, slot, tag, gram, bulk, corr_near, normals_near, rbf_near = call(
         routing,
         [
             shape((8 * peers, 4 * count), bf16),
-            shape((4 * count, 8 * peers), bf16),
+            shape((4 * count, 1)),
             shape((peers, nodes)),
             shape((1, nodes)),
+            shape((5, depth, lanes), bf16),
+            shape(correlation.shape, jnp.int32),
+            shape(normals.shape),
+            shape(rbf.shape, bf16),
         ],
         routes.reshape(1, count), targets.reshape(1, count), diff_res,
-    )
+        density, velocity, pressure, correlation, normals, rbf,
+        fetched=(0, 1, 2, 3, 4, 5),
+        remote=(6, 7, 8),
+        scratch=[pltpu.SemaphoreType.DMA((3,))],
+    )
+    bulk_below = lax.ppermute(bulk, AXES, ring)
+    bulk_above = lax.ppermute(bulk, AXES, back)
     kernel = functools.partial(loads, depth)
     kernel.__name__ = "loads"
     sent = call(
         kernel,
         shape((8 * peers, nodes)),
-        own, second, below, above, correlation, normals, rbf, scatter, tag, gram,
+        own, second, below, above, corr_near, normals_near, rbf_near, scatter, tag, gram,
         scratch=[pltpu.VMEM((4 * count, nodes), f32)] * 2,
     )
     got = exchange(sent.reshape(peers, 8, nodes)).reshape(8 * peers, nodes)
     keep = (lax.axis_index(AXES) > 0).astype(jnp.int32).reshape(1)
-    stiff_call = pl.pallas_call(
+    product = call(
         solid,
-        out_shape=shape((3, blocks, nodes)),
-        in_specs=[pl.BlockSpec(memory_space=pltpu.SMEM)]
-        + [pl.BlockSpec(memory_space=pltpu.VMEM)] * 4,
-        scratch_shapes=[
+        shape((3, blocks, nodes)),
+        keep, displacement, below, stiffness, coupling,
+        fetched=(3, 4),
+        scalars=(0,),
+        scratch=[
             pltpu.VMEM((4 * blocks, nodes), f32),
             pltpu.VMEM((4 * blocks + 8, nodes), f32),
             pltpu.VMEM((4 * blocks, nodes), f32),
         ],
-        compiler_params=pltpu.CompilerParams(vmem_limit_bytes=48 * 2**20),
-        name="solid",
-    )
-    product = stiff_call(keep, displacement, below, stiffness, coupling)
+    )
     base, share = call(
         residual,
         [shape((3, blocks, nodes)), shape((peers, nodes))],
@@ -475,11 +570,12 @@
         fluid,
         shape((5, 1, depth, lanes)),
         density, velocity, pressure, bulk_below, bulk_above,
+        fetched=(0, 1, 2, 3, 4),
     )
     wall_motion = call(
         motion,
         shape((3, count, nodes)),
-        returned, pick, rbf,
+        returned, slot, rbf,
         scratch=[pltpu.VMEM((4 * count, nodes), f32)] * 2,
     )
     return (

time: 81 us -> 70.7 us (0.87)
  local copies, waits for them, and re-layouts: 16.2 us -> 0.02 us
  Pallas kernels: 14 us -> 18.8 us
  waiting for transfers between devices: 22.9 us -> 23.8 us
    unnamed x52 -> x10, local copies, waits for them, and re-layouts: 16.2 us -> 0.02 us
    pallas_call x9, Pallas kernels: 14 us -> 18.8 us  [call(): pl.pallas_call(kernel, out_shape=out, in_specs=[pl.BlockSpec(memory_space...]
  transfers between devices with their start and end apart: 7 -> 7, of which waited for: 3 -> 4; matrix products, arithmetic and copies ran while one was open for 0% -> 0% of each run, Pallas kernels for 12% -> 20%
where the time goes in v2:
time: 70.7 us; the launch traced here: 70.3 us
  starting transfers between devices  27 us (38%)
  waiting for transfers between devices  23.8 us (34%)
  Pallas kernels  18.8 us (27%)
  between operations  0.73 us (1%)
    all_to_all x3, waiting for transfers between devices, exchange(): return lax.all_to_all(value, AXES, split_axis=0, concat_axis=0, tiled=True)  23.6 us
    all_to_all x3, starting transfers between devices, exchange(): return lax.all_to_all(value, AXES, split_axis=0, concat_axis=0, tiled=True)  22.1 us
    pallas_call x9, Pallas kernels, call(): pl.pallas_call(kernel, out_shape=out, in_specs=[pl.BlockSpec(memory_space...  18.8 us
    ppermute x1, starting transfers between devices, on_device(): below = lax.ppermute(own, AXES, ring)  3.1 us
    ppermute x1, starting transfers between devices, on_device(): bulk_below = lax.ppermute(bulk, AXES, ring)  1.82 us
  transfers between devices with their start and end apart: 7, of which 4 were waited for; matrix products, arithmetic and copies ran while one was open for 0% of the time, Pallas kernels for 20%

profile of v2, /device:TPU:1, one launch (start us, length us, event | category | flops | bytes accessed | tf_op | source)
XLA Modules:
  0.0 70.3 jit_solution(2702853952610487257)
XLA Ops:
  0.6 1.5 %edges.1 = (f32[8,384]{1,0:T(8,128)S(1)}, f32[8,384]{1,0:T(8,128)S(1)}) custom-call(f32[1,320,128]{2,1,0:T(8,128)} %dens_hbm.5, f32[3,1,320,128]{3,2,1,0:T(8,128)} %vel_hbm.5, f32[1,320,128]{2,1,0:T(8,128)} %press_hbm.5, f32[3,32,128]{2,1,0:T(8,128)} %bitcast.23), custom_call_target="tpu_custom_call" | custom-call | tf_op jit(solution)/shard_map/edges/pallas_call | solution.py:30
  2.2 3.1 %collective-permute-start.2 = (f32[8,384]{1,0:T(8,128)S(1)}, f32[8,384]{1,0:T(8,128)S(1)}, u32[]{:S(2)}, u32[]{:S(2)}) collective-permute-start(f32[8,384]{1,0:T(8,128)S(1)} %get-tuple-element.20.own_ref), channel_id=1, source_target_pairs={{0,1},{1,2},{2,3},{3,4},{4,5},{5,6},{6,7},{7,8},{8,9},{9,10},{10,1... | collective-permute-start | bytes 36872 | tf_op jit(solution)/shard_map/ppermute | solution.py:509
  5.3 0.0 collective-permute-start.3
  5.3 3.0 %routing.1 = (bf16[1024,256]{1,0:T(8,128)(2,1)S(1)}, f32[256,1]{1,0:T(8,128)S(1)}, f32[128,128]{1,0:T(8,128)S(1)}, f32[1,128]{1,0:T(1,128)S(1)}, bf16[5,320,128]...) custom-call(s32[1,64]{1,0:T(1,128)} %bitcast.31, ...), custom_call_target="tpu_custom_call" | custom-call | tf_op jit(solution)/shard_map/routing/pallas_call | solution.py:30
  8.2 0.0 collective-permute-done.2.below_ref
  8.2 0.1 collective-permute-done.3.above_ref
  8.4 0.0 copy-start.2
  8.4 1.9 %loads.1 = f32[1024,128]{1,0:T(8,128)} custom-call(f32[8,384]{1,0:T(8,128)S(1)} %get-tuple-element.20.own_ref, f32[8,384]{1,0:T(8,128)S(1)} %get-tuple-element.21.second_ref, f32[8,384]{1,0:T(8,128)S(1)} %collective-permute-done.2.below_ref, f32[8,384]{1,0:T(8,128)S(1)} %collective-permute-done.3.above_ref, s32[64,128]{1,0:T(8,128)S(1)} %get-tuple-element.22.corr_ref, ...), custom_call_target="tpu_custom_call" | custom-call | tf_op jit(solution)/shard_map/loads/pallas_call | solution.py:30
  10.2 0.0 copy-start.1
  10.3 0.0 copy-start.4
  10.3 13.0 %all-to-all-start = ((f32[128,8,128]{2,1,0:T(8,128)}), f32[128,8,128]{2,1,0:T(8,128)S(1)}, u32[]{:S(2)}, u32[]{:S(2)}) async-start(f32[128,8,128]{2,1,0:T(8,128)} %bitcast.5), calls=%async_computation | async-start | bytes 1048576 | tf_op jit(solution)/shard_map/all_to_all | solution.py:482
  23.2 0.0 copy-start.3
  23.2 1.8 %collective-permute-start = (bf16[5,320,128]{2,1,0:T(8,128)(2,1)}, bf16[5,320,128]{2,1,0:T(8,128)(2,1)}, u32[]{:S(2)}, u32[]{:S(2)}) collective-permute-start(bf16[5,320,128]{2,1,0:T(8,128)(2,1)} %get-tuple-element.19), channel_id=1, source_target_pairs={{0,1},{1,2},{2,3},{3,4},{4,5},{5,6},{6,7},{7,8},{8,9},{9,10},{10,1... | collective-permute-start | bytes 1228808 | tf_op jit(solution)/shard_map/ppermute | solution.py:528
  25.1 0.0 collective-permute-start.1
  25.1 0.0 copy-done.2
  25.1 2.2 %solid.1.kd_ref = f32[3,32,128]{2,1,0:T(8,128)S(1)} custom-call(s32[1]{0:T(128)} %bitcast.7.keep_ref, f32[3,32,128]{2,1,0:T(8,128)S(1)} %bitcast.24, f32[8,384]{1,0:T(8,128)S(1)} %collective-permute-done.2.below_ref, bf16[32,128,128]{2,1,0:T(8,128)(2,1)} %stiff_hbm.1, bf16[32,128,128]{2,1,0:T(8,128)(2,1)} %coup_hbm.1), custom_call_target="tpu_custom_call" | custom-call | tf_op jit(solution)/shard_map/solid/pallas_call | solution.py:30
  27.3 9.9 %all-to-all-done = f32[128,8,128]{2,1,0:T(8,128)S(1)} async-done(((f32[128,8,128]{2,1,0:T(8,128)}), f32[128,8,128]{2,1,0:T(8,128)S(1)}, u32[]{:S(2)}, u32[]{:S(2)}) %all-to-all-start) | async-done | bytes 524320 | tf_op jit(solution)/shard_map/all_to_all | solution.py:482
  37.2 0.0 copy-done.1
  37.2 0.0 copy-done.4
  37.2 1.0 %residual.1 = (f32[3,32,128]{2,1,0:T(8,128)S(1)}, f32[128,128]{1,0:T(8,128)}) custom-call(f32[1024,128]{1,0:T(8,128)S(1)} %bitcast.18, f32[3,32,128]{2,1,0:T(8,128)S(1)} %solid.1.kd_ref, f32[3,32,128]{2,1,0:T(8,128)S(1)} %bitcast.28, f32[3,32,128]{2,1,0:T(8,128)S(1)} %bitcast.25, f32[8,3,32,128]{3,2,1,0:T(8,128)S(1)} %bitcast.21), custom_call_target="tpu_custom_call" | custom-call | tf_op jit(solution)/shard_map/residual/pallas_call | solution.py:30
  38.2 4.3 %all-to-all-start.1 = ((f32[128,1,128]{2,1,0:T(1,128)}), f32[128,1,128]{2,1,0:T(1,128)S(1)}, u32[]{:S(2)}, u32[]{:S(2)}) async-start(f32[128,1,128]{2,1,0:T(1,128)} %bitcast.10), calls=%async_computation.1 | async-start | bytes 131072 | tf_op jit(solution)/shard_map/all_to_all | solution.py:482
  42.5 0.0 copy-start
  42.6 0.8 %factor.1 = (f32[8,128]{1,0:T(8,128)S(1)}, bf16[1024,128]{1,0:T(8,128)(2,1)S(1)}) custom-call(f32[1024,128]{1,0:T(8,128)S(1)} %bitcast.19), custom_call_target="tpu_custom_call" | custom-call | tf_op jit(solution)/shard_map/factor/pallas_call | solution.py:30
  43.4 8.5 %all-to-all-done.1 = f32[128,1,128]{2,1,0:T(1,128)S(1)} async-done(((f32[128,1,128]{2,1,0:T(1,128)}), f32[128,1,128]{2,1,0:T(1,128)S(1)}, u32[]{:S(2)}, u32[]{:S(2)}) %all-to-all-start.1) | async-done | bytes 65568 | tf_op jit(solution)/shard_map/all_to_all | solution.py:482
  51.9 0.0 copy-done.3
  51.9 1.1 %update.1 = (f32[3,32,128]{2,1,0:T(8,128)}, bf16[1024,128]{1,0:T(8,128)(2,1)}) custom-call(f32[128,128]{1,0:T(8,128)S(1)} %bitcast.27, f32[8,128]{1,0:T(8,128)S(1)} %get-tuple-element.29.inverse_ref, f32[3,32,128]{2,1,0:T(8,128)S(1)} %get-tuple-element.30.base_ref, f32[8,3,32,128]{3,2,1,0:T(8,128)S(1)} %bitcast.26, ...), custom_call_target="tpu_custom_call" | custom-call | tf_op jit(solution)/shard_map/update/pallas_call | solution.py:30
  53.0 4.8 %all-to-all-start.2 = ((bf16[128,8,128]{2,1,0:T(8,128)(2,1)}), bf16[128,8,128]{2,1,0:T(8,128)(2,1)S(1)}, u32[]{:S(2)}, u32[]{:S(2)}) async-start(bf16[128,8,128]{2,1,0:T(8,128)(2,1)} %bitcast.14), calls=%async_computation.2 | async-start | bytes 524288 | tf_op jit(solution)/shard_map/all_to_all | solution.py:482
  57.8 0.0 collective-permute-done.below_hbm
  57.8 0.0 collective-permute-done.1.above_hbm
  57.8 5.7 %fluid.1 = f32[5,1,320,128]{3,2,1,0:T(8,128)} custom-call(f32[1,320,128]{2,1,0:T(8,128)} %dens_hbm.5, f32[3,1,320,128]{3,2,1,0:T(8,128)} %vel_hbm.5, f32[1,320,128]{2,1,0:T(8,128)} %press_hbm.5, bf16[5,320,128]{2,1,0:T(8,128)(2,1)} %collective-permute-done.below_hbm, bf16[5,320,128]{2,1,0:T(8,128)(2,1)} %collective-permute-done.1.above_hbm), custom_call_target="tpu_custom_call" | custom-call | tf_op jit(solution)/shard_map/fluid/pallas_call | solution.py:30
  63.5 5.2 %all-to-all-done.2 = bf16[128,8,128]{2,1,0:T(8,128)(2,1)S(1)} async-done(((bf16[128,8,128]{2,1,0:T(8,128)(2,1)}), bf16[128,8,128]{2,1,0:T(8,128)(2,1)S(1)}, u32[]{:S(2)}, u32[]{:S(2)}) %all-to-all-start.2) | async-done | bytes 262176 | tf_op jit(solution)/shard_map/all_to_all | solution.py:482
  68.7 0.0 copy-done
  68.7 1.6 %motion.1 = f32[3,64,128]{2,1,0:T(8,128)} custom-call(bf16[1024,128]{1,0:T(8,128)(2,1)S(1)} %bitcast.22, f32[256,1]{1,0:T(8,128)S(1)} %get-tuple-element.34.slot_ref, bf16[64,128,128]{2,1,0:T(8,128)(2,1)S(1)} %copy-done), custom_call_target="tpu_custom_call" | custom-call | tf_op jit(solution)/shard_map/motion/pallas_call | solution.py:30
Async XLA Ops:
  2.2 6.1 %collective-permute-start.2 = (f32[8,384]{1,0:T(8,128)S(1)}, f32[8,384]{1,0:T(8,128)S(1)}, u32[]{:S(2)}, u32[]{:S(2)}) collective-permute-start(f32[8,384]{1,0:T(8,128)S(1)} %get-tuple-element.20.own_ref), channel_id=1, source_target_pairs={{0,1},{1,2},{2,3},{3,4},{4,5},{5,6},{6,7},{7,8},{8,9},{9,10},{10,1... | collective-permute-start | bytes 36872 | tf_op jit(solution)/shard_map/ppermute | solution.py:509
  5.3 3.1 %collective-permute-start.3 = (f32[8,384]{1,0:T(8,128)S(1)}, f32[8,384]{1,0:T(8,128)S(1)}, u32[]{:S(2)}, u32[]{:S(2)}) collective-permute-start(f32[8,384]{1,0:T(8,128)S(1)} %get-tuple-element.20.own_ref), channel_id=1, source_target_pairs={{1,0},{2,1},{3,2},{4,3},{5,4},{6,5},{7,6},{8,7},{9,8},{10,9},{11,1... | collective-permute-start | bytes 36872 | tf_op jit(solution)/shard_map/ppermute | solution.py:508
  8.4 16.7 %copy-start.2 = (f32[32,3,128]{2,0,1:T(8,128)S(1)}, f32[32,3,128]{2,0,1:T(8,128)}, u32[]{:S(2)}) copy-start(f32[32,3,128]{2,0,1:T(8,128)} %param.25) | copy-start | bytes 147460
  10.2 26.9 %copy-start.1 = (f32[8,32,3,128]{3,1,2,0:T(8,128)S(1)}, f32[8,32,3,128]{3,1,2,0:T(8,128)}, u32[]{:S(2)}) copy-start(f32[8,32,3,128]{3,1,2,0:T(8,128)} %param.26) | copy-start | bytes 1179652
  10.3 26.9 %copy-start.4 = (f32[32,3,128]{2,0,1:T(8,128)S(1)}, f32[32,3,128]{2,0,1:T(8,128)}, u32[]{:S(2)}) copy-start(f32[32,3,128]{2,0,1:T(8,128)} %param.24) | copy-start | bytes 147460
  10.3 26.9 %all-to-all-start = ((f32[128,8,128]{2,1,0:T(8,128)}), f32[128,8,128]{2,1,0:T(8,128)S(1)}, u32[]{:S(2)}, u32[]{:S(2)}) async-start(f32[128,8,128]{2,1,0:T(8,128)} %bitcast.5), calls=%async_computation | async-start | bytes 1048576 | tf_op jit(solution)/shard_map/all_to_all | solution.py:482
  23.2 28.7 %copy-start.3 = (f32[8,32,3,128]{3,1,2,0:T(8,128)S(1)}, f32[8,32,3,128]{3,1,2,0:T(8,128)}, u32[]{:S(2)}) copy-start(f32[8,32,3,128]{3,1,2,0:T(8,128)} %param.27) | copy-start | bytes 1179652
  23.2 34.6 %collective-permute-start = (bf16[5,320,128]{2,1,0:T(8,128)(2,1)}, bf16[5,320,128]{2,1,0:T(8,128)(2,1)}, u32[]{:S(2)}, u32[]{:S(2)}) collective-permute-start(bf16[5,320,128]{2,1,0:T(8,128)(2,1)} %get-tuple-element.19), channel_id=1, source_target_pairs={{0,1},{1,2},{2,3},{3,4},{4,5},{5,6},{6,7},{7,8},{8,9},{9,10},{10,1... | collective-permute-start | bytes 1228808 | tf_op jit(solution)/shard_map/ppermute | solution.py:528
  25.1 32.7 %collective-permute-start.1 = (bf16[5,320,128]{2,1,0:T(8,128)(2,1)}, bf16[5,320,128]{2,1,0:T(8,128)(2,1)}, u32[]{:S(2)}, u32[]{:S(2)}) collective-permute-start(bf16[5,320,128]{2,1,0:T(8,128)(2,1)} %get-tuple-element.19), channel_id=1, source_target_pairs={{1,0},{2,1},{3,2},{4,3},{5,4},{6,5},{7,6},{8,7},{9,8},{10,9},{11,1... | collective-permute-start | bytes 1228808 | tf_op jit(solution)/shard_map/ppermute | solution.py:529
  38.2 13.7 %all-to-all-start.1 = ((f32[128,1,128]{2,1,0:T(1,128)}), f32[128,1,128]{2,1,0:T(1,128)S(1)}, u32[]{:S(2)}, u32[]{:S(2)}) async-start(f32[128,1,128]{2,1,0:T(1,128)} %bitcast.10), calls=%async_computation.1 | async-start | bytes 131072 | tf_op jit(solution)/shard_map/all_to_all | solution.py:482
  42.5 26.2 %copy-start = (bf16[64,128,128]{2,1,0:T(8,128)(2,1)S(1)}, bf16[64,128,128]{2,1,0:T(8,128)(2,1)}, u32[]{:S(2)}) copy-start(bf16[64,128,128]{2,1,0:T(8,128)(2,1)} %rbf_ref.1) | copy-start | bytes 6291460
  53.0 15.7 %all-to-all-start.2 = ((bf16[128,8,128]{2,1,0:T(8,128)(2,1)}), bf16[128,8,128]{2,1,0:T(8,128)(2,1)S(1)}, u32[]{:S(2)}, u32[]{:S(2)}) async-start(bf16[128,8,128]{2,1,0:T(8,128)(2,1)} %bitcast.14), calls=%async_computation.2 | async-start | bytes 524288 | tf_op jit(solution)/shard_map/all_to_all | solution.py:482

commit v3 on v2

--- a/solution.py
+++ b/solution.py
@@ -216,11 +216,14 @@
     lax.fori_loop(0, depth // rows, step, tuple(rusanov(last, first, 1)))
 
 
-def wall_pressure(depth, own, second, below, above):
+def row_cell(ref):
+    return [ref[i : i + 1, :] for i in range(5)]
+
+
+def wall_start(depth, own, second):
     wide = own[0].shape[1]
     lane = iota((1, wide), 1)
     me = with_speed(own)
-    total = divergence(with_speed(below), me, with_speed(above), 0)
 
     def up(x):
         return jnp.where(lane == depth - 1, x[:, 0:1], pltpu.roll(x, wide - 1, 1))
@@ -229,20 +232,25 @@
         return jnp.where(lane == 0, x[:, depth - 1 : depth], pltpu.roll(x, 1, 1))
 
     face = rusanov(me, with_speed([up(x) for x in own]), 1)
-    total = [t + f - down(f) for t, f in zip(total, face)]
+    total = [f - down(f) for f in face]
     face = rusanov(me, with_speed(second), 2)
     total = [t + f for t, f in zip(total, face)]
     total[3] = total[3] - wall_flux(me)
-    q = [c - half_step * t for c, t in zip(me[1], total)]
+    return [c - half_step * t for c, t in zip(me[1], total)]
+
+
+def wall_pressure(start, own, below, above):
+    total = divergence(with_speed(below), with_speed(own), with_speed(above), 0)
+    q = [c - half_step * t for c, t in zip(start, total)]
     return (ratio_heat - 1.0) * (
         q[4] - 0.5 * (q[1] * q[1] + q[2] * q[2] + q[3] * q[3]) / q[0]
     )
 
 
 def routing(
-    routes_hbm, targets_hbm, diff_hbm, dens_hbm, vel_hbm, press_hbm,
-    corr_hbm, normals_hbm, rbf_hbm,
-    scatter_ref, slot_ref, tag_ref, gram_ref, bulk_ref, corr_ref, normals_ref, rbf_ref,
+    groups, routes_hbm, targets_hbm, diff_hbm, dens_hbm, vel_hbm, press_hbm,
+    corr_hbm, normals_hbm, rbf_hbm, own_ref, second_ref,
+    start_ref, scatter_ref, slot_ref, tag_ref, gram_ref, bulk_ref, corr_ref, normals_ref, rbf_ref,
     routes_ref, targets_ref, diff_ref, dens_ref, vel_ref, press_ref, semaphores, ahead,
 ):
     copies = fetch(
@@ -251,13 +259,20 @@
         semaphores,
     )
     later = fetch((corr_hbm, normals_hbm, rbf_hbm), (corr_ref, normals_ref, rbf_ref), ahead)
+    start = wall_start(dens_ref.shape[1], row_cell(own_ref), row_cell(second_ref))
+    for i in range(5):
+        start_ref[i : i + 1, :] = start[i]
+    start_ref[5:8, :] = jnp.zeros((3, start_ref.shape[1]), f32)
     copies[0].wait()
     copies[1].wait()
     count = routes_ref.shape[1]
     spread, taken = scatter_ref.shape
     peers = tag_ref.shape[0]
     ii, jj = iota((count, count), 0), iota((count, count), 1)
-    route_row = jnp.broadcast_to(routes_ref[...], (count, count)).astype(f32)
+    inner = peers // groups
+    routes = routes_ref[...]
+    routes = (routes & (inner - 1)) * groups + (routes >> (inner.bit_length() - 1))
+    route_row = jnp.broadcast_to(routes, (count, count)).astype(f32)
     target_row = jnp.broadcast_to(targets_ref[...], (count, count)).astype(f32)
     route_col = jnp.sum(jnp.where(ii == jj, route_row, 0.0), axis=1, keepdims=True)
     target_col = jnp.sum(jnp.where(ii == jj, target_row, 0.0), axis=1, keepdims=True)
@@ -333,13 +348,12 @@
 
 
 def loads(
-    depth, own_ref, second_ref, below_ref, above_ref, corr_ref, normals_ref, rbf_ref,
+    start_ref, own_ref, below_ref, above_ref, corr_ref, normals_ref, rbf_ref,
     scatter_ref, tag_ref, gram_ref, send_ref, weighted, mapped,
 ):
-    def cell(ref):
-        return [ref[i : i + 1, :] for i in range(5)]
-
-    wall = wall_pressure(depth, cell(own_ref), cell(second_ref), cell(below_ref), cell(above_ref))
+    wall = wall_pressure(
+        row_cell(start_ref), row_cell(own_ref), row_cell(below_ref), row_cell(above_ref)
+    )
     count, nodes = corr_ref.shape
     at = corr_ref[...]
     within, part = at & (nodes - 1), at >> (nodes.bit_length() - 1)
@@ -420,7 +434,10 @@
     share_ref[...] = jnp.broadcast_to(row, share_ref.shape)
 
 
-def factor(blocks, got_ref, inverse_ref, serve_ref):
+def factor(
+    blocks, got_ref, dd_hbm, inverse_ref, serve_ref, turned_ref, dd_ref, semaphores
+):
+    copies = fetch((dd_hbm,), (dd_ref,), semaphores)
     spread, lanes = serve_ref.shape
     peers = spread // 8
     row = iota((8, lanes), 0)
@@ -442,19 +459,24 @@
         pivot = work[k : k + 1, :] * lax.rsqrt(work[k : k + 1, k : k + 1])
         below = work[:, k : k + 1] * lax.rsqrt(work[k : k + 1, k : k + 1])
         work = jnp.where(row == k, pivot, jnp.where(row > k, work - below * pivot, work))
-    inverse_ref[...] = jnp.where(lane < n, pltpu.roll(work, lanes - n, 1), 0.0)
-
-
-def update(share_ref, inverse_ref, base_ref, dd_ref, serve_ref, next_ref, reply_ref):
+    inverse = jnp.where(lane < n, pltpu.roll(work, lanes - n, 1), 0.0)
+    inverse_ref[...] = inverse
+    copies[0].wait()
+    for k in range(n):
+        for c in range(3):
+            turned_ref[k, c] = sum(
+                inverse[k : k + 1, m : m + 1] * dd_ref[m, c] for m in range(k + 1)
+            )
+
+
+def update(share_ref, inverse_ref, base_ref, turned_ref, serve_ref, next_ref, reply_ref):
     projected = jnp.sum(share_ref[...], axis=0, keepdims=True)
-    inverse = inverse_ref[...]
-    middle = jnp.sum(inverse * projected, axis=1, keepdims=True)
-    mixing = -jnp.sum(inverse * middle, axis=0, keepdims=True)
+    middle = jnp.sum(inverse_ref[...] * projected, axis=1, keepdims=True)
     rows = []
     for c in range(3):
         value = base_ref[c]
-        for m in range(dd_ref.shape[0]):
-            value = value + mixing[:, m : m + 1] * dd_ref[m, c]
+        for k in range(turned_ref.shape[0]):
+            value = value - middle[k : k + 1, :] * turned_ref[k, c]
         next_ref[c] = value
         rows.append(value)
     blocks = jnp.concatenate(rows, axis=0).astype(bf16)
@@ -465,21 +487,29 @@
     ).astype(bf16)
 
 
-def motion(back_ref, slot_ref, rbf_ref, out_ref, picked, made):
-    count = rbf_ref.shape[0]
-    whole = (slot_ref.shape[0], back_ref.shape[0])
-    pick = jnp.where(iota(whole, 1).astype(f32) == slot_ref[...], 1.0, 0.0).astype(bf16)
-    picked[...] = jnp.dot(pick, back_ref[...], preferred_element_type=f32)
+def prepare(slot_ref, rbf_hbm, pick_ref, turned_ref, rbf_ref, semaphores):
+    copies = fetch((rbf_hbm,), (rbf_ref,), semaphores)
+    wanted = iota(pick_ref.shape, 1).astype(f32) == slot_ref[...]
+    pick_ref[...] = jnp.where(wanted, 1.0, 0.0).astype(bf16)
+    copies[0].wait()
+    for b in range(rbf_ref.shape[0]):
+        turned_ref[b] = rbf_ref[b].T
+
+
+def motion(back_ref, pick_ref, turned_ref, out_ref, picked, made):
+    count = turned_ref.shape[0]
+    picked[...] = jnp.dot(pick_ref[...], back_ref[...], preferred_element_type=f32)
     for k in range(count // 2):
         rows = slice(8 * k, 8 * k + 8)
-        both = jnp.concatenate([rbf_ref[2 * k], rbf_ref[2 * k + 1]], axis=0)
-        made[rows, :] = pick_half(nt_dot(picked[rows, :].astype(bf16), both))
+        both = jnp.concatenate([turned_ref[2 * k], turned_ref[2 * k + 1]], axis=1)
+        left = picked[rows, :].astype(bf16)
+        made[rows, :] = pick_half(jnp.dot(left, both, preferred_element_type=f32))
     for c in range(3):
         out_ref[c] = made[pl.ds(c, count, stride=4), :]
 
 
 def exchange(value):
-    return lax.all_to_all(value, AXES, split_axis=0, concat_axis=0, tiled=True)
+    return lax.all_to_all(value, AXES[::-1], split_axis=0, concat_axis=0, tiled=True)
 
 
 def on_device(
@@ -507,9 +537,12 @@
     )
     above = lax.ppermute(own, AXES, back)
     below = lax.ppermute(own, AXES, ring)
-    scatter, slot, tag, gram, bulk, corr_near, normals_near, rbf_near = call(
-        routing,
+    kernel = functools.partial(routing, lax.axis_size(AXES[0]))
+    kernel.__name__ = "routing"
+    start, scatter, slot, tag, gram, bulk, corr_near, normals_near, rbf_near = call(
+        kernel,
         [
+            shape((8, wide)),
             shape((8 * peers, 4 * count), bf16),
             shape((4 * count, 1)),
             shape((peers, nodes)),
@@ -520,19 +553,17 @@
             shape(rbf.shape, bf16),
         ],
         routes.reshape(1, count), targets.reshape(1, count), diff_res,
-        density, velocity, pressure, correlation, normals, rbf,
+        density, velocity, pressure, correlation, normals, rbf, own, second,
         fetched=(0, 1, 2, 3, 4, 5),
         remote=(6, 7, 8),
         scratch=[pltpu.SemaphoreType.DMA((3,))],
     )
     bulk_below = lax.ppermute(bulk, AXES, ring)
     bulk_above = lax.ppermute(bulk, AXES, back)
-    kernel = functools.partial(loads, depth)
-    kernel.__name__ = "loads"
     sent = call(
-        kernel,
+        loads,
         shape((8 * peers, nodes)),
-        own, second, below, above, corr_near, normals_near, rbf_near, scatter, tag, gram,
+        start, own, below, above, corr_near, normals_near, rbf_near, scatter, tag, gram,
         scratch=[pltpu.VMEM((4 * count, nodes), f32)] * 2,
     )
     got = exchange(sent.reshape(peers, 8, nodes)).reshape(8 * peers, nodes)
@@ -557,13 +588,20 @@
     shares = exchange(share)
     kernel = functools.partial(factor, blocks)
     kernel.__name__ = "factor"
-    inverse, serve = call(
-        kernel, [shape((columns, nodes)), shape((8 * peers, nodes), bf16)], got
+    inverse, serve, turned = call(
+        kernel,
+        [
+            shape((columns, nodes)),
+            shape((8 * peers, nodes), bf16),
+            shape((columns, 3, blocks, nodes)),
+        ],
+        got, diff_disp,
+        fetched=(1,),
     )
     disp_next, reply = call(
         update,
         [shape((3, blocks, nodes)), shape((8 * peers, nodes), bf16)],
-        shares, inverse, base, diff_disp, serve,
+        shares, inverse, base, turned, serve,
     )
     returned = exchange(reply.reshape(peers, 8, nodes)).reshape(8 * peers, nodes)
     fluid_next = call(
@@ -572,10 +610,16 @@
         density, velocity, pressure, bulk_below, bulk_above,
         fetched=(0, 1, 2, 3, 4),
     )
+    pick, rbf_turned = call(
+        prepare,
+        [shape((4 * count, 8 * peers), bf16), shape(rbf.shape, bf16)],
+        slot, rbf,
+        fetched=(1,),
+    )
     wall_motion = call(
         motion,
         shape((3, count, nodes)),
-        returned, slot, rbf,
+        returned, pick, rbf_turned,
         scratch=[pltpu.VMEM((4 * count, nodes), f32)] * 2,
     )
     return (

time: 70.7 us -> 69.9 us (0.989)
  Pallas kernels: 18.8 us -> 20.7 us
  starting transfers between devices: 27 us -> 25.5 us
  waiting for transfers between devices: 23.8 us -> 22.5 us
    all_to_all x3, waiting for transfers between devices: 23.6 us -> 21.6 us  [exchange(): lax.all_to_all(value, AXES[::-1], split_axis=0, concat_axis=0, tiled=True)]
    pallas_call x9 -> x10, Pallas kernels: 18.8 us -> 20.7 us  [call(): pl.pallas_call(kernel, out_shape=out, in_specs=[pl.BlockSpec(memory_space...]
    all_to_all x3, starting transfers between devices: 22.1 us -> 20.6 us  [exchange(): lax.all_to_all(value, AXES[::-1], split_axis=0, concat_axis=0, tiled=True)]
    ppermute x1, waiting for transfers between devices: 0.14 us -> 0.9 us  [on_device(): above = lax.ppermute(own, AXES, back)]
  transfers between devices with their start and end apart: 7 -> 7, of which waited for: 4 -> 4; matrix products, arithmetic and copies ran while one was open for 0% -> 0% of each run, Pallas kernels for 20% -> 23%
where the time goes in v3:
time: 69.9 us; the launch traced here: 69.5 us
  starting transfers between devices  25.5 us (36%)
  waiting for transfers between devices  22.5 us (32%)
  Pallas kernels  20.7 us (30%)
  between operations  0.73 us (1%)
    all_to_all x3, waiting for transfers between devices, exchange(): lax.all_to_all(value, AXES[::-1], split_axis=0, concat_axis=0, tiled=True)  21.6 us
    pallas_call x10, Pallas kernels, call(): pl.pallas_call(kernel, out_shape=out, in_specs=[pl.BlockSpec(memory_space...  20.7 us
    all_to_all x3, starting transfers between devices, exchange(): lax.all_to_all(value, AXES[::-1], split_axis=0, concat_axis=0, tiled=True)  20.6 us
    ppermute x1, starting transfers between devices, on_device(): below = lax.ppermute(own, AXES, ring)  3.1 us
    ppermute x1, starting transfers between devices, on_device(): bulk_below = lax.ppermute(bulk, AXES, ring)  1.82 us
  transfers between devices with their start and end apart: 7, of which 4 were waited for; matrix products, arithmetic and copies ran while one was open for 0% of the time, Pallas kernels for 23%

profile of v3, /device:TPU:1, one launch (start us, length us, event | category | flops | bytes accessed | tf_op | source)
XLA Modules:
  0.0 69.5 jit_solution(17455883476277337097)
XLA Ops:
  0.6 1.5 %edges.1 = (f32[8,384]{1,0:T(8,128)S(1)}, f32[8,384]{1,0:T(8,128)S(1)}) custom-call(f32[1,320,128]{2,1,0:T(8,128)} %dens_hbm.5, f32[3,1,320,128]{3,2,1,0:T(8,128)} %vel_hbm.5, f32[1,320,128]{2,1,0:T(8,128)} %press_hbm.5, f32[3,32,128]{2,1,0:T(8,128)} %bitcast.23), custom_call_target="tpu_custom_call" | custom-call | tf_op jit(solution)/shard_map/edges/pallas_call | solution.py:30
  2.2 3.1 %collective-permute-start.2 = (f32[8,384]{1,0:T(8,128)S(1)}, f32[8,384]{1,0:T(8,128)S(1)}, u32[]{:S(2)}, u32[]{:S(2)}) collective-permute-start(f32[8,384]{1,0:T(8,128)S(1)} %get-tuple-element.23.own_ref), channel_id=1, source_target_pairs={{0,1},{1,2},{2,3},{3,4},{4,5},{5,6},{6,7},{7,8},{8,9},{9,10},{10,1... | collective-permute-start | bytes 36872 | tf_op jit(solution)/shard_map/ppermute | solution.py:539
  5.3 0.0 collective-permute-start.3
  5.3 2.2 %routing.1 = (f32[8,384]{1,0:T(8,128)S(1)}, bf16[1024,256]{1,0:T(8,128)(2,1)S(1)}, f32[256,1]{1,0:T(8,128)S(1)}, f32[128,128]{1,0:T(8,128)S(1)}, f32[1,128]{1,0:...) custom-call(s32[1,64]{1,0:T(1,128)} %bitcast.31, ...), custom_call_target="tpu_custom_call" | custom-call | tf_op jit(solution)/shard_map/routing/pallas_call | solution.py:30
  7.5 0.0 collective-permute-done.2.below_ref
  7.5 0.9 %collective-permute-done.3.above_ref = f32[8,384]{1,0:T(8,128)S(1)} collective-permute-done((f32[8,384]{1,0:T(8,128)S(1)}, f32[8,384]{1,0:T(8,128)S(1)}, u32[]{:S(2)}, u32[]{:S(2)}) %collective-permute-start.3) | collective-permute-done | bytes 12320 | tf_op jit(solution)/shard_map/ppermute | solution.py:538
  8.4 0.0 copy-start.1
  8.4 1.7 %loads.1 = f32[1024,128]{1,0:T(8,128)} custom-call(f32[8,384]{1,0:T(8,128)S(1)} %get-tuple-element.26.start_ref, f32[8,384]{1,0:T(8,128)S(1)} %get-tuple-element.23.own_ref, f32[8,384]{1,0:T(8,128)S(1)} %collective-permute-done.2.below_ref, f32[8,384]{1,0:T(8,128)S(1)} %collective-permute-done.3.above_ref, s32[64,128]{1,0:T(8,128)S(1)} %get-tuple-element.27.corr_ref, ...), custom_call_target="tpu_custom_call" | custom-call | tf_op jit(solution)/shard_map/loads/pallas_call | solution.py:30
  10.1 0.0 copy-start
  10.1 0.0 copy-start.2
  10.1 13.0 %all-to-all-start = ((f32[128,8,128]{2,1,0:T(8,128)}), f32[128,8,128]{2,1,0:T(8,128)S(1)}, u32[]{:S(2)}, u32[]{:S(2)}) async-start(f32[128,8,128]{2,1,0:T(8,128)} %bitcast.5), calls=%async_computation | async-start | bytes 1048576 | tf_op jit(solution)/shard_map/all_to_all | solution.py:512
  23.1 1.8 %collective-permute-start = (bf16[5,320,128]{2,1,0:T(8,128)(2,1)S(1)}, bf16[5,320,128]{2,1,0:T(8,128)(2,1)}, u32[]{:S(2)}, u32[]{:S(2)}) collective-permute-start(bf16[5,320,128]{2,1,0:T(8,128)(2,1)S(1)} %get-tuple-element.25), channel_id=1, source_target_pairs={{0,1},{1,2},{2,3},{3,4},{4,5},{5,6},{6,7},{7,8},{8,9},{9,10},{10,1... | collective-permute-start | bytes 1228808 | tf_op jit(solution)/shard_map/ppermute | solution.py:561
  24.9 0.0 collective-permute-start.1
  24.9 0.0 copy-done.1
  24.9 2.2 %solid.1.kd_ref = f32[3,32,128]{2,1,0:T(8,128)S(1)} custom-call(s32[1]{0:T(128)} %bitcast.7.keep_ref, f32[3,32,128]{2,1,0:T(8,128)S(1)} %bitcast.24, f32[8,384]{1,0:T(8,128)S(1)} %collective-permute-done.2.below_ref, bf16[32,128,128]{2,1,0:T(8,128)(2,1)} %stiff_hbm.1, bf16[32,128,128]{2,1,0:T(8,128)(2,1)} %coup_hbm.1), custom_call_target="tpu_custom_call" | custom-call | tf_op jit(solution)/shard_map/solid/pallas_call | solution.py:30
  27.1 10.1 %all-to-all-done = f32[128,8,128]{2,1,0:T(8,128)S(1)} async-done(((f32[128,8,128]{2,1,0:T(8,128)}), f32[128,8,128]{2,1,0:T(8,128)S(1)}, u32[]{:S(2)}, u32[]{:S(2)}) %all-to-all-start) | async-done | bytes 524320 | tf_op jit(solution)/shard_map/all_to_all | solution.py:512
  37.3 0.0 copy-done
  37.3 0.0 copy-done.2
  37.3 1.0 %residual.1 = (f32[3,32,128]{2,1,0:T(8,128)S(1)}, f32[128,128]{1,0:T(8,128)}) custom-call(f32[1024,128]{1,0:T(8,128)S(1)} %bitcast.18, f32[3,32,128]{2,1,0:T(8,128)S(1)} %solid.1.kd_ref, f32[3,32,128]{2,1,0:T(8,128)S(1)} %bitcast.27, f32[3,32,128]{2,1,0:T(8,128)S(1)} %bitcast.25, f32[8,3,32,128]{3,2,1,0:T(8,128)S(1)} %bitcast.21), custom_call_target="tpu_custom_call" | custom-call | tf_op jit(solution)/shard_map/residual/pallas_call | solution.py:30
  38.3 3.5 %all-to-all-start.1 = ((f32[128,1,128]{2,1,0:T(1,128)}), f32[128,1,128]{2,1,0:T(1,128)S(1)}, u32[]{:S(2)}, u32[]{:S(2)}) async-start(f32[128,1,128]{2,1,0:T(1,128)} %bitcast.10), calls=%async_computation.1 | async-start | bytes 131072 | tf_op jit(solution)/shard_map/all_to_all | solution.py:512
  41.8 1.9 %factor.1 = (f32[8,128]{1,0:T(8,128)S(1)}, bf16[1024,128]{1,0:T(8,128)(2,1)S(1)}, f32[8,3,32,128]{3,2,1,0:T(8,128)S(1)}) custom-call(f32[1024,128]{1,0:T(8,128)S(1)} %bitcast.19, f32[8,3,32,128]{3,2,1,0:T(8,128)} %bitcast.28), custom_call_target="tpu_custom_call" | custom-call | tf_op jit(solution)/shard_map/factor/pallas_call | solution.py:30
  43.7 8.1 %all-to-all-done.1 = f32[128,1,128]{2,1,0:T(1,128)S(1)} async-done(((f32[128,1,128]{2,1,0:T(1,128)}), f32[128,1,128]{2,1,0:T(1,128)S(1)}, u32[]{:S(2)}, u32[]{:S(2)}) %all-to-all-start.1) | async-done | bytes 65568 | tf_op jit(solution)/shard_map/all_to_all | solution.py:512
  51.8 1.0 %update.1 = (f32[3,32,128]{2,1,0:T(8,128)}, bf16[1024,128]{1,0:T(8,128)(2,1)}) custom-call(f32[128,128]{1,0:T(8,128)S(1)} %bitcast.26, f32[8,128]{1,0:T(8,128)S(1)} %get-tuple-element.34.inverse_ref, f32[3,32,128]{2,1,0:T(8,128)S(1)} %get-tuple-element.35.base_ref, f32[8,3,32,128]{3,2,1,0:T(8,128)S(1)} %get-tuple-element.36.turned_ref, ...), custom_call_target="tpu_custom_call" | custom-call | tf_op jit(solution)/shard_map/update/pallas_call | solution.py:30
  52.8 4.1 %all-to-all-start.2 = ((bf16[128,8,128]{2,1,0:T(8,128)(2,1)}), bf16[128,8,128]{2,1,0:T(8,128)(2,1)S(1)}, u32[]{:S(2)}, u32[]{:S(2)}) async-start(bf16[128,8,128]{2,1,0:T(8,128)(2,1)} %bitcast.14), calls=%async_computation.2 | async-start | bytes 524288 | tf_op jit(solution)/shard_map/all_to_all | solution.py:512
  56.9 2.2 %prepare.1 = (bf16[256,1024]{1,0:T(8,128)(2,1)S(1)}, bf16[64,128,128]{2,1,0:T(8,128)(2,1)S(1)}) custom-call(f32[256,1]{1,0:T(8,128)S(1)} %get-tuple-element.40.slot_ref, bf16[64,128,128]{2,1,0:T(8,128)(2,1)} %rbf_hbm.3), custom_call_target="tpu_custom_call" | custom-call | tf_op jit(solution)/shard_map/prepare/pallas_call | solution.py:30
  59.1 0.0 collective-permute-done.below_hbm
  59.1 0.0 collective-permute-done.1.above_hbm
  59.1 5.7 %fluid.1 = f32[5,1,320,128]{3,2,1,0:T(8,128)} custom-call(f32[1,320,128]{2,1,0:T(8,128)} %dens_hbm.5, f32[3,1,320,128]{3,2,1,0:T(8,128)} %vel_hbm.5, f32[1,320,128]{2,1,0:T(8,128)} %press_hbm.5, bf16[5,320,128]{2,1,0:T(8,128)(2,1)} %collective-permute-done.below_hbm, bf16[5,320,128]{2,1,0:T(8,128)(2,1)} %collective-permute-done.1.above_hbm), custom_call_target="tpu_custom_call" | custom-call | tf_op jit(solution)/shard_map/fluid/pallas_call | solution.py:30
  64.8 3.4 %all-to-all-done.2 = bf16[128,8,128]{2,1,0:T(8,128)(2,1)S(1)} async-done(((bf16[128,8,128]{2,1,0:T(8,128)(2,1)}), bf16[128,8,128]{2,1,0:T(8,128)(2,1)S(1)}, u32[]{:S(2)}, u32[]{:S(2)}) %all-to-all-start.2) | async-done | bytes 262176 | tf_op jit(solution)/shard_map/all_to_all | solution.py:512
  68.2 1.2 %motion.1 = f32[3,64,128]{2,1,0:T(8,128)} custom-call(bf16[1024,128]{1,0:T(8,128)(2,1)S(1)} %bitcast.22, bf16[256,1024]{1,0:T(8,128)(2,1)S(1)} %get-tuple-element.41.pick_ref, bf16[64,128,128]{2,1,0:T(8,128)(2,1)S(1)} %get-tuple-element.42.turned_ref), custom_call_target="tpu_custom_call" | custom-call | tf_op jit(solution)/shard_map/motion/pallas_call | solution.py:30
Async XLA Ops:
  2.2 5.3 %collective-permute-start.2 = (f32[8,384]{1,0:T(8,128)S(1)}, f32[8,384]{1,0:T(8,128)S(1)}, u32[]{:S(2)}, u32[]{:S(2)}) collective-permute-start(f32[8,384]{1,0:T(8,128)S(1)} %get-tuple-element.23.own_ref), channel_id=1, source_target_pairs={{0,1},{1,2},{2,3},{3,4},{4,5},{5,6},{6,7},{7,8},{8,9},{9,10},{10,1... | collective-permute-start | bytes 36872 | tf_op jit(solution)/shard_map/ppermute | solution.py:539
  5.3 3.1 %collective-permute-start.3 = (f32[8,384]{1,0:T(8,128)S(1)}, f32[8,384]{1,0:T(8,128)S(1)}, u32[]{:S(2)}, u32[]{:S(2)}) collective-permute-start(f32[8,384]{1,0:T(8,128)S(1)} %get-tuple-element.23.own_ref), channel_id=1, source_target_pairs={{1,0},{2,1},{3,2},{4,3},{5,4},{6,5},{7,6},{8,7},{9,8},{10,9},{11,1... | collective-permute-start | bytes 36872 | tf_op jit(solution)/shard_map/ppermute | solution.py:538
  8.4 16.5 %copy-start.1 = (f32[32,3,128]{2,0,1:T(8,128)S(1)}, f32[32,3,128]{2,0,1:T(8,128)}, u32[]{:S(2)}) copy-start(f32[32,3,128]{2,0,1:T(8,128)} %param.25) | copy-start | bytes 147460
  10.1 27.2 %copy-start = (f32[8,32,3,128]{3,1,2,0:T(8,128)S(1)}, f32[8,32,3,128]{3,1,2,0:T(8,128)}, u32[]{:S(2)}) copy-start(f32[8,32,3,128]{3,1,2,0:T(8,128)} %param.26) | copy-start | bytes 1179652
  10.1 27.2 %copy-start.2 = (f32[32,3,128]{2,0,1:T(8,128)S(1)}, f32[32,3,128]{2,0,1:T(8,128)}, u32[]{:S(2)}) copy-start(f32[32,3,128]{2,0,1:T(8,128)} %param.24) | copy-start | bytes 147460
  10.1 27.2 %all-to-all-start = ((f32[128,8,128]{2,1,0:T(8,128)}), f32[128,8,128]{2,1,0:T(8,128)S(1)}, u32[]{:S(2)}, u32[]{:S(2)}) async-start(f32[128,8,128]{2,1,0:T(8,128)} %bitcast.5), calls=%async_computation | async-start | bytes 1048576 | tf_op jit(solution)/shard_map/all_to_all | solution.py:512
  23.1 36.0 %collective-permute-start = (bf16[5,320,128]{2,1,0:T(8,128)(2,1)S(1)}, bf16[5,320,128]{2,1,0:T(8,128)(2,1)}, u32[]{:S(2)}, u32[]{:S(2)}) collective-permute-start(bf16[5,320,128]{2,1,0:T(8,128)(2,1)S(1)} %get-tuple-element.25), channel_id=1, source_target_pairs={{0,1},{1,2},{2,3},{3,4},{4,5},{5,6},{6,7},{7,8},{8,9},{9,10},{10,1... | collective-permute-start | bytes 1228808 | tf_op jit(solution)/shard_map/ppermute | solution.py:561
  24.9 34.2 %collective-permute-start.1 = (bf16[5,320,128]{2,1,0:T(8,128)(2,1)S(1)}, bf16[5,320,128]{2,1,0:T(8,128)(2,1)}, u32[]{:S(2)}, u32[]{:S(2)}) collective-permute-start(bf16[5,320,128]{2,1,0:T(8,128)(2,1)S(1)} %get-tuple-element.25), channel_id=1, source_target_pairs={{1,0},{2,1},{3,2},{4,3},{5,4},{6,5},{7,6},{8,7},{9,8},{10,9},{11,1... | collective-permute-start | bytes 1228808 | tf_op jit(solution)/shard_map/ppermute | solution.py:562
  38.3 13.5 %all-to-all-start.1 = ((f32[128,1,128]{2,1,0:T(1,128)}), f32[128,1,128]{2,1,0:T(1,128)S(1)}, u32[]{:S(2)}, u32[]{:S(2)}) async-start(f32[128,1,128]{2,1,0:T(1,128)} %bitcast.10), calls=%async_computation.1 | async-start | bytes 131072 | tf_op jit(solution)/shard_map/all_to_all | solution.py:512
  52.8 15.4 %all-to-all-start.2 = ((bf16[128,8,128]{2,1,0:T(8,128)(2,1)}), bf16[128,8,128]{2,1,0:T(8,128)(2,1)S(1)}, u32[]{:S(2)}, u32[]{:S(2)}) async-start(bf16[128,8,128]{2,1,0:T(8,128)(2,1)} %bitcast.14), calls=%async_computation.2 | async-start | bytes 524288 | tf_op jit(solution)/shard_map/all_to_all | solution.py:512

commit v4 on v3

--- a/solution.py
+++ b/solution.py
@@ -247,10 +247,15 @@
     )
 
 
+sent_rows = 7
+reply_rows = 6
+gram_lane = 64
+
+
 def routing(
     groups, routes_hbm, targets_hbm, diff_hbm, dens_hbm, vel_hbm, press_hbm,
     corr_hbm, normals_hbm, rbf_hbm, own_ref, second_ref,
-    start_ref, scatter_ref, slot_ref, tag_ref, gram_ref, bulk_ref, corr_ref, normals_ref, rbf_ref,
+    start_ref, scatter_ref, slot_ref, meta_ref, bulk_ref, corr_ref, normals_ref, rbf_ref,
     routes_ref, targets_ref, diff_ref, dens_ref, vel_ref, press_ref, semaphores, ahead,
 ):
     copies = fetch(
@@ -267,7 +272,7 @@
     copies[1].wait()
     count = routes_ref.shape[1]
     spread, taken = scatter_ref.shape
-    peers = tag_ref.shape[0]
+    peers = meta_ref.shape[0]
     ii, jj = iota((count, count), 0), iota((count, count), 1)
     inner = peers // groups
     routes = routes_ref[...]
@@ -279,8 +284,8 @@
     same = jnp.where(route_col == route_row, 1.0, 0.0)
     place_col = jnp.sum(jnp.where(jj < ii, same, 0.0), axis=1, keepdims=True)
     place_row = jnp.sum(jnp.where(ii < jj, same, 0.0), axis=0, keepdims=True)
-    slot_col = route_col * 8.0 + place_col * 3.0
-    slot_row = route_row[0:1, :] * 8.0 + place_row * 3.0
+    slot_col = route_col * float(sent_rows) + place_col * 3.0
+    slot_row = route_row[0:1, :] * float(reply_rows) + place_row
     own = (iota((count, taken), 1) >> 2) == iota((count, taken), 0)
     comp = iota((1, taken), 1) & 3
     at_row = jnp.sum(jnp.where(own, slot_col, 0.0), axis=0, keepdims=True)
@@ -291,17 +296,15 @@
     own = (iota((taken, count), 0) >> 2) == iota((taken, count), 1)
     comp = iota((taken, 1), 0) & 3
     at_col = jnp.sum(jnp.where(own, slot_row, 0.0), axis=1, keepdims=True)
-    at_col = jnp.where(comp < 3, at_col + comp.astype(f32), -1.0)
+    at_col = jnp.where(comp < 3, at_col + 2.0 * comp.astype(f32), -1.0)
     slot_ref[...] = at_col
     to_peer = jnp.where(
         iota((peers, count), 0).astype(f32) == route_row[0:1, :], 1.0, 0.0
     )
     named = jnp.where(
-        iota((count, tag_ref.shape[1]), 1).astype(f32) == place_col, target_col + 1.0, 0.0
-    )
-    tag_ref[...] = (
-        jnp.dot(to_peer.astype(bf16), named.astype(bf16), preferred_element_type=f32) - 1.0
-    )
+        iota((count, meta_ref.shape[1]), 1).astype(f32) == place_col, target_col + 1.0, 0.0
+    )
+    tags = jnp.dot(to_peer.astype(bf16), named.astype(bf16), preferred_element_type=f32) - 1.0
     copies[2].wait()
     columns = diff_ref.shape[0]
     lanes = diff_ref.shape[3]
@@ -314,8 +317,9 @@
         [sums[min(m, n), max(m, n)] for m in range(columns) for n in range(columns)], axis=0
     )
     col = jnp.sum(stacked, axis=1, keepdims=True)
-    diag = iota((columns * columns, lanes), 0) == iota((columns * columns, lanes), 1)
-    gram_ref[...] = jnp.sum(jnp.where(diag, col, 0.0), axis=0, keepdims=True)
+    diag = iota((columns * columns, lanes), 0) == iota((columns * columns, lanes), 1) - gram_lane
+    gram = jnp.sum(jnp.where(diag, col, 0.0), axis=0, keepdims=True)
+    meta_ref[...] = jnp.where(iota(meta_ref.shape, 1) < gram_lane, tags, gram)
     for copy in copies[3:] + later:
         copy.wait()
     bulk_ref[0] = dens_ref[0].astype(bf16)
@@ -349,7 +353,7 @@
 
 def loads(
     start_ref, own_ref, below_ref, above_ref, corr_ref, normals_ref, rbf_ref,
-    scatter_ref, tag_ref, gram_ref, send_ref, weighted, mapped,
+    scatter_ref, meta_ref, send_ref, weighted, mapped,
 ):
     wall = wall_pressure(
         row_cell(start_ref), row_cell(own_ref), row_cell(below_ref), row_cell(above_ref)
@@ -372,9 +376,7 @@
             jnp.dot(left, both, preferred_element_type=f32)
         )
     send_ref[...] = exact_dot(scatter_ref[...], mapped[...])
-    peers = tag_ref.shape[0]
-    send_ref[pl.ds(6, peers, stride=8), :] = tag_ref[...]
-    send_ref[pl.ds(7, peers, stride=8), :] = jnp.broadcast_to(gram_ref[...], tag_ref.shape)
+    send_ref[pl.ds(sent_rows - 1, meta_ref.shape[0], stride=sent_rows), :] = meta_ref[...]
 
 
 def solid(
@@ -410,7 +412,7 @@
 def residual(got_ref, kd_ref, inv_ref, disp_ref, diff_ref, base_ref, share_ref):
     count, nodes = disp_ref.shape[1:]
     peers = share_ref.shape[0]
-    turned = got_ref[pl.ds(6, peers, stride=8), :].T
+    turned = got_ref[pl.ds(sent_rows - 1, peers, stride=sent_rows), :].T
     block = iota((count, peers), 0).astype(f32)
     chosen = jnp.concatenate(
         [jnp.where(block == turned[i : i + 1, :], 1.0, 0.0) for i in range(2)], axis=1
@@ -418,7 +420,7 @@
     res = []
     for c in range(3):
         rows = jnp.concatenate(
-            [got_ref[pl.ds(c + 3 * i, peers, stride=8), :] for i in range(2)], axis=0
+            [got_ref[pl.ds(c + 3 * i, peers, stride=sent_rows), :] for i in range(2)], axis=0
         )
         part = -inv_ref[c] * (kd_ref[c] - exact_dot(chosen, rows))
         base_ref[c] = disp_ref[c] + part
@@ -435,21 +437,24 @@
 
 
 def factor(
-    blocks, got_ref, dd_hbm, inverse_ref, serve_ref, turned_ref, dd_ref, semaphores
+    blocks, got_ref, dd_hbm, inverse_ref, serve_ref, turned_ref, dd_ref, semaphores, spread
 ):
     copies = fetch((dd_hbm,), (dd_ref,), semaphores)
-    spread, lanes = serve_ref.shape
-    peers = spread // 8
+    lanes = serve_ref.shape[1]
+    peers = serve_ref.shape[0] // reply_rows
+    meta = got_ref[pl.ds(sent_rows - 1, peers, stride=sent_rows), :]
+    block = iota((peers, lanes), 1).astype(f32)
+    for i in range(2):
+        tag = jnp.broadcast_to(meta[:, i : i + 1], (peers, lanes))
+        for c in range(3):
+            wanted = jnp.where(tag >= 0.0, tag + float(c * blocks), -1.0)
+            hot = jnp.where(block == wanted, 1.0, 0.0)
+            spread[pl.ds(2 * c + i, peers, stride=reply_rows), :] = hot
+    serve_ref[...] = spread[...].astype(bf16)
     row = iota((8, lanes), 0)
     lane = iota((8, lanes), 1)
-    second = row >= 3
-    kept = ((lane // blocks) == jnp.where(second, row - 3, row)) & (row < 6)
-    wanted = jnp.where(kept, lane % blocks, -2).astype(f32)
-    for d in range(peers):
-        tags = got_ref[8 * d + 6 : 8 * d + 7, :]
-        tag = jnp.where(second, tags[:, 1:2], tags[:, 0:1])
-        serve_ref[8 * d : 8 * d + 8, :] = jnp.where(tag == wanted, 1.0, 0.0).astype(bf16)
-    total = jnp.sum(got_ref[pl.ds(7, peers, stride=8), :], axis=0, keepdims=True)
+    total = jnp.sum(meta, axis=0, keepdims=True)
+    total = pltpu.roll(total, lanes - gram_lane, 1)
     n = 8
     gram = jnp.concatenate(
         [total if m == 0 else pltpu.roll(total, lanes - n * m, 1) for m in range(n)], axis=0
@@ -539,14 +544,13 @@
     below = lax.ppermute(own, AXES, ring)
     kernel = functools.partial(routing, lax.axis_size(AXES[0]))
     kernel.__name__ = "routing"
-    start, scatter, slot, tag, gram, bulk, corr_near, normals_near, rbf_near = call(
+    start, scatter, slot, meta, bulk, corr_near, normals_near, rbf_near = call(
         kernel,
         [
             shape((8, wide)),
-            shape((8 * peers, 4 * count), bf16),
+            shape((sent_rows * peers, 4 * count), bf16),
             shape((4 * count, 1)),
             shape((peers, nodes)),
-            shape((1, nodes)),
             shape((5, depth, lanes), bf16),
             shape(correlation.shape, jnp.int32),
             shape(normals.shape),
@@ -562,11 +566,11 @@
     bulk_above = lax.ppermute(bulk, AXES, back)
     sent = call(
         loads,
-        shape((8 * peers, nodes)),
-        start, own, below, above, corr_near, normals_near, rbf_near, scatter, tag, gram,
+        shape((sent_rows * peers, nodes)),
+        start, own, below, above, corr_near, normals_near, rbf_near, scatter, meta,
         scratch=[pltpu.VMEM((4 * count, nodes), f32)] * 2,
     )
-    got = exchange(sent.reshape(peers, 8, nodes)).reshape(8 * peers, nodes)
+    got = exchange(sent.reshape(peers, 1, sent_rows * nodes)).reshape(sent_rows * peers, nodes)
     keep = (lax.axis_index(AXES) > 0).astype(jnp.int32).reshape(1)
     product = call(
         solid,
@@ -592,18 +596,21 @@
         kernel,
         [
             shape((columns, nodes)),
-            shape((8 * peers, nodes), bf16),
+            shape((reply_rows * peers, nodes), bf16),
             shape((columns, 3, blocks, nodes)),
         ],
         got, diff_disp,
         fetched=(1,),
+        scratch=[pltpu.VMEM((reply_rows * peers, nodes), f32)],
     )
     disp_next, reply = call(
         update,
-        [shape((3, blocks, nodes)), shape((8 * peers, nodes), bf16)],
+        [shape((3, blocks, nodes)), shape((reply_rows * peers, nodes), bf16)],
         shares, inverse, base, turned, serve,
     )
-    returned = exchange(reply.reshape(peers, 8, nodes)).reshape(8 * peers, nodes)
+    reply = jnp.transpose(reply.reshape(peers, 3, 2, nodes), (0, 2, 1, 3))
+    returned = exchange(reply.reshape(peers, 2, 3 * nodes)).reshape(peers, 2, 3, nodes)
+    returned = jnp.transpose(returned, (0, 2, 1, 3)).reshape(reply_rows * peers, nodes)
     fluid_next = call(
         fluid,
         shape((5, 1, depth, lanes)),
@@ -612,7 +619,7 @@
     )
     pick, rbf_turned = call(
         prepare,
-        [shape((4 * count, 8 * peers), bf16), shape(rbf.shape, bf16)],
+        [shape((4 * count, reply_rows * peers), bf16), shape(rbf.shape, bf16)],
         slot, rbf,
         fetched=(1,),
     )

time: 69.9 us -> 68.4 us (0.979)
  waiting for transfers between devices: 22.5 us -> 21.7 us
  Pallas kernels: 20.7 us -> 20 us
    all_to_all x3, waiting for transfers between devices: 21.6 us -> 20.8 us  [exchange(): lax.all_to_all(value, AXES[::-1], split_axis=0, concat_axis=0, tiled=True)]
    pallas_call x10, Pallas kernels: 20.7 us -> 20 us  [call(): pl.pallas_call(kernel, out_shape=out, in_specs=[pl.BlockSpec(memory_space...]
where the time goes in v4:
time: 68.4 us; the launch traced here: 68 us
  starting transfers between devices  25.6 us (37%)
  waiting for transfers between devices  21.7 us (32%)
  Pallas kernels  20 us (29%)
  between operations  0.73 us (1%)
    all_to_all x3, waiting for transfers between devices, exchange(): lax.all_to_all(value, AXES[::-1], split_axis=0, concat_axis=0, tiled=True)  20.8 us
    all_to_all x3, starting transfers between devices, exchange(): lax.all_to_all(value, AXES[::-1], split_axis=0, concat_axis=0, tiled=True)  20.6 us
    pallas_call x10, Pallas kernels, call(): pl.pallas_call(kernel, out_shape=out, in_specs=[pl.BlockSpec(memory_space...  20 us
    ppermute x1, starting transfers between devices, on_device(): below = lax.ppermute(own, AXES, ring)  3.1 us
    ppermute x1, starting transfers between devices, on_device(): bulk_below = lax.ppermute(bulk, AXES, ring)  1.82 us
  transfers between devices with their start and end apart: 7, of which 4 were waited for; matrix products, arithmetic and copies ran while one was open for 0% of the time, Pallas kernels for 23%

profile of v4, /device:TPU:1, one launch (start us, length us, event | category | flops | bytes accessed | tf_op | source)
XLA Modules:
  0.0 68.0 jit_solution(8735417185756865152)
XLA Ops:
  0.6 1.5 %edges.1 = (f32[8,384]{1,0:T(8,128)S(1)}, f32[8,384]{1,0:T(8,128)S(1)}) custom-call(f32[1,320,128]{2,1,0:T(8,128)} %dens_hbm.5, f32[3,1,320,128]{3,2,1,0:T(8,128)} %vel_hbm.5, f32[1,320,128]{2,1,0:T(8,128)} %press_hbm.5, f32[3,32,128]{2,1,0:T(8,128)} %bitcast.31), custom_call_target="tpu_custom_call" | custom-call | tf_op jit(solution)/shard_map/edges/pallas_call | solution.py:30
  2.2 3.1 %collective-permute-start.2 = (f32[8,384]{1,0:T(8,128)S(1)}, f32[8,384]{1,0:T(8,128)S(1)}, u32[]{:S(2)}, u32[]{:S(2)}) collective-permute-start(f32[8,384]{1,0:T(8,128)S(1)} %get-tuple-element.22.own_ref), channel_id=1, source_target_pairs={{0,1},{1,2},{2,3},{3,4},{4,5},{5,6},{6,7},{7,8},{8,9},{9,10},{10,1... | collective-permute-start | bytes 36872 | tf_op jit(solution)/shard_map/ppermute | solution.py:544
  5.3 0.0 collective-permute-start.3
  5.3 2.2 %routing.1 = (f32[8,384]{1,0:T(8,128)S(1)}, bf16[896,256]{1,0:T(8,128)(2,1)S(1)}, f32[256,1]{1,0:T(8,128)S(1)}, f32[128,128]{1,0:T(8,128)S(1)}, bf16[5,320,128]{...) custom-call(s32[1,64]{1,0:T(1,128)} %bitcast.39, ...), custom_call_target="tpu_custom_call" | custom-call | tf_op jit(solution)/shard_map/routing/pallas_call | solution.py:30
  7.5 0.0 collective-permute-done.2.below_ref
  7.5 0.9 %collective-permute-done.3.above_ref = f32[8,384]{1,0:T(8,128)S(1)} collective-permute-done((f32[8,384]{1,0:T(8,128)S(1)}, f32[8,384]{1,0:T(8,128)S(1)}, u32[]{:S(2)}, u32[]{:S(2)}) %collective-permute-start.3) | collective-permute-done | bytes 12320 | tf_op jit(solution)/shard_map/ppermute | solution.py:543
  8.4 0.0 copy-start.1
  8.4 1.6 %loads.1 = f32[896,128]{1,0:T(8,128)} custom-call(f32[8,384]{1,0:T(8,128)S(1)} %get-tuple-element.25.start_ref, f32[8,384]{1,0:T(8,128)S(1)} %get-tuple-element.22.own_ref, f32[8,384]{1,0:T(8,128)S(1)} %collective-permute-done.2.below_ref, f32[8,384]{1,0:T(8,128)S(1)} %collective-permute-done.3.above_ref, s32[64,128]{1,0:T(8,128)S(1)} %get-tuple-element.26.corr_ref, ...), custom_call_target="tpu_custom_call" | custom-call | tf_op jit(solution)/shard_map/loads/pallas_call | solution.py:30
  10.0 0.0 copy-start
  10.0 0.0 copy-start.2
  10.0 13.0 %all-to-all-start = ((f32[128,1,896]{2,1,0:T(1,128)}), f32[128,1,896]{2,1,0:T(1,128)S(1)}, u32[]{:S(2)}, u32[]{:S(2)}) async-start(f32[128,1,896]{2,1,0:T(1,128)} %bitcast.5), calls=%async_computation | async-start | bytes 917504 | tf_op jit(solution)/shard_map/all_to_all | solution.py:517
  23.0 1.8 %collective-permute-start = (bf16[5,320,128]{2,1,0:T(8,128)(2,1)S(1)}, bf16[5,320,128]{2,1,0:T(8,128)(2,1)}, u32[]{:S(2)}, u32[]{:S(2)}) collective-permute-start(bf16[5,320,128]{2,1,0:T(8,128)(2,1)S(1)} %get-tuple-element.24), channel_id=1, source_target_pairs={{0,1},{1,2},{2,3},{3,4},{4,5},{5,6},{6,7},{7,8},{8,9},{9,10},{10,1... | collective-permute-start | bytes 1228808 | tf_op jit(solution)/shard_map/ppermute | solution.py:565
  24.8 0.0 collective-permute-start.1
  24.8 0.0 copy-done.1
  24.8 2.2 %solid.1.kd_ref = f32[3,32,128]{2,1,0:T(8,128)S(1)} custom-call(s32[1]{0:T(128)} %bitcast.7.keep_ref, f32[3,32,128]{2,1,0:T(8,128)S(1)} %bitcast.32, f32[8,384]{1,0:T(8,128)S(1)} %collective-permute-done.2.below_ref, bf16[32,128,128]{2,1,0:T(8,128)(2,1)} %stiff_hbm.1, bf16[32,128,128]{2,1,0:T(8,128)(2,1)} %coup_hbm.1), custom_call_target="tpu_custom_call" | custom-call | tf_op jit(solution)/shard_map/solid/pallas_call | solution.py:30
  27.1 9.4 %all-to-all-done = f32[128,1,896]{2,1,0:T(1,128)S(1)} async-done(((f32[128,1,896]{2,1,0:T(1,128)}), f32[128,1,896]{2,1,0:T(1,128)S(1)}, u32[]{:S(2)}, u32[]{:S(2)}) %all-to-all-start) | async-done | bytes 458784 | tf_op jit(solution)/shard_map/all_to_all | solution.py:517
  36.5 0.0 copy-done
  36.5 0.0 copy-done.2
  36.5 1.0 %residual.1 = (f32[3,32,128]{2,1,0:T(8,128)S(1)}, f32[128,128]{1,0:T(8,128)}) custom-call(f32[896,128]{1,0:T(8,128)S(1)} %bitcast.26, f32[3,32,128]{2,1,0:T(8,128)S(1)} %solid.1.kd_ref, f32[3,32,128]{2,1,0:T(8,128)S(1)} %bitcast.35, f32[3,32,128]{2,1,0:T(8,128)S(1)} %bitcast.33, f32[8,3,32,128]{3,2,1,0:T(8,128)S(1)} %bitcast.29), custom_call_target="tpu_custom_call" | custom-call | tf_op jit(solution)/shard_map/residual/pallas_call | solution.py:30
  37.5 3.6 %all-to-all-start.1 = ((f32[128,1,128]{2,1,0:T(1,128)}), f32[128,1,128]{2,1,0:T(1,128)S(1)}, u32[]{:S(2)}, u32[]{:S(2)}) async-start(f32[128,1,128]{2,1,0:T(1,128)} %bitcast.10), calls=%async_computation.1 | async-start | bytes 131072 | tf_op jit(solution)/shard_map/all_to_all | solution.py:517
  41.1 1.2 %factor.1 = (f32[8,128]{1,0:T(8,128)S(1)}, bf16[768,128]{1,0:T(8,128)(2,1)S(1)}, f32[8,3,32,128]{3,2,1,0:T(8,128)S(1)}) custom-call(f32[896,128]{1,0:T(8,128)S(1)} %bitcast.27, f32[8,3,32,128]{3,2,1,0:T(8,128)} %bitcast.36), custom_call_target="tpu_custom_call" | custom-call | tf_op jit(solution)/shard_map/factor/pallas_call | solution.py:30
  42.4 8.7 %all-to-all-done.1 = f32[128,1,128]{2,1,0:T(1,128)S(1)} async-done(((f32[128,1,128]{2,1,0:T(1,128)}), f32[128,1,128]{2,1,0:T(1,128)S(1)}, u32[]{:S(2)}, u32[]{:S(2)}) %all-to-all-start.1) | async-done | bytes 65568 | tf_op jit(solution)/shard_map/all_to_all | solution.py:517
  51.0 1.0 %update.1 = (f32[3,32,128]{2,1,0:T(8,128)}, bf16[768,128]{1,0:T(8,128)(2,1)}) custom-call(f32[128,128]{1,0:T(8,128)S(1)} %bitcast.34, f32[8,128]{1,0:T(8,128)S(1)} %get-tuple-element.32.inverse_ref, f32[3,32,128]{2,1,0:T(8,128)S(1)} %get-tuple-element.33.base_ref, f32[8,3,32,128]{3,2,1,0:T(8,128)S(1)} %get-tuple-element.34.turned_ref, ...), custom_call_target="tpu_custom_call" | custom-call | tf_op jit(solution)/shard_map/update/pallas_call | solution.py:30
  52.0 4.1 %all-to-all-start.2 = ((bf16[128,2,384]{2,1,0:T(2,128)(2,1)}), bf16[128,2,384]{2,1,0:T(2,128)(2,1)S(1)}, u32[]{:S(2)}, u32[]{:S(2)}) async-start(bf16[128,2,384]{2,1,0:T(2,128)(2,1)} %bitcast.16), calls=%async_computation.2 | async-start | bytes 393216 | tf_op jit(solution)/shard_map/all_to_all | solution.py:517
  56.1 2.2 %prepare.1 = (bf16[256,768]{1,0:T(8,128)(2,1)S(1)}, bf16[64,128,128]{2,1,0:T(8,128)(2,1)S(1)}) custom-call(f32[256,1]{1,0:T(8,128)S(1)} %get-tuple-element.38.slot_ref, bf16[64,128,128]{2,1,0:T(8,128)(2,1)} %rbf_hbm.3), custom_call_target="tpu_custom_call" | custom-call | tf_op jit(solution)/shard_map/prepare/pallas_call | solution.py:30
  58.3 0.0 collective-permute-done.below_hbm
  58.3 0.0 collective-permute-done.1.above_hbm
  58.3 5.7 %fluid.1 = f32[5,1,320,128]{3,2,1,0:T(8,128)} custom-call(f32[1,320,128]{2,1,0:T(8,128)} %dens_hbm.5, f32[3,1,320,128]{3,2,1,0:T(8,128)} %vel_hbm.5, f32[1,320,128]{2,1,0:T(8,128)} %press_hbm.5, bf16[5,320,128]{2,1,0:T(8,128)(2,1)} %collective-permute-done.below_hbm, bf16[5,320,128]{2,1,0:T(8,128)(2,1)} %collective-permute-done.1.above_hbm), custom_call_target="tpu_custom_call" | custom-call | tf_op jit(solution)/shard_map/fluid/pallas_call | solution.py:30
  64.0 2.7 %all-to-all-done.2 = bf16[128,2,384]{2,1,0:T(2,128)(2,1)S(1)} async-done(((bf16[128,2,384]{2,1,0:T(2,128)(2,1)}), bf16[128,2,384]{2,1,0:T(2,128)(2,1)S(1)}, u32[]{:S(2)}, u32[]{:S(2)}) %all-to-all-start.2) | async-done | bytes 196640 | tf_op jit(solution)/shard_map/all_to_all | solution.py:517
  66.7 1.3 %motion.1 = f32[3,64,128]{2,1,0:T(8,128)} custom-call(bf16[768,128]{1,0:T(8,128)(2,1)S(1)} %bitcast.30, bf16[256,768]{1,0:T(8,128)(2,1)S(1)} %get-tuple-element.39.pick_ref, bf16[64,128,128]{2,1,0:T(8,128)(2,1)S(1)} %get-tuple-element.40.turned_ref), custom_call_target="tpu_custom_call" | custom-call | tf_op jit(solution)/shard_map/motion/pallas_call | solution.py:30
Async XLA Ops:
  2.2 5.3 %collective-permute-start.2 = (f32[8,384]{1,0:T(8,128)S(1)}, f32[8,384]{1,0:T(8,128)S(1)}, u32[]{:S(2)}, u32[]{:S(2)}) collective-permute-start(f32[8,384]{1,0:T(8,128)S(1)} %get-tuple-element.22.own_ref), channel_id=1, source_target_pairs={{0,1},{1,2},{2,3},{3,4},{4,5},{5,6},{6,7},{7,8},{8,9},{9,10},{10,1... | collective-permute-start | bytes 36872 | tf_op jit(solution)/shard_map/ppermute | solution.py:544
  5.3 3.1 %collective-permute-start.3 = (f32[8,384]{1,0:T(8,128)S(1)}, f32[8,384]{1,0:T(8,128)S(1)}, u32[]{:S(2)}, u32[]{:S(2)}) collective-permute-start(f32[8,384]{1,0:T(8,128)S(1)} %get-tuple-element.22.own_ref), channel_id=1, source_target_pairs={{1,0},{2,1},{3,2},{4,3},{5,4},{6,5},{7,6},{8,7},{9,8},{10,9},{11,1... | collective-permute-start | bytes 36872 | tf_op jit(solution)/shard_map/ppermute | solution.py:543
  8.4 16.4 %copy-start.1 = (f32[32,3,128]{2,0,1:T(8,128)S(1)}, f32[32,3,128]{2,0,1:T(8,128)}, u32[]{:S(2)}) copy-start(f32[32,3,128]{2,0,1:T(8,128)} %param.25) | copy-start | bytes 147460
  10.0 26.5 %copy-start = (f32[8,32,3,128]{3,1,2,0:T(8,128)S(1)}, f32[8,32,3,128]{3,1,2,0:T(8,128)}, u32[]{:S(2)}) copy-start(f32[8,32,3,128]{3,1,2,0:T(8,128)} %param.26) | copy-start | bytes 1179652
  10.0 26.5 %copy-start.2 = (f32[32,3,128]{2,0,1:T(8,128)S(1)}, f32[32,3,128]{2,0,1:T(8,128)}, u32[]{:S(2)}) copy-start(f32[32,3,128]{2,0,1:T(8,128)} %param.24) | copy-start | bytes 147460
  10.0 26.5 %all-to-all-start = ((f32[128,1,896]{2,1,0:T(1,128)}), f32[128,1,896]{2,1,0:T(1,128)S(1)}, u32[]{:S(2)}, u32[]{:S(2)}) async-start(f32[128,1,896]{2,1,0:T(1,128)} %bitcast.5), calls=%async_computation | async-start | bytes 917504 | tf_op jit(solution)/shard_map/all_to_all | solution.py:517
  23.0 35.3 %collective-permute-start = (bf16[5,320,128]{2,1,0:T(8,128)(2,1)S(1)}, bf16[5,320,128]{2,1,0:T(8,128)(2,1)}, u32[]{:S(2)}, u32[]{:S(2)}) collective-permute-start(bf16[5,320,128]{2,1,0:T(8,128)(2,1)S(1)} %get-tuple-element.24), channel_id=1, source_target_pairs={{0,1},{1,2},{2,3},{3,4},{4,5},{5,6},{6,7},{7,8},{8,9},{9,10},{10,1... | collective-permute-start | bytes 1228808 | tf_op jit(solution)/shard_map/ppermute | solution.py:565
  24.8 33.5 %collective-permute-start.1 = (bf16[5,320,128]{2,1,0:T(8,128)(2,1)S(1)}, bf16[5,320,128]{2,1,0:T(8,128)(2,1)}, u32[]{:S(2)}, u32[]{:S(2)}) collective-permute-start(bf16[5,320,128]{2,1,0:T(8,128)(2,1)S(1)} %get-tuple-element.24), channel_id=1, source_target_pairs={{1,0},{2,1},{3,2},{4,3},{5,4},{6,5},{7,6},{8,7},{9,8},{10,9},{11,1... | collective-permute-start | bytes 1228808 | tf_op jit(solution)/shard_map/ppermute | solution.py:566
  37.5 13.5 %all-to-all-start.1 = ((f32[128,1,128]{2,1,0:T(1,128)}), f32[128,1,128]{2,1,0:T(1,128)S(1)}, u32[]{:S(2)}, u32[]{:S(2)}) async-start(f32[128,1,128]{2,1,0:T(1,128)} %bitcast.10), calls=%async_computation.1 | async-start | bytes 131072 | tf_op jit(solution)/shard_map/all_to_all | solution.py:517
  52.0 14.7 %all-to-all-start.2 = ((bf16[128,2,384]{2,1,0:T(2,128)(2,1)}), bf16[128,2,384]{2,1,0:T(2,128)(2,1)S(1)}, u32[]{:S(2)}, u32[]{:S(2)}) async-start(bf16[128,2,384]{2,1,0:T(2,128)(2,1)} %bitcast.16), calls=%async_computation.2 | async-start | bytes 393216 | tf_op jit(solution)/shard_map/all_to_all | solution.py:517

commit v5 on v4

--- a/solution.py
+++ b/solution.py
@@ -18,7 +18,7 @@
     return lax.broadcasted_iota(jnp.int32, shape, dim)
 
 
-def call(kernel, out, *args, fetched=(), remote=(), scalars=(), scratch=(), limit=48):
+def call(kernel, out, *args, fetched=(), remote=(), scalars=(), scratch=(), out_specs=None, limit=48):
     held = (*fetched, *remote)
     buffers = [pltpu.VMEM(args[i].shape, args[i].dtype) for i in fetched]
     if fetched:
@@ -27,9 +27,11 @@
         pltpu.with_memory_space_constraint(x, pltpu.HBM) if i in held else x
         for i, x in enumerate(args)
     ]
+    more = {} if out_specs is None else {"out_specs": out_specs}
     return pl.pallas_call(
         kernel,
         out_shape=out,
+        **more,
         in_specs=[
             pl.BlockSpec(
                 memory_space=pltpu.HBM
@@ -353,7 +355,7 @@
 
 def loads(
     start_ref, own_ref, below_ref, above_ref, corr_ref, normals_ref, rbf_ref,
-    scatter_ref, meta_ref, send_ref, weighted, mapped,
+    scatter_ref, meta_ref, send_hbm, weighted, mapped, made_ref, semaphores,
 ):
     wall = wall_pressure(
         row_cell(start_ref), row_cell(own_ref), row_cell(below_ref), row_cell(above_ref)
@@ -375,8 +377,22 @@
         mapped[8 * k : 8 * k + 8, :] = pick_half(
             jnp.dot(left, both, preferred_element_type=f32)
         )
-    send_ref[...] = exact_dot(scatter_ref[...], mapped[...])
-    send_ref[pl.ds(sent_rows - 1, meta_ref.shape[0], stride=sent_rows), :] = meta_ref[...]
+    peers = meta_ref.shape[0]
+    parts = jnp.concatenate(thirds(mapped[...]), axis=1)
+    share = peers // 4
+    copies = []
+    for i in range(4):
+        rows = slice(i * share * sent_rows, (i + 1) * share * sent_rows)
+        made = jnp.dot(scatter_ref[rows, :], parts, preferred_element_type=f32)
+        made_ref[rows, :] = made[:, :nodes] + made[:, nodes : 2 * nodes] + made[:, 2 * nodes :]
+        at = pl.ds((i * share + 1) * sent_rows - 1, share, stride=sent_rows)
+        made_ref[at, :] = meta_ref[i * share : (i + 1) * share, :]
+        copies.append(
+            pltpu.make_async_copy(made_ref.at[rows, :], send_hbm.at[rows, :], semaphores.at[i])
+        )
+        copies[-1].start()
+    for copy in copies:
+        copy.wait()
 
 
 def solid(
@@ -568,7 +584,13 @@
         loads,
         shape((sent_rows * peers, nodes)),
         start, own, below, above, corr_near, normals_near, rbf_near, scatter, meta,
-        scratch=[pltpu.VMEM((4 * count, nodes), f32)] * 2,
+        scratch=[
+            pltpu.VMEM((4 * count, nodes), f32),
+            pltpu.VMEM((4 * count, nodes), f32),
+            pltpu.VMEM((sent_rows * peers, nodes), f32),
+            pltpu.SemaphoreType.DMA((4,)),
+        ],
+        out_specs=pl.BlockSpec(memory_space=pltpu.HBM),
     )
     got = exchange(sent.reshape(peers, 1, sent_rows * nodes)).reshape(sent_rows * peers, nodes)
     keep = (lax.axis_index(AXES) > 0).astype(jnp.int32).reshape(1)

time: 68.4 us -> 68.3 us (level)
  no operation moved by 1% of the time
where the time goes in v5:
time: 68.3 us; the launch traced here: 67.9 us
  starting transfers between devices  25.6 us (37%)
  waiting for transfers between devices  21.7 us (32%)
  Pallas kernels  19.9 us (29%)
  between operations  0.76 us (1%)
    all_to_all x3, waiting for transfers between devices, exchange(): lax.all_to_all(value, AXES[::-1], split_axis=0, concat_axis=0, tiled=True)  20.8 us
    all_to_all x3, starting transfers between devices, exchange(): lax.all_to_all(value, AXES[::-1], split_axis=0, concat_axis=0, tiled=True)  20.6 us
    pallas_call x10, Pallas kernels, call(): pl.pallas_call(kernel, out_shape=out, **more, in_specs=[pl.BlockSpec(memo...  19.9 us
    ppermute x1, starting transfers between devices, on_device(): below = lax.ppermute(own, AXES, ring)  3.1 us
    ppermute x1, starting transfers between devices, on_device(): bulk_below = lax.ppermute(bulk, AXES, ring)  1.82 us
  transfers between devices with their start and end apart: 7, of which 4 were waited for; matrix products, arithmetic and copies ran while one was open for 0% of the time, Pallas kernels for 23%

profile of v5, /device:TPU:1, one launch (start us, length us, event | category | flops | bytes accessed | tf_op | source)
XLA Modules:
  0.0 67.9 jit_solution(16495363849605657649)
XLA Ops:
  0.6 1.5 %edges.1 = (f32[8,384]{1,0:T(8,128)S(1)}, f32[8,384]{1,0:T(8,128)S(1)}) custom-call(f32[1,320,128]{2,1,0:T(8,128)} %dens_hbm.5, f32[3,1,320,128]{3,2,1,0:T(8,128)} %vel_hbm.5, f32[1,320,128]{2,1,0:T(8,128)} %press_hbm.5, f32[3,32,128]{2,1,0:T(8,128)} %bitcast.31), custom_call_target="tpu_custom_call" | custom-call | tf_op jit(solution)/shard_map/edges/pallas_call | solution.py:31
  2.2 3.1 %collective-permute-start.2 = (f32[8,384]{1,0:T(8,128)S(1)}, f32[8,384]{1,0:T(8,128)S(1)}, u32[]{:S(2)}, u32[]{:S(2)}) collective-permute-start(f32[8,384]{1,0:T(8,128)S(1)} %get-tuple-element.22.own_ref), channel_id=1, source_target_pairs={{0,1},{1,2},{2,3},{3,4},{4,5},{5,6},{6,7},{7,8},{8,9},{9,10},{10,1... | collective-permute-start | bytes 36872 | tf_op jit(solution)/shard_map/ppermute | solution.py:560
  5.3 0.0 collective-permute-start.3
  5.3 2.2 %routing.1 = (f32[8,384]{1,0:T(8,128)S(1)}, bf16[896,256]{1,0:T(8,128)(2,1)S(1)}, f32[256,1]{1,0:T(8,128)S(1)}, f32[128,128]{1,0:T(8,128)S(1)}, bf16[5,320,128]{...) custom-call(s32[1,64]{1,0:T(1,128)} %bitcast.39, ...), custom_call_target="tpu_custom_call" | custom-call | tf_op jit(solution)/shard_map/routing/pallas_call | solution.py:31
  7.5 0.0 collective-permute-done.2.below_ref
  7.5 0.9 %collective-permute-done.3.above_ref = f32[8,384]{1,0:T(8,128)S(1)} collective-permute-done((f32[8,384]{1,0:T(8,128)S(1)}, f32[8,384]{1,0:T(8,128)S(1)}, u32[]{:S(2)}, u32[]{:S(2)}) %collective-permute-start.3) | collective-permute-done | bytes 12320 | tf_op jit(solution)/shard_map/ppermute | solution.py:559
  8.4 0.0 copy-start.1
  8.4 1.6 %loads.1 = f32[896,128]{1,0:T(8,128)} custom-call(f32[8,384]{1,0:T(8,128)S(1)} %get-tuple-element.25.start_ref, f32[8,384]{1,0:T(8,128)S(1)} %get-tuple-element.22.own_ref, f32[8,384]{1,0:T(8,128)S(1)} %collective-permute-done.2.below_ref, f32[8,384]{1,0:T(8,128)S(1)} %collective-permute-done.3.above_ref, s32[64,128]{1,0:T(8,128)S(1)} %get-tuple-element.26.corr_ref, ...), custom_call_target="tpu_custom_call" | custom-call | tf_op jit(solution)/shard_map/loads/pallas_call | solution.py:31
  10.0 0.0 copy-start
  10.0 0.0 copy-start.2
  10.0 13.0 %all-to-all-start = ((f32[128,1,896]{2,1,0:T(1,128)}), f32[128,1,896]{2,1,0:T(1,128)S(1)}, u32[]{:S(2)}, u32[]{:S(2)}) async-start(f32[128,1,896]{2,1,0:T(1,128)} %bitcast.5), calls=%async_computation | async-start | bytes 917504 | tf_op jit(solution)/shard_map/all_to_all | solution.py:533
  23.0 1.8 %collective-permute-start = (bf16[5,320,128]{2,1,0:T(8,128)(2,1)S(1)}, bf16[5,320,128]{2,1,0:T(8,128)(2,1)}, u32[]{:S(2)}, u32[]{:S(2)}) collective-permute-start(bf16[5,320,128]{2,1,0:T(8,128)(2,1)S(1)} %get-tuple-element.24), channel_id=1, source_target_pairs={{0,1},{1,2},{2,3},{3,4},{4,5},{5,6},{6,7},{7,8},{8,9},{9,10},{10,1... | collective-permute-start | bytes 1228808 | tf_op jit(solution)/shard_map/ppermute | solution.py:581
  24.8 0.0 collective-permute-start.1
  24.8 0.0 copy-done.1
  24.8 2.2 %solid.1.kd_ref = f32[3,32,128]{2,1,0:T(8,128)S(1)} custom-call(s32[1]{0:T(128)} %bitcast.7.keep_ref, f32[3,32,128]{2,1,0:T(8,128)S(1)} %bitcast.32, f32[8,384]{1,0:T(8,128)S(1)} %collective-permute-done.2.below_ref, bf16[32,128,128]{2,1,0:T(8,128)(2,1)} %stiff_hbm.1, bf16[32,128,128]{2,1,0:T(8,128)(2,1)} %coup_hbm.1), custom_call_target="tpu_custom_call" | custom-call | tf_op jit(solution)/shard_map/solid/pallas_call | solution.py:31
  27.0 9.4 %all-to-all-done = f32[128,1,896]{2,1,0:T(1,128)S(1)} async-done(((f32[128,1,896]{2,1,0:T(1,128)}), f32[128,1,896]{2,1,0:T(1,128)S(1)}, u32[]{:S(2)}, u32[]{:S(2)}) %all-to-all-start) | async-done | bytes 458784 | tf_op jit(solution)/shard_map/all_to_all | solution.py:533
  36.5 0.0 copy-done
  36.5 0.0 copy-done.2
  36.5 1.0 %residual.1 = (f32[3,32,128]{2,1,0:T(8,128)S(1)}, f32[128,128]{1,0:T(8,128)}) custom-call(f32[896,128]{1,0:T(8,128)S(1)} %bitcast.26, f32[3,32,128]{2,1,0:T(8,128)S(1)} %solid.1.kd_ref, f32[3,32,128]{2,1,0:T(8,128)S(1)} %bitcast.35, f32[3,32,128]{2,1,0:T(8,128)S(1)} %bitcast.33, f32[8,3,32,128]{3,2,1,0:T(8,128)S(1)} %bitcast.29), custom_call_target="tpu_custom_call" | custom-call | tf_op jit(solution)/shard_map/residual/pallas_call | solution.py:31
  37.5 3.6 %all-to-all-start.1 = ((f32[128,1,128]{2,1,0:T(1,128)}), f32[128,1,128]{2,1,0:T(1,128)S(1)}, u32[]{:S(2)}, u32[]{:S(2)}) async-start(f32[128,1,128]{2,1,0:T(1,128)} %bitcast.10), calls=%async_computation.1 | async-start | bytes 131072 | tf_op jit(solution)/shard_map/all_to_all | solution.py:533
  41.1 1.2 %factor.1 = (f32[8,128]{1,0:T(8,128)S(1)}, bf16[768,128]{1,0:T(8,128)(2,1)S(1)}, f32[8,3,32,128]{3,2,1,0:T(8,128)S(1)}) custom-call(f32[896,128]{1,0:T(8,128)S(1)} %bitcast.27, f32[8,3,32,128]{3,2,1,0:T(8,128)} %bitcast.36), custom_call_target="tpu_custom_call" | custom-call | tf_op jit(solution)/shard_map/factor/pallas_call | solution.py:31
  42.3 8.7 %all-to-all-done.1 = f32[128,1,128]{2,1,0:T(1,128)S(1)} async-done(((f32[128,1,128]{2,1,0:T(1,128)}), f32[128,1,128]{2,1,0:T(1,128)S(1)}, u32[]{:S(2)}, u32[]{:S(2)}) %all-to-all-start.1) | async-done | bytes 65568 | tf_op jit(solution)/shard_map/all_to_all | solution.py:533
  51.0 1.0 %update.1 = (f32[3,32,128]{2,1,0:T(8,128)}, bf16[768,128]{1,0:T(8,128)(2,1)}) custom-call(f32[128,128]{1,0:T(8,128)S(1)} %bitcast.34, f32[8,128]{1,0:T(8,128)S(1)} %get-tuple-element.32.inverse_ref, f32[3,32,128]{2,1,0:T(8,128)S(1)} %get-tuple-element.33.base_ref, f32[8,3,32,128]{3,2,1,0:T(8,128)S(1)} %get-tuple-element.34.turned_ref, ...), custom_call_target="tpu_custom_call" | custom-call | tf_op jit(solution)/shard_map/update/pallas_call | solution.py:31
  52.0 4.1 %all-to-all-start.2 = ((bf16[128,2,384]{2,1,0:T(2,128)(2,1)}), bf16[128,2,384]{2,1,0:T(2,128)(2,1)S(1)}, u32[]{:S(2)}, u32[]{:S(2)}) async-start(bf16[128,2,384]{2,1,0:T(2,128)(2,1)} %bitcast.16), calls=%async_computation.2 | async-start | bytes 393216 | tf_op jit(solution)/shard_map/all_to_all | solution.py:533
  56.0 2.2 %prepare.1 = (bf16[256,768]{1,0:T(8,128)(2,1)S(1)}, bf16[64,128,128]{2,1,0:T(8,128)(2,1)S(1)}) custom-call(f32[256,1]{1,0:T(8,128)S(1)} %get-tuple-element.38.slot_ref, bf16[64,128,128]{2,1,0:T(8,128)(2,1)} %rbf_hbm.3), custom_call_target="tpu_custom_call" | custom-call | tf_op jit(solution)/shard_map/prepare/pallas_call | solution.py:31
  58.2 0.0 collective-permute-done.below_hbm
  58.3 0.0 collective-permute-done.1.above_hbm
  58.3 5.7 %fluid.1 = f32[5,1,320,128]{3,2,1,0:T(8,128)} custom-call(f32[1,320,128]{2,1,0:T(8,128)} %dens_hbm.5, f32[3,1,320,128]{3,2,1,0:T(8,128)} %vel_hbm.5, f32[1,320,128]{2,1,0:T(8,128)} %press_hbm.5, bf16[5,320,128]{2,1,0:T(8,128)(2,1)} %collective-permute-done.below_hbm, bf16[5,320,128]{2,1,0:T(8,128)(2,1)} %collective-permute-done.1.above_hbm), custom_call_target="tpu_custom_call" | custom-call | tf_op jit(solution)/shard_map/fluid/pallas_call | solution.py:31
  64.0 2.7 %all-to-all-done.2 = bf16[128,2,384]{2,1,0:T(2,128)(2,1)S(1)} async-done(((bf16[128,2,384]{2,1,0:T(2,128)(2,1)}), bf16[128,2,384]{2,1,0:T(2,128)(2,1)S(1)}, u32[]{:S(2)}, u32[]{:S(2)}) %all-to-all-start.2) | async-done | bytes 196640 | tf_op jit(solution)/shard_map/all_to_all | solution.py:533
  66.7 1.3 %motion.1 = f32[3,64,128]{2,1,0:T(8,128)} custom-call(bf16[768,128]{1,0:T(8,128)(2,1)S(1)} %bitcast.30, bf16[256,768]{1,0:T(8,128)(2,1)S(1)} %get-tuple-element.39.pick_ref, bf16[64,128,128]{2,1,0:T(8,128)(2,1)S(1)} %get-tuple-element.40.turned_ref), custom_call_target="tpu_custom_call" | custom-call | tf_op jit(solution)/shard_map/motion/pallas_call | solution.py:31
Async XLA Ops:
  2.2 5.3 %collective-permute-start.2 = (f32[8,384]{1,0:T(8,128)S(1)}, f32[8,384]{1,0:T(8,128)S(1)}, u32[]{:S(2)}, u32[]{:S(2)}) collective-permute-start(f32[8,384]{1,0:T(8,128)S(1)} %get-tuple-element.22.own_ref), channel_id=1, source_target_pairs={{0,1},{1,2},{2,3},{3,4},{4,5},{5,6},{6,7},{7,8},{8,9},{9,10},{10,1... | collective-permute-start | bytes 36872 | tf_op jit(solution)/shard_map/ppermute | solution.py:560
  5.3 3.1 %collective-permute-start.3 = (f32[8,384]{1,0:T(8,128)S(1)}, f32[8,384]{1,0:T(8,128)S(1)}, u32[]{:S(2)}, u32[]{:S(2)}) collective-permute-start(f32[8,384]{1,0:T(8,128)S(1)} %get-tuple-element.22.own_ref), channel_id=1, source_target_pairs={{1,0},{2,1},{3,2},{4,3},{5,4},{6,5},{7,6},{8,7},{9,8},{10,9},{11,1... | collective-permute-start | bytes 36872 | tf_op jit(solution)/shard_map/ppermute | solution.py:559
  8.4 16.4 %copy-start.1 = (f32[32,3,128]{2,0,1:T(8,128)S(1)}, f32[32,3,128]{2,0,1:T(8,128)}, u32[]{:S(2)}) copy-start(f32[32,3,128]{2,0,1:T(8,128)} %param.25) | copy-start | bytes 147460
  10.0 26.5 %copy-start = (f32[8,32,3,128]{3,1,2,0:T(8,128)S(1)}, f32[8,32,3,128]{3,1,2,0:T(8,128)}, u32[]{:S(2)}) copy-start(f32[8,32,3,128]{3,1,2,0:T(8,128)} %param.26) | copy-start | bytes 1179652
  10.0 26.5 %copy-start.2 = (f32[32,3,128]{2,0,1:T(8,128)S(1)}, f32[32,3,128]{2,0,1:T(8,128)}, u32[]{:S(2)}) copy-start(f32[32,3,128]{2,0,1:T(8,128)} %param.24) | copy-start | bytes 147460
  10.0 26.5 %all-to-all-start = ((f32[128,1,896]{2,1,0:T(1,128)}), f32[128,1,896]{2,1,0:T(1,128)S(1)}, u32[]{:S(2)}, u32[]{:S(2)}) async-start(f32[128,1,896]{2,1,0:T(1,128)} %bitcast.5), calls=%async_computation | async-start | bytes 917504 | tf_op jit(solution)/shard_map/all_to_all | solution.py:533
  23.0 35.3 %collective-permute-start = (bf16[5,320,128]{2,1,0:T(8,128)(2,1)S(1)}, bf16[5,320,128]{2,1,0:T(8,128)(2,1)}, u32[]{:S(2)}, u32[]{:S(2)}) collective-permute-start(bf16[5,320,128]{2,1,0:T(8,128)(2,1)S(1)} %get-tuple-element.24), channel_id=1, source_target_pairs={{0,1},{1,2},{2,3},{3,4},{4,5},{5,6},{6,7},{7,8},{8,9},{9,10},{10,1... | collective-permute-start | bytes 1228808 | tf_op jit(solution)/shard_map/ppermute | solution.py:581
  24.8 33.5 %collective-permute-start.1 = (bf16[5,320,128]{2,1,0:T(8,128)(2,1)S(1)}, bf16[5,320,128]{2,1,0:T(8,128)(2,1)}, u32[]{:S(2)}, u32[]{:S(2)}) collective-permute-start(bf16[5,320,128]{2,1,0:T(8,128)(2,1)S(1)} %get-tuple-element.24), channel_id=1, source_target_pairs={{1,0},{2,1},{3,2},{4,3},{5,4},{6,5},{7,6},{8,7},{9,8},{10,9},{11,1... | collective-permute-start | bytes 1228808 | tf_op jit(solution)/shard_map/ppermute | solution.py:582
  37.5 13.5 %all-to-all-start.1 = ((f32[128,1,128]{2,1,0:T(1,128)}), f32[128,1,128]{2,1,0:T(1,128)S(1)}, u32[]{:S(2)}, u32[]{:S(2)}) async-start(f32[128,1,128]{2,1,0:T(1,128)} %bitcast.10), calls=%async_computation.1 | async-start | bytes 131072 | tf_op jit(solution)/shard_map/all_to_all | solution.py:533
  52.0 14.7 %all-to-all-start.2 = ((bf16[128,2,384]{2,1,0:T(2,128)(2,1)}), bf16[128,2,384]{2,1,0:T(2,128)(2,1)S(1)}, u32[]{:S(2)}, u32[]{:S(2)}) async-start(bf16[128,2,384]{2,1,0:T(2,128)(2,1)} %bitcast.16), calls=%async_computation.2 | async-start | bytes 393216 | tf_op jit(solution)/shard_map/all_to_all | solution.py:533

commit v6 on v4

--- a/solution.py
+++ b/solution.py
@@ -353,7 +353,7 @@
 
 def loads(
     start_ref, own_ref, below_ref, above_ref, corr_ref, normals_ref, rbf_ref,
-    scatter_ref, meta_ref, send_ref, weighted, mapped,
+    scatter_ref, meta_ref, product_ref, send_ref, weighted, mapped,
 ):
     wall = wall_pressure(
         row_cell(start_ref), row_cell(own_ref), row_cell(below_ref), row_cell(above_ref)
@@ -564,13 +564,6 @@
     )
     bulk_below = lax.ppermute(bulk, AXES, ring)
     bulk_above = lax.ppermute(bulk, AXES, back)
-    sent = call(
-        loads,
-        shape((sent_rows * peers, nodes)),
-        start, own, below, above, corr_near, normals_near, rbf_near, scatter, meta,
-        scratch=[pltpu.VMEM((4 * count, nodes), f32)] * 2,
-    )
-    got = exchange(sent.reshape(peers, 1, sent_rows * nodes)).reshape(sent_rows * peers, nodes)
     keep = (lax.axis_index(AXES) > 0).astype(jnp.int32).reshape(1)
     product = call(
         solid,
@@ -584,6 +577,13 @@
             pltpu.VMEM((4 * blocks, nodes), f32),
         ],
     )
+    sent = call(
+        loads,
+        shape((sent_rows * peers, nodes)),
+        start, own, below, above, corr_near, normals_near, rbf_near, scatter, meta, product,
+        scratch=[pltpu.VMEM((4 * count, nodes), f32)] * 2,
+    )
+    got = exchange(sent.reshape(peers, 1, sent_rows * nodes)).reshape(sent_rows * peers, nodes)
     base, share = call(
         residual,
         [shape((3, blocks, nodes)), shape((peers, nodes))],

time: 68.4 us -> 68.4 us (level)
  starting transfers between devices: 25.6 us -> 24.3 us
  waiting for transfers between devices: 21.7 us -> 22.9 us
    all_to_all x3, waiting for transfers between devices: 20.8 us -> 22.9 us  [exchange(): lax.all_to_all(value, AXES[::-1], split_axis=0, concat_axis=0, tiled=True)]
    all_to_all x3, starting transfers between devices: 20.6 us -> 19.3 us  [exchange(): lax.all_to_all(value, AXES[::-1], split_axis=0, concat_axis=0, tiled=True)]
    ppermute x1, starting transfers between devices: 0.01 us -> 1.14 us  [on_device(): bulk_above = lax.ppermute(bulk, AXES, back)]
    ppermute x1, starting transfers between devices: 1.82 us -> 0.77 us  [on_device(): bulk_below = lax.ppermute(bulk, AXES, ring)]
    ppermute x1, waiting for transfers between devices: 0.9 us -> 0.01 us  [on_device(): above = lax.ppermute(own, AXES, back)]
  transfers between devices with their start and end apart: 7 -> 7, of which waited for: 4 -> 3; matrix products, arithmetic and copies ran while one was open for 0% -> 0% of each run, Pallas kernels for 23% -> 23%
where the time goes in v6:
time: 68.4 us; the launch traced here: 68 us
  starting transfers between devices  24.3 us (36%)
  waiting for transfers between devices  22.9 us (33%)
  Pallas kernels  20 us (29%)
  between operations  0.77 us (1%)
    all_to_all x3, waiting for transfers between devices, exchange(): lax.all_to_all(value, AXES[::-1], split_axis=0, concat_axis=0, tiled=True)  22.9 us
    pallas_call x10, Pallas kernels, call(): pl.pallas_call(kernel, out_shape=out, in_specs=[pl.BlockSpec(memory_space...  20 us
    all_to_all x3, starting transfers between devices, exchange(): lax.all_to_all(value, AXES[::-1], split_axis=0, concat_axis=0, tiled=True)  19.3 us
    ppermute x1, starting transfers between devices, on_device(): below = lax.ppermute(own, AXES, ring)  3.1 us
  transfers between devices with their start and end apart: 7, of which 3 were waited for; matrix products, arithmetic and copies ran while one was open for 0% of the time, Pallas kernels for 23%

profile of v6, /device:TPU:1, one launch (start us, length us, event | category | flops | bytes accessed | tf_op | source)
XLA Modules:
  0.0 68.0 jit_solution(16382768640301510334)
XLA Ops:
  0.6 0.0 copy-start.1
  0.6 1.5 %edges.1 = (f32[8,384]{1,0:T(8,128)S(1)}, f32[8,384]{1,0:T(8,128)S(1)}) custom-call(f32[1,320,128]{2,1,0:T(8,128)} %dens_hbm.5, f32[3,1,320,128]{3,2,1,0:T(8,128)} %vel_hbm.5, f32[1,320,128]{2,1,0:T(8,128)} %press_hbm.5, f32[3,32,128]{2,1,0:T(8,128)} %bitcast.31), custom_call_target="tpu_custom_call" | custom-call | tf_op jit(solution)/shard_map/edges/pallas_call | solution.py:30
  2.2 3.1 %collective-permute-start.2 = (f32[8,384]{1,0:T(8,128)S(1)}, f32[8,384]{1,0:T(8,128)S(1)}, u32[]{:S(2)}, u32[]{:S(2)}) collective-permute-start(f32[8,384]{1,0:T(8,128)S(1)} %get-tuple-element.22.own_ref), channel_id=1, source_target_pairs={{0,1},{1,2},{2,3},{3,4},{4,5},{5,6},{6,7},{7,8},{8,9},{9,10},{10,1... | collective-permute-start | bytes 36872 | tf_op jit(solution)/shard_map/ppermute | solution.py:544
  5.3 0.0 collective-permute-start.3
  5.3 2.2 %routing.1 = (f32[8,384]{1,0:T(8,128)S(1)}, bf16[896,256]{1,0:T(8,128)(2,1)S(1)}, f32[256,1]{1,0:T(8,128)S(1)}, f32[128,128]{1,0:T(8,128)S(1)}, bf16[5,320,128]{...) custom-call(s32[1,64]{1,0:T(1,128)} %bitcast.39, ...), custom_call_target="tpu_custom_call" | custom-call | tf_op jit(solution)/shard_map/routing/pallas_call | solution.py:30
  7.5 0.0 collective-permute-done.2.below_ref
  7.5 0.0 copy-done.1
  7.5 2.2 %solid.1.product_ref.kd_ref = f32[3,32,128]{2,1,0:T(8,128)S(1)} custom-call(s32[1]{0:T(128)} %bitcast.5.keep_ref, f32[3,32,128]{2,1,0:T(8,128)S(1)} %bitcast.32, f32[8,384]{1,0:T(8,128)S(1)} %collective-permute-done.2.below_ref, bf16[32,128,128]{2,1,0:T(8,128)(2,1)} %stiff_hbm.1, bf16[32,128,128]{2,1,0:T(8,128)(2,1)} %coup_hbm.1), custom_call_target="tpu_custom_call" | custom-call | tf_op jit(solution)/shard_map/solid/pallas_call | solution.py:30
  9.8 0.0 collective-permute-done.3.above_ref
  9.8 0.0 copy-start
  9.8 0.0 copy-start.2
  9.8 1.6 %loads.1 = f32[896,128]{1,0:T(8,128)} custom-call(f32[8,384]{1,0:T(8,128)S(1)} %get-tuple-element.25.start_ref, f32[8,384]{1,0:T(8,128)S(1)} %get-tuple-element.22.own_ref, f32[8,384]{1,0:T(8,128)S(1)} %collective-permute-done.2.below_ref, f32[8,384]{1,0:T(8,128)S(1)} %collective-permute-done.3.above_ref, s32[64,128]{1,0:T(8,128)S(1)} %get-tuple-element.26.corr_ref, ...), custom_call_target="tpu_custom_call" | custom-call | tf_op jit(solution)/shard_map/loads/pallas_call | solution.py:30
  11.4 11.6 %all-to-all-start = ((f32[128,1,896]{2,1,0:T(1,128)}), f32[128,1,896]{2,1,0:T(1,128)S(1)}, u32[]{:S(2)}, u32[]{:S(2)}) async-start(f32[128,1,896]{2,1,0:T(1,128)} %bitcast.6), calls=%async_computation | async-start | bytes 917504 | tf_op jit(solution)/shard_map/all_to_all | solution.py:517
  23.0 1.1 %collective-permute-start.1 = (bf16[5,320,128]{2,1,0:T(8,128)(2,1)S(1)}, bf16[5,320,128]{2,1,0:T(8,128)(2,1)}, u32[]{:S(2)}, u32[]{:S(2)}) collective-permute-start(bf16[5,320,128]{2,1,0:T(8,128)(2,1)S(1)} %get-tuple-element.24), channel_id=1, source_target_pairs={{1,0},{2,1},{3,2},{4,3},{5,4},{6,5},{7,6},{8,7},{9,8},{10,9},{11,1... | collective-permute-start | bytes 1228808 | tf_op jit(solution)/shard_map/ppermute | solution.py:566
  24.2 0.8 %collective-permute-start = (bf16[5,320,128]{2,1,0:T(8,128)(2,1)S(1)}, bf16[5,320,128]{2,1,0:T(8,128)(2,1)}, u32[]{:S(2)}, u32[]{:S(2)}) collective-permute-start(bf16[5,320,128]{2,1,0:T(8,128)(2,1)S(1)} %get-tuple-element.24), channel_id=1, source_target_pairs={{0,1},{1,2},{2,3},{3,4},{4,5},{5,6},{6,7},{7,8},{8,9},{9,10},{10,1... | collective-permute-start | bytes 1228808 | tf_op jit(solution)/shard_map/ppermute | solution.py:565
  24.9 11.5 %all-to-all-done = f32[128,1,896]{2,1,0:T(1,128)S(1)} async-done(((f32[128,1,896]{2,1,0:T(1,128)}), f32[128,1,896]{2,1,0:T(1,128)S(1)}, u32[]{:S(2)}, u32[]{:S(2)}) %all-to-all-start) | async-done | bytes 458784 | tf_op jit(solution)/shard_map/all_to_all | solution.py:517
  36.5 0.0 copy-done
  36.5 0.0 copy-done.2
  36.5 1.0 %residual.1 = (f32[3,32,128]{2,1,0:T(8,128)S(1)}, f32[128,128]{1,0:T(8,128)}) custom-call(f32[896,128]{1,0:T(8,128)S(1)} %bitcast.26, f32[3,32,128]{2,1,0:T(8,128)S(1)} %solid.1.product_ref.kd_ref, f32[3,32,128]{2,1,0:T(8,128)S(1)} %bitcast.35, f32[3,32,128]{2,1,0:T(8,128)S(1)} %bitcast.33, f32[8,3,32,128]{3,2,1,0:T(8,128)S(1)} %bitcast.29), custom_call_target="tpu_custom_call" | custom-call | tf_op jit(solution)/shard_map/residual/pallas_call | solution.py:30
  37.5 3.7 %all-to-all-start.1 = ((f32[128,1,128]{2,1,0:T(1,128)}), f32[128,1,128]{2,1,0:T(1,128)S(1)}, u32[]{:S(2)}, u32[]{:S(2)}) async-start(f32[128,1,128]{2,1,0:T(1,128)} %bitcast.10), calls=%async_computation.1 | async-start | bytes 131072 | tf_op jit(solution)/shard_map/all_to_all | solution.py:517
  41.1 1.2 %factor.1 = (f32[8,128]{1,0:T(8,128)S(1)}, bf16[768,128]{1,0:T(8,128)(2,1)S(1)}, f32[8,3,32,128]{3,2,1,0:T(8,128)S(1)}) custom-call(f32[896,128]{1,0:T(8,128)S(1)} %bitcast.27, f32[8,3,32,128]{3,2,1,0:T(8,128)} %bitcast.36), custom_call_target="tpu_custom_call" | custom-call | tf_op jit(solution)/shard_map/factor/pallas_call | solution.py:30
  42.4 8.7 %all-to-all-done.1 = f32[128,1,128]{2,1,0:T(1,128)S(1)} async-done(((f32[128,1,128]{2,1,0:T(1,128)}), f32[128,1,128]{2,1,0:T(1,128)S(1)}, u32[]{:S(2)}, u32[]{:S(2)}) %all-to-all-start.1) | async-done | bytes 65568 | tf_op jit(solution)/shard_map/all_to_all | solution.py:517
  51.0 1.0 %update.1 = (f32[3,32,128]{2,1,0:T(8,128)}, bf16[768,128]{1,0:T(8,128)(2,1)}) custom-call(f32[128,128]{1,0:T(8,128)S(1)} %bitcast.34, f32[8,128]{1,0:T(8,128)S(1)} %get-tuple-element.32.inverse_ref, f32[3,32,128]{2,1,0:T(8,128)S(1)} %get-tuple-element.33.base_ref, f32[8,3,32,128]{3,2,1,0:T(8,128)S(1)} %get-tuple-element.34.turned_ref, ...), custom_call_target="tpu_custom_call" | custom-call | tf_op jit(solution)/shard_map/update/pallas_call | solution.py:30
  52.0 4.1 %all-to-all-start.2 = ((bf16[128,2,384]{2,1,0:T(2,128)(2,1)}), bf16[128,2,384]{2,1,0:T(2,128)(2,1)S(1)}, u32[]{:S(2)}, u32[]{:S(2)}) async-start(bf16[128,2,384]{2,1,0:T(2,128)(2,1)} %bitcast.16), calls=%async_computation.2 | async-start | bytes 393216 | tf_op jit(solution)/shard_map/all_to_all | solution.py:517
  56.1 2.2 %prepare.1 = (bf16[256,768]{1,0:T(8,128)(2,1)S(1)}, bf16[64,128,128]{2,1,0:T(8,128)(2,1)S(1)}) custom-call(f32[256,1]{1,0:T(8,128)S(1)} %get-tuple-element.38.slot_ref, bf16[64,128,128]{2,1,0:T(8,128)(2,1)} %rbf_hbm.3), custom_call_target="tpu_custom_call" | custom-call | tf_op jit(solution)/shard_map/prepare/pallas_call | solution.py:30
  58.3 0.0 collective-permute-done.1.above_hbm
  58.3 0.0 collective-permute-done.below_hbm
  58.3 5.7 %fluid.1 = f32[5,1,320,128]{3,2,1,0:T(8,128)} custom-call(f32[1,320,128]{2,1,0:T(8,128)} %dens_hbm.5, f32[3,1,320,128]{3,2,1,0:T(8,128)} %vel_hbm.5, f32[1,320,128]{2,1,0:T(8,128)} %press_hbm.5, bf16[5,320,128]{2,1,0:T(8,128)(2,1)} %collective-permute-done.below_hbm, bf16[5,320,128]{2,1,0:T(8,128)(2,1)} %collective-permute-done.1.above_hbm), custom_call_target="tpu_custom_call" | custom-call | tf_op jit(solution)/shard_map/fluid/pallas_call | solution.py:30
  64.0 2.7 %all-to-all-done.2 = bf16[128,2,384]{2,1,0:T(2,128)(2,1)S(1)} async-done(((bf16[128,2,384]{2,1,0:T(2,128)(2,1)}), bf16[128,2,384]{2,1,0:T(2,128)(2,1)S(1)}, u32[]{:S(2)}, u32[]{:S(2)}) %all-to-all-start.2) | async-done | bytes 196640 | tf_op jit(solution)/shard_map/all_to_all | solution.py:517
  66.7 1.3 %motion.1 = f32[3,64,128]{2,1,0:T(8,128)} custom-call(bf16[768,128]{1,0:T(8,128)(2,1)S(1)} %bitcast.30, bf16[256,768]{1,0:T(8,128)(2,1)S(1)} %get-tuple-element.39.pick_ref, bf16[64,128,128]{2,1,0:T(8,128)(2,1)S(1)} %get-tuple-element.40.turned_ref), custom_call_target="tpu_custom_call" | custom-call | tf_op jit(solution)/shard_map/motion/pallas_call | solution.py:30
Async XLA Ops:
  0.6 6.9 %copy-start.1 = (f32[32,3,128]{2,0,1:T(8,128)S(1)}, f32[32,3,128]{2,0,1:T(8,128)}, u32[]{:S(2)}) copy-start(f32[32,3,128]{2,0,1:T(8,128)} %param.25) | copy-start | bytes 147460
  2.2 5.3 %collective-permute-start.2 = (f32[8,384]{1,0:T(8,128)S(1)}, f32[8,384]{1,0:T(8,128)S(1)}, u32[]{:S(2)}, u32[]{:S(2)}) collective-permute-start(f32[8,384]{1,0:T(8,128)S(1)} %get-tuple-element.22.own_ref), channel_id=1, source_target_pairs={{0,1},{1,2},{2,3},{3,4},{4,5},{5,6},{6,7},{7,8},{8,9},{9,10},{10,1... | collective-permute-start | bytes 36872 | tf_op jit(solution)/shard_map/ppermute | solution.py:544
  5.3 4.5 %collective-permute-start.3 = (f32[8,384]{1,0:T(8,128)S(1)}, f32[8,384]{1,0:T(8,128)S(1)}, u32[]{:S(2)}, u32[]{:S(2)}) collective-permute-start(f32[8,384]{1,0:T(8,128)S(1)} %get-tuple-element.22.own_ref), channel_id=1, source_target_pairs={{1,0},{2,1},{3,2},{4,3},{5,4},{6,5},{7,6},{8,7},{9,8},{10,9},{11,1... | collective-permute-start | bytes 36872 | tf_op jit(solution)/shard_map/ppermute | solution.py:543
  9.8 26.7 %copy-start = (f32[8,32,3,128]{3,1,2,0:T(8,128)S(1)}, f32[8,32,3,128]{3,1,2,0:T(8,128)}, u32[]{:S(2)}) copy-start(f32[8,32,3,128]{3,1,2,0:T(8,128)} %param.26) | copy-start | bytes 1179652
  9.8 26.7 %copy-start.2 = (f32[32,3,128]{2,0,1:T(8,128)S(1)}, f32[32,3,128]{2,0,1:T(8,128)}, u32[]{:S(2)}) copy-start(f32[32,3,128]{2,0,1:T(8,128)} %param.24) | copy-start | bytes 147460
  11.4 25.0 %all-to-all-start = ((f32[128,1,896]{2,1,0:T(1,128)}), f32[128,1,896]{2,1,0:T(1,128)S(1)}, u32[]{:S(2)}, u32[]{:S(2)}) async-start(f32[128,1,896]{2,1,0:T(1,128)} %bitcast.6), calls=%async_computation | async-start | bytes 917504 | tf_op jit(solution)/shard_map/all_to_all | solution.py:517
  23.0 35.3 %collective-permute-start.1 = (bf16[5,320,128]{2,1,0:T(8,128)(2,1)S(1)}, bf16[5,320,128]{2,1,0:T(8,128)(2,1)}, u32[]{:S(2)}, u32[]{:S(2)}) collective-permute-start(bf16[5,320,128]{2,1,0:T(8,128)(2,1)S(1)} %get-tuple-element.24), channel_id=1, source_target_pairs={{1,0},{2,1},{3,2},{4,3},{5,4},{6,5},{7,6},{8,7},{9,8},{10,9},{11,1... | collective-permute-start | bytes 1228808 | tf_op jit(solution)/shard_map/ppermute | solution.py:566
  24.2 34.1 %collective-permute-start = (bf16[5,320,128]{2,1,0:T(8,128)(2,1)S(1)}, bf16[5,320,128]{2,1,0:T(8,128)(2,1)}, u32[]{:S(2)}, u32[]{:S(2)}) collective-permute-start(bf16[5,320,128]{2,1,0:T(8,128)(2,1)S(1)} %get-tuple-element.24), channel_id=1, source_target_pairs={{0,1},{1,2},{2,3},{3,4},{4,5},{5,6},{6,7},{7,8},{8,9},{9,10},{10,1... | collective-permute-start | bytes 1228808 | tf_op jit(solution)/shard_map/ppermute | solution.py:565
  37.5 13.6 %all-to-all-start.1 = ((f32[128,1,128]{2,1,0:T(1,128)}), f32[128,1,128]{2,1,0:T(1,128)S(1)}, u32[]{:S(2)}, u32[]{:S(2)}) async-start(f32[128,1,128]{2,1,0:T(1,128)} %bitcast.10), calls=%async_computation.1 | async-start | bytes 131072 | tf_op jit(solution)/shard_map/all_to_all | solution.py:517
  52.0 14.7 %all-to-all-start.2 = ((bf16[128,2,384]{2,1,0:T(2,128)(2,1)}), bf16[128,2,384]{2,1,0:T(2,128)(2,1)S(1)}, u32[]{:S(2)}, u32[]{:S(2)}) async-start(bf16[128,2,384]{2,1,0:T(2,128)(2,1)} %bitcast.16), calls=%async_computation.2 | async-start | bytes 393216 | tf_op jit(solution)/shard_map/all_to_all | solution.py:517
